TPU v7x, 32 devices: a whole 2x2x4 slice. The times are simulated.
32 devices in a mesh: section: 2 (over core), fsdp: 4 (over z), ctx: 4 (over y, x).
Axes of the slice: x: 2, y: 2, z: 4, core: 2. Of those that a mesh axis runs over, the one named last changes fastest.
Arguments:
- inputs: bfloat16 [2, 4, 2048, 640], P(None, 'fsdp', 'ctx'), may hold values from -6 to 6
- grad_out: bfloat16 [2, 4, 2048, 640], P(None, 'fsdp', 'ctx'), may hold values from -6 to 6
- lengths: int32 [2, 4, 3], P(None, 'fsdp'), may hold values from 1 to 1537, 2048 in all within a row
- in_gain: bfloat16 [2, 640], P('section', 'fsdp'), may hold values from 0.099609375 to 1.8984375
- query_weight: bfloat16 [2, 640, 1024], P('section', 'fsdp'), may hold values from -0.25 to 0.25
- key_weight: bfloat16 [2, 640, 256], P('section', 'fsdp'), may hold values from -0.25 to 0.25
- value_weight: bfloat16 [2, 640, 256], P('section', 'fsdp'), may hold values from -0.25 to 0.25
- query_gain: bfloat16 [2, 256], P('section', 'fsdp'), may hold values from 0.099609375 to 1.8984375
- key_gain: bfloat16 [2, 256], P('section', 'fsdp'), may hold values from 0.099609375 to 1.8984375
- out_weight: bfloat16 [2, 1024, 640], P('section', 'fsdp'), may hold values from -0.1875 to 0.1875
- attn_gain: bfloat16 [2, 640], P('section', 'fsdp'), may hold values from 0.099609375 to 1.8984375
- ffn_gain: bfloat16 [2, 640], P('section', 'fsdp'), may hold values from 0.099609375 to 1.8984375
- gate_weight: bfloat16 [2, 640, 2048], P('section', 'fsdp'), may hold values from -0.25 to 0.25
- up_weight: bfloat16 [2, 640, 2048], P('section', 'fsdp'), may hold values from -0.25 to 0.25
- down_weight: bfloat16 [2, 2048, 640], P('section', 'fsdp'), may hold values from -0.125 to 0.125
- post_gain: bfloat16 [2, 640], P('section', 'fsdp'), may hold values from 0.099609375 to 1.8984375
Outputs:
- activations: bfloat16 [2, 2, 4, 2048, 640], P('section', None, 'fsdp', 'ctx')
- input_grads: bfloat16 [2, 2, 4, 2048, 640], P('section', None, 'fsdp', 'ctx')
- in_gain_grad: float32 [2, 640], P('section', 'fsdp')
- query_weight_grad: float32 [2, 640, 1024], P('section', 'fsdp')
- key_weight_grad: float32 [2, 640, 256], P('section', 'fsdp')
- value_weight_grad: float32 [2, 640, 256], P('section', 'fsdp')
- query_gain_grad: float32 [2, 256], P('section', 'fsdp')
- key_gain_grad: float32 [2, 256], P('section', 'fsdp')
- out_weight_grad: float32 [2, 1024, 640], P('section', 'fsdp')
- attn_gain_grad: float32 [2, 640], P('section', 'fsdp')
- ffn_gain_grad: float32 [2, 640], P('section', 'fsdp')
- gate_weight_grad: float32 [2, 640, 2048], P('section', 'fsdp')
- up_weight_grad: float32 [2, 640, 2048], P('section', 'fsdp')
- down_weight_grad: float32 [2, 2048, 640], P('section', 'fsdp')
- post_gain_grad: float32 [2, 640], P('section', 'fsdp')
Inputs may be any that keep to these rules, and one draw needn't show every extreme that they name: The lengths of each row sum to 2048, and the longest sequence of every row has exactly 1537 tokens.
All inputs are finite; a program needn't handle non-finite values.
Results may differ from a plain program's by a relative error of at most 0.029.
Values may be sent and summed in bfloat16 or wider, within the bound.
No kernel may reach another device: no remote copies, remote signals or barrier semaphores. Data moves between devices by JAX's collectives and lax.ppermute only.
A program may use at most 256 MiB of HBM per device.

v0:
```python
from functools import partial

import jax
import jax.numpy as jnp
from jax import lax
from jax.sharding import PartitionSpec as P

HD = 256
WINDOW = 512


EPS = 1e-06


def passed_along(array, axis, by):
    devices = lax.axis_size(axis)
    pairs = [(i, i + by) for i in range(devices) if 0 <= i + by < devices]
    return lax.ppermute(array, axis, pairs)


def as_sent(array):
    return jax.tree.map(lambda a: a.astype(jnp.bfloat16) if a.dtype == jnp.float32 else a, array)


def rms_norm(values, gain_vec):
    return values * lax.rsqrt(jnp.mean(values * values, axis=-1, keepdims=True) + EPS) * gain_vec


def norm_back(values, gain_vec, grad_vec):
    unused, pull_back = jax.vjp(rms_norm, values, gain_vec)
    return pull_back(grad_vec)


def rotary(values, cos_tab, sin_tab):
    half_dim = values.shape[-1] // 2
    lower_half = values[..., :half_dim]
    upper_half = values[..., half_dim:]
    return jnp.concatenate(
        [lower_half * cos_tab - upper_half * sin_tab, upper_half * cos_tab + lower_half * sin_tab],
        axis=-1,
    )


def head_norm(cos_tab, sin_tab, pre_norm, gain_vec):
    return rotary(rms_norm(pre_norm, gain_vec), cos_tab, sin_tab)


def gelu_mul(gate_pre, up_pre):
    return jax.nn.gelu(gate_pre, approximate=True) * up_pre


def rope_tables(offset):
    half_dim = HD // 2
    inv_freq = 10000.0 ** (-(jnp.arange(half_dim).astype(jnp.float32) * 2.0 / HD))
    angles = offset.astype(jnp.float32)[:, None] * inv_freq[None, :]
    return (jnp.cos(angles), jnp.sin(angles))


def row_layout(seq_lens, first_place, tok_count):
    seq_ends = jnp.cumsum(seq_lens)
    seq_starts = seq_ends - seq_lens
    places = first_place + jnp.arange(tok_count)
    segment = jnp.sum((places[:, None] >= seq_ends[None, :]).astype(jnp.int32), axis=1)
    labels = jnp.arange(seq_lens.shape[0])
    seg_hit = segment[:, None] == labels[None, :]
    offset = places - jnp.sum(jnp.where(seg_hit, seq_starts[None, :], 0), axis=1)
    return (places, segment, offset)


def layout_for(lengths, mb_slot, tok_count, ctx_index):
    seq_lens = lax.dynamic_index_in_dim(lengths[:, 0], mb_slot, 0, keepdims=False)
    first_place = ctx_index * tok_count
    places, segment, offset = row_layout(seq_lens, first_place, tok_count)
    far_places, far_segment, unused = row_layout(seq_lens, first_place - WINDOW, WINDOW)
    return (
        places,
        segment,
        offset,
        jnp.concatenate([far_places, places]),
        jnp.concatenate([far_segment, segment]),
    )


def mask_for(q_places, q_segment, k_places, k_segment):
    distance = q_places[:, None] - k_places[None, :]
    return (
        (q_segment[:, None] == k_segment[None, :])
        & (distance >= 0)
        & (distance < WINDOW)
        & (k_places[None, :] >= 0)
    )


def scores_for(queries, all_keys, allowed):
    raw_scores = jnp.einsum(
        "qhd,kd->hqk", queries, all_keys, preferred_element_type=jnp.float32
    ) * HD ** (-0.5)
    return jnp.where(allowed[None], raw_scores, -1e30)


def empty_pieces(micro, tok_count, heads, width, q_width, ff_width):
    f32 = jnp.float32
    b16 = jnp.bfloat16
    shapes = {
        "hidden": ((tok_count, width), f32),
        "normed": ((tok_count, width), b16),
        "cos_tab": ((tok_count, HD // 2), f32),
        "sin_tab": ((tok_count, HD // 2), f32),
        "query_pre": ((tok_count, heads, HD), f32),
        "key_pre": ((tok_count, HD), f32),
        "queries": ((tok_count, heads, HD), b16),
        "all_keys": ((tok_count + WINDOW, HD), b16),
        "all_vals": ((tok_count + WINDOW, HD), b16),
        "log_norm": ((heads, tok_count, 1), f32),
        "mixed_heads": ((tok_count, q_width), b16),
        "branch": ((tok_count, width), f32),
        "middle": ((tok_count, width), f32),
        "ffn_in": ((tok_count, width), b16),
        "gate_pre": ((tok_count, ff_width), f32),
        "up_pre": ((tok_count, ff_width), f32),
        "product": ((tok_count, ff_width), b16),
        "down_out": ((tok_count, width), f32),
    }
    return {label: jnp.zeros((micro,) + entry[0], entry[1]) for label, entry in shapes.items()}


def layer_pieces(params, hidden_bf, layout_info):
    (
        in_gain,
        query_weight,
        key_weight,
        value_weight,
        query_gain,
        key_gain,
        out_weight,
        attn_gain,
        ffn_gain,
        gate_weight,
        up_weight,
        down_weight,
        post_gain,
    ) = params
    places, segment, offset, k_places, k_segment = layout_info
    tok_count = hidden_bf.shape[0]
    hidden = hidden_bf.astype(jnp.float32)
    normed = rms_norm(hidden, in_gain.astype(jnp.float32)).astype(jnp.bfloat16)
    cos_tab, sin_tab = rope_tables(offset)
    query_pre = jnp.dot(normed, query_weight, preferred_element_type=jnp.float32).reshape(
        tok_count, -1, HD
    )
    key_pre = jnp.dot(normed, key_weight, preferred_element_type=jnp.float32)
    value_pre = jnp.dot(normed, value_weight, preferred_element_type=jnp.float32)
    queries = head_norm(
        cos_tab[:, None], sin_tab[:, None], query_pre, query_gain.astype(jnp.float32)
    ).astype(jnp.bfloat16)
    near_keys = head_norm(cos_tab, sin_tab, key_pre, key_gain.astype(jnp.float32)).astype(
        jnp.bfloat16
    )
    near_vals = value_pre.astype(jnp.bfloat16)
    far_keys, far_vals = passed_along((near_keys, near_vals), "ctx", 1)
    all_keys = jnp.concatenate([far_keys, near_keys], axis=0)
    all_vals = jnp.concatenate([far_vals, near_vals], axis=0)
    allowed = mask_for(places, segment, k_places, k_segment)
    scores = scores_for(queries, all_keys, allowed)
    row_max = jnp.max(scores, axis=-1, keepdims=True)
    exp_scores = jnp.exp(scores - row_max)
    row_total = jnp.sum(exp_scores, axis=-1, keepdims=True)
    soft_probs = (exp_scores / row_total).astype(jnp.bfloat16)
    mixed_parts = [
        jnp.einsum("hqk,kd->qhd", soft_probs, all_vals, preferred_element_type=jnp.float32)
    ]
    norm_parts = [row_max + jnp.log(row_total)]
    mixed_heads = jnp.concatenate(mixed_parts, axis=0).reshape(tok_count, -1).astype(jnp.bfloat16)
    log_norm = jnp.concatenate(norm_parts, axis=1)
    branch = jnp.dot(mixed_heads, out_weight, preferred_element_type=jnp.float32)
    middle = hidden + rms_norm(branch, attn_gain.astype(jnp.float32))
    ffn_in = rms_norm(middle, ffn_gain.astype(jnp.float32)).astype(jnp.bfloat16)
    gate_pre = jnp.dot(ffn_in, gate_weight, preferred_element_type=jnp.float32)
    up_pre = jnp.dot(ffn_in, up_weight, preferred_element_type=jnp.float32)
    product = gelu_mul(gate_pre, up_pre).astype(jnp.bfloat16)
    down_out = jnp.dot(product, down_weight, preferred_element_type=jnp.float32)
    result = middle + rms_norm(down_out, post_gain.astype(jnp.float32))
    kept_pieces = {
        "hidden": hidden,
        "normed": normed,
        "cos_tab": cos_tab,
        "sin_tab": sin_tab,
        "query_pre": query_pre,
        "key_pre": key_pre,
        "queries": queries,
        "all_keys": all_keys,
        "all_vals": all_vals,
        "log_norm": log_norm,
        "mixed_heads": mixed_heads,
        "branch": branch,
        "middle": middle,
        "ffn_in": ffn_in,
        "gate_pre": gate_pre,
        "up_pre": up_pre,
        "product": product,
        "down_out": down_out,
    }
    return (result, kept_pieces)


def layer_back(params, layout_info, cotangent, kept):
    (
        in_gain,
        query_weight,
        key_weight,
        value_weight,
        query_gain,
        key_gain,
        out_weight,
        attn_gain,
        ffn_gain,
        gate_weight,
        up_weight,
        down_weight,
        post_gain,
    ) = params
    places, segment, offset, k_places, k_segment = layout_info
    tok_count = cotangent.shape[0]
    d_down32, post_gain_grad = norm_back(kept["down_out"], post_gain.astype(jnp.float32), cotangent)
    d_down = d_down32.astype(jnp.bfloat16)
    down_grad = jnp.einsum("tf,td->fd", kept["product"], d_down, preferred_element_type=jnp.float32)
    d_product = jnp.einsum("td,fd->tf", d_down, down_weight, preferred_element_type=jnp.float32)
    unused, pull_gelu = jax.vjp(gelu_mul, kept["gate_pre"], kept["up_pre"])
    d_gate32, d_up32 = pull_gelu(d_product)
    d_gate = d_gate32.astype(jnp.bfloat16)
    d_up = d_up32.astype(jnp.bfloat16)
    gate_grad = jnp.einsum("td,tf->df", kept["ffn_in"], d_gate, preferred_element_type=jnp.float32)
    up_grad = jnp.einsum("td,tf->df", kept["ffn_in"], d_up, preferred_element_type=jnp.float32)
    d_ffn_in = jnp.einsum("tf,df->td", d_gate, gate_weight, preferred_element_type=jnp.float32)
    d_ffn_in = d_ffn_in + jnp.einsum(
        "tf,df->td", d_up, up_weight, preferred_element_type=jnp.float32
    )
    d_middle_add, ffn_gain_grad = norm_back(kept["middle"], ffn_gain.astype(jnp.float32), d_ffn_in)
    d_middle = cotangent + d_middle_add
    d_branch32, attn_gain_grad = norm_back(kept["branch"], attn_gain.astype(jnp.float32), d_middle)
    d_branch = d_branch32.astype(jnp.bfloat16)
    out_grad = jnp.einsum(
        "te,td->ed", kept["mixed_heads"], d_branch, preferred_element_type=jnp.float32
    )
    d_mixed = (
        jnp.einsum("td,ed->te", d_branch, out_weight, preferred_element_type=jnp.float32)
        .astype(jnp.bfloat16)
        .reshape(tok_count, -1, HD)
    )
    queries = kept["queries"]
    all_keys = kept["all_keys"]
    all_vals = kept["all_vals"]
    score_scale = HD ** (-0.5)
    q_block = min(512, tok_count)
    d_keys = jnp.zeros(all_keys.shape, jnp.float32)
    d_vals = jnp.zeros(all_vals.shape, jnp.float32)
    col_span = slice(0, q_block + WINDOW)
    allowed = mask_for(places, segment, k_places, k_segment)
    scores = scores_for(queries, all_keys, allowed)
    soft_probs = jnp.exp(scores - kept["log_norm"])
    d_probs = jnp.einsum("qhd,kd->hqk", d_mixed, all_vals, preferred_element_type=jnp.float32)
    inner_sum = jnp.sum(soft_probs * d_probs, axis=-1, keepdims=True)
    d_scores = (soft_probs * (d_probs - inner_sum)).astype(jnp.bfloat16)
    d_query_parts = [
        jnp.einsum("hqk,kd->qhd", d_scores, all_keys, preferred_element_type=jnp.float32)
        * score_scale
    ]
    d_keys = d_keys.at[col_span].add(
        jnp.einsum("hqk,qhd->kd", d_scores, queries, preferred_element_type=jnp.float32)
        * score_scale
    )
    d_vals = d_vals.at[col_span].add(
        jnp.einsum(
            "hqk,qhd->kd",
            soft_probs.astype(jnp.bfloat16),
            d_mixed,
            preferred_element_type=jnp.float32,
        )
    )
    d_queries = jnp.concatenate(d_query_parts, axis=0)
    back_keys, back_vals = (
        passed_along(d_keys[:WINDOW].astype(jnp.bfloat16), "ctx", -1).astype(jnp.float32),
        passed_along(d_vals[:WINDOW].astype(jnp.bfloat16), "ctx", -1).astype(jnp.float32),
    )
    near_dk = d_keys[WINDOW:].at[tok_count - WINDOW :].add(back_keys)
    near_dv = d_vals[WINDOW:].at[tok_count - WINDOW :].add(back_vals)
    cos_tab = kept["cos_tab"]
    sin_tab = kept["sin_tab"]
    unused, pull_query = jax.vjp(
        partial(head_norm, cos_tab[:, None], sin_tab[:, None]),
        kept["query_pre"],
        query_gain.astype(jnp.float32),
    )
    d_query_pre32, query_gain_grad = pull_query(d_queries)
    unused, pull_key = jax.vjp(
        partial(head_norm, cos_tab, sin_tab), kept["key_pre"], key_gain.astype(jnp.float32)
    )
    d_key_pre32, key_gain_grad = pull_key(near_dk)
    d_query_pre = d_query_pre32.reshape(tok_count, -1).astype(jnp.bfloat16)
    d_key_pre = d_key_pre32.astype(jnp.bfloat16)
    d_value_pre = near_dv.astype(jnp.bfloat16)
    normed = kept["normed"]
    query_grad = jnp.einsum("td,te->de", normed, d_query_pre, preferred_element_type=jnp.float32)
    key_grad = jnp.einsum("td,te->de", normed, d_key_pre, preferred_element_type=jnp.float32)
    value_grad = jnp.einsum("td,te->de", normed, d_value_pre, preferred_element_type=jnp.float32)
    d_normed = jnp.einsum(
        "te,de->td", d_query_pre, query_weight, preferred_element_type=jnp.float32
    )
    d_normed = d_normed + jnp.einsum(
        "te,de->td", d_key_pre, key_weight, preferred_element_type=jnp.float32
    )
    d_normed = d_normed + jnp.einsum(
        "te,de->td", d_value_pre, value_weight, preferred_element_type=jnp.float32
    )
    d_hidden_add, in_gain_grad = norm_back(kept["hidden"], in_gain.astype(jnp.float32), d_normed)
    grad_in = d_middle + d_hidden_add
    grad_terms = (
        in_gain_grad,
        query_grad,
        key_grad,
        value_grad,
        query_gain_grad,
        key_gain_grad,
        out_grad,
        attn_gain_grad,
        ffn_gain_grad,
        gate_grad,
        up_grad,
        down_grad,
        post_gain_grad,
    )
    return (grad_in, grad_terms)


def per_device(
    inputs,
    grad_out,
    lengths,
    in_gain,
    query_weight,
    key_weight,
    value_weight,
    query_gain,
    key_gain,
    out_weight,
    attn_gain,
    ffn_gain,
    gate_weight,
    up_weight,
    down_weight,
    post_gain,
):
    section_index = lax.axis_index("section")
    ctx_index = lax.axis_index("ctx")
    gathered = (
        lax.all_gather(in_gain, "fsdp", axis=1, tiled=True),
        lax.all_gather(query_weight, "fsdp", axis=1, tiled=True),
        lax.all_gather(key_weight, "fsdp", axis=1, tiled=True),
        lax.all_gather(value_weight, "fsdp", axis=1, tiled=True),
        lax.all_gather(query_gain, "fsdp", axis=1, tiled=True),
        lax.all_gather(key_gain, "fsdp", axis=1, tiled=True),
        lax.all_gather(out_weight, "fsdp", axis=1, tiled=True),
        lax.all_gather(attn_gain, "fsdp", axis=1, tiled=True),
        lax.all_gather(ffn_gain, "fsdp", axis=1, tiled=True),
        lax.all_gather(gate_weight, "fsdp", axis=1, tiled=True),
        lax.all_gather(up_weight, "fsdp", axis=1, tiled=True),
        lax.all_gather(down_weight, "fsdp", axis=1, tiled=True),
        lax.all_gather(post_gain, "fsdp", axis=1, tiled=True),
    )
    params = tuple((piece[0] for piece in gathered))
    micro = inputs.shape[0]
    tok_count = inputs.shape[2]
    width = inputs.shape[3]
    q_width = params[1].shape[1]
    ff_width = params[9].shape[1]
    heads = q_width // HD
    section_first = section_index == 0
    fresh_rows = inputs[:, 0]
    cot_rows = grad_out[:, 0]

    def store_slot(stash, pieces, mb_slot):
        return jax.tree.map(
            lambda whole, one: lax.dynamic_update_index_in_dim(whole, one, mb_slot, 0),
            stash,
            pieces,
        )

    def forward_tick(tick_index, carried):
        arrived, kept_in, kept_out, stash = carried
        mb_slot = jnp.clip(tick_index - section_index, 0, micro - 1)
        fresh_in = lax.dynamic_index_in_dim(
            fresh_rows, jnp.minimum(tick_index, micro - 1), 0, keepdims=False
        )
        layer_in = jnp.where(section_first, fresh_in, arrived)
        layout_info = layout_for(lengths, mb_slot, tok_count, ctx_index)
        result, pieces = layer_pieces(params, layer_in, layout_info)
        result = result.astype(jnp.bfloat16)
        kept_in = lax.dynamic_update_index_in_dim(kept_in, layer_in, mb_slot, 0)
        kept_out = lax.dynamic_update_index_in_dim(kept_out, result, mb_slot, 0)
        stash = store_slot(stash, pieces, mb_slot)
        arrived = passed_along(result, "section", 1)
        return (arrived, kept_in, kept_out, stash)

    empty_rows = jnp.zeros((micro, tok_count, width), jnp.bfloat16)
    start_stash = empty_pieces(micro, tok_count, heads, width, q_width, ff_width)
    start_fwd = (jnp.zeros((tok_count, width), jnp.bfloat16), empty_rows, empty_rows, start_stash)
    unused_arrived, kept_in, kept_out, stash = lax.fori_loop(0, micro + 1, forward_tick, start_fwd)

    def backward_tick(tick_index, carried):
        arrived, in_grads, grad_sums = carried
        wanted = tick_index - 1 + section_index
        active_tick = (wanted >= 0) & (wanted < micro)
        mb_slot = jnp.clip(wanted, 0, micro - 1)
        given_cot = lax.dynamic_index_in_dim(cot_rows, mb_slot, 0, keepdims=False)
        given_cot = jnp.where(active_tick, given_cot, jnp.zeros_like(given_cot))
        cotangent = jnp.where(section_first, arrived, given_cot).astype(jnp.float32)
        layout_info = layout_for(lengths, mb_slot, tok_count, ctx_index)
        kept = jax.tree.map(
            lambda whole: lax.dynamic_index_in_dim(whole, mb_slot, 0, keepdims=False), stash
        )
        grad_in, grad_terms = layer_back(params, layout_info, cotangent, kept)
        grad_in = grad_in.astype(jnp.bfloat16)
        previous = lax.dynamic_index_in_dim(in_grads, mb_slot, 0, keepdims=False)
        in_grads = lax.dynamic_update_index_in_dim(
            in_grads, jnp.where(active_tick, grad_in, previous), mb_slot, 0
        )
        grad_sums = tuple((total + term for total, term in zip(grad_sums, grad_terms)))
        arrived = passed_along(grad_in, "section", -1)
        return (arrived, in_grads, grad_sums)

    start_sums = tuple((jnp.zeros(piece.shape, jnp.float32) for piece in params))
    start_bwd = (jnp.zeros((tok_count, width), jnp.bfloat16), empty_rows, start_sums)
    unused_arrived, in_grads, grad_sums = lax.fori_loop(0, micro + 1, backward_tick, start_bwd)
    stacked = tuple((total[None] for total in grad_sums))
    shard_sums = jax.tree.map(
        lambda part: part.astype(jnp.float32),
        lax.psum_scatter(as_sent(stacked), "fsdp", scatter_dimension=1, tiled=True),
    )
    final_grads = jax.tree.map(
        lambda part: part.astype(jnp.float32), lax.psum(as_sent(shard_sums), "ctx")
    )
    return (kept_out[None, :, None], in_grads[None, :, None]) + tuple(final_grads)


def solution(mesh):
    return jax.shard_map(
        per_device,
        mesh=mesh,
        in_specs=(
            P(None, "fsdp", "ctx", None),
            P(None, "fsdp", "ctx", None),
            P(None, "fsdp", None),
            P("section", "fsdp"),
            P("section", "fsdp", None),
            P("section", "fsdp", None),
            P("section", "fsdp", None),
            P("section", "fsdp"),
            P("section", "fsdp"),
            P("section", "fsdp", None),
            P("section", "fsdp"),
            P("section", "fsdp"),
            P("section", "fsdp", None),
            P("section", "fsdp", None),
            P("section", "fsdp", None),
            P("section", "fsdp"),
        ),
        out_specs=(
            P("section", None, "fsdp", "ctx", None),
            P("section", None, "fsdp", "ctx", None),
            P("section", "fsdp"),
            P("section", "fsdp", None),
            P("section", "fsdp", None),
            P("section", "fsdp", None),
            P("section", "fsdp"),
            P("section", "fsdp"),
            P("section", "fsdp", None),
            P("section", "fsdp"),
            P("section", "fsdp"),
            P("section", "fsdp", None),
            P("section", "fsdp", None),
            P("section", "fsdp", None),
            P("section", "fsdp"),
        ),
        check_vma=False,
    )
```

profile of v0, /device:TPU:0, one launch (start us, length us, event | category | flops | bytes accessed | tf_op | source)
XLA Modules:
  0.0 1360.5 jit_solution(16794300055397983364)
XLA Ops:
  14.2 15.0 %all-reduce.12 = (bf16[640]{0:T(1024)(128)(2,1)S(1)}, bf16[256]{0:T(256)(128)(2,1)}, bf16[256]{0:T(256)(128)(2,1)}, bf16[640]{0:T(1024)(128)(2,1)}, bf16[640]{0:T(1024)(128)(2,1)}, /*index=5*/bf16[640]{0:T(1024)(128)(2,1)}) all-reduce(bf16[640]{0:T(1024)(128)(2,1)S(1)} %dynamic-update-slice.8, ...), channel_id=1, replica_groups=mesh['section'=2,'fsdp'=4,'ctx'=4] {'fsdp'}, use_global_device_ids=true, to_apply=%add.4 | all-reduce | flops 3072 | bytes 12288 | tf_op jit(solution)/shard_map/squeeze | solution.py:370
  29.2 17.6 %all_gather.40 = bf16[1,640,256]{2,1,0:T(8,128)(2,1)} all-gather(bf16[1,160,256]{2,1,0:T(8,128)(2,1)S(1)} %copy-done.102), channel_id=1, replica_groups=mesh['section'=2,'fsdp'=4,'ctx'=4] {'fsdp'}, dimensions={1}, use_global_device_ids=true | all-gather | bytes 409600 | tf_op jit(solution)/shard_map/all_gather | solution.py:359
  46.8 14.8 %all_gather.41 = bf16[1,640,256]{2,1,0:T(8,128)(2,1)} all-gather(bf16[1,160,256]{2,1,0:T(8,128)(2,1)S(1)} %copy-done.103), channel_id=1, replica_groups=mesh['section'=2,'fsdp'=4,'ctx'=4] {'fsdp'}, dimensions={1}, use_global_device_ids=true | all-gather | bytes 409600 | tf_op jit(solution)/shard_map/all_gather | solution.py:358
  61.6 24.3 %all-gather.8.cloned.1.call-done = bf16[1,1024,640]{2,1,0:T(8,128)(2,1)} async-done(((bf16[1,256,640]{2,1,0:T(8,128)(2,1)}), bf16[1,1024,640]{2,1,0:T(8,128)(2,1)}) %all-gather.8.cloned.1.call-update) | async-done | bytes 1310736 | tf_op jit(solution)/shard_map/all_gather | solution.py:362
  85.9 55.4 %all-gather.10.cloned.1.call-done = bf16[1,640,2048]{2,1,0:T(8,128)(2,1)} async-done(((bf16[1,160,2048]{2,1,0:T(8,128)(2,1)}), bf16[1,640,2048]{2,1,0:T(8,128)(2,1)}) %all-gather.10.cloned.1.call-update) | async-done | bytes 2621456 | tf_op jit(solution)/shard_map/all_gather | solution.py:365
  141.3 55.0 %all-gather.12.cloned.1.call-done = bf16[1,640,2048]{2,1,0:T(8,128)(2,1)} async-done(((bf16[1,160,2048]{2,1,0:T(8,128)(2,1)}), bf16[1,640,2048]{2,1,0:T(8,128)(2,1)}) %all-gather.12.cloned.1.call-update) | async-done | bytes 2621456 | tf_op jit(solution)/shard_map/all_gather | solution.py:366
  196.4 55.0 %all-gather.14.cloned.1.call-done = bf16[1,2048,640]{2,1,0:T(8,128)(2,1)} async-done(((bf16[1,512,640]{2,1,0:T(8,128)(2,1)}), bf16[1,2048,640]{2,1,0:T(8,128)(2,1)}) %all-gather.14.cloned.1.call-update) | async-done | bytes 2621456 | tf_op jit(solution)/shard_map/all_gather | solution.py:367
  251.4 4.4 broadcast.1202
  255.8 4.3 broadcast.1202.clone
  284.8 224.3 %while.133 = (s32[]{:T(128)}, bf16[512,640]{1,0:T(8,128)(2,1)}, bf16[2,512,640]{2,1,0:T(8,128)(2,1)}, bf16[2,1024,256]{1,2,0:T(8,128)(2,1)}, bf16[2,1024,256]{2,...) while((s32[]{:T(128)}, bf16[512,640]{1,0:T(8,128)(2,1)}, ...), condition=%wide.region_13.14_spmd, body=%wide.region_0.13_spmd.sunk | while | flops 7923130880 | bytes 416638048 | solution.py:407
  294.9 4.1 collective-permute-start
  301.1 3.4 collective-permute-start.1
  334.9 4.1 fusion.297
  371.3 3.4 collective-permute-start
  409.5 4.1 fusion.297
  468.4 3.4 constant_dynamic-update-slice_fusion.5
  482.5 4.1 fusion.297
  511.1 351.0 %while.134 = (s32[]{:T(128)}, bf16[512,640]{1,0:T(8,128)(2,1)}, bf16[2,512,640]{2,1,0:T(8,128)(2,1)}, f32[640]{0:T(1024)}, f32[640,1024]{1,0:T(8,128)}, /*index=...) while((s32[]{:T(128)}, bf16[512,640]{1,0:T(8,128)(2,1)}, ...), condition=%wide.region_37.38_spmd.clone, body=%wide.region_14.37_spmd.clone.sunk | while | flops 16887751680 | bytes 561041920 | solution.py:433
  539.3 7.5 fusion.340
  577.7 4.9 multiply_bitcast_fusion.2
  590.7 5.8 select_add_fusion.29
  604.1 4.4 select_add_fusion.31
  644.9 7.5 fusion.340
  683.3 4.9 multiply_bitcast_fusion.2
  696.4 7.4 select_add_fusion.29
  711.3 6.9 select_add_fusion.31
  754.6 7.5 fusion.340
  793.0 4.9 multiply_bitcast_fusion.2
  806.1 7.4 select_add_fusion.29
  821.0 6.9 select_add_fusion.31
  870.5 4.4 convert_bitcast_fusion.3
  874.9 4.4 convert_bitcast_fusion.2
  879.4 4.3 convert_bitcast_fusion.1
  889.6 3.4 reduce-scatter.28.cloned.1.call-done
  893.0 21.1 %reduce-scatter.30.cloned.1.call-done = bf16[1,160,256]{2,1,0:T(8,128)(2,1)} async-done(((bf16[1,640,256]{2,1,0:T(8,128)(2,1)}), bf16[1,160,256]{2,1,0:T(8,128)(2,1)}) %reduce-scatter.30.cloned.1.call-update) | async-done | bytes 81936 | tf_op jit(solution)/shard_map/reduce_scatter | solution.py:437
  914.1 32.4 %reduce-scatter.26.cloned.1.call-done = bf16[1,160,1024]{2,1,0:T(8,128)(2,1)} async-done(((bf16[1,640,1024]{2,1,0:T(8,128)(2,1)}), bf16[1,160,1024]{2,1,0:T(8,128)(2,1)}) %reduce-scatter.26.cloned.1.call-update) | async-done | bytes 327696 | tf_op jit(solution)/shard_map/reduce_scatter | solution.py:437
  946.5 32.9 %reduce-scatter.32.cloned.1.call-done = bf16[1,256,640]{2,1,0:T(8,128)(2,1)} async-done(((bf16[1,1024,640]{2,1,0:T(8,128)(2,1)}), bf16[1,256,640]{2,1,0:T(8,128)(2,1)}) %reduce-scatter.32.cloned.1.call-update) | async-done | bytes 327696 | tf_op jit(solution)/shard_map/reduce_scatter | solution.py:437
  979.4 53.1 %reduce-scatter.34.cloned.1.call-done = bf16[1,160,2048]{2,1,0:T(8,128)(2,1)} async-done(((bf16[1,640,2048]{2,1,0:T(8,128)(2,1)}), bf16[1,160,2048]{2,1,0:T(8,128)(2,1)}) %reduce-scatter.34.cloned.1.call-update) | async-done | bytes 655376 | tf_op jit(solution)/shard_map/reduce_scatter | solution.py:437
  1032.5 54.1 %reduce-scatter.36.cloned.1.call-done = bf16[1,160,2048]{2,1,0:T(8,128)(2,1)} async-done(((bf16[1,640,2048]{2,1,0:T(8,128)(2,1)}), bf16[1,160,2048]{2,1,0:T(8,128)(2,1)}) %reduce-scatter.36.cloned.1.call-update) | async-done | bytes 655376 | tf_op jit(solution)/shard_map/reduce_scatter | solution.py:437
  1086.6 54.0 %reduce-scatter.38.cloned.1.call-done = bf16[1,512,640]{2,1,0:T(8,128)(2,1)} async-done(((bf16[1,2048,640]{2,1,0:T(8,128)(2,1)}), bf16[1,512,640]{2,1,0:T(8,128)(2,1)}) %reduce-scatter.38.cloned.1.call-update) | async-done | bytes 655376 | tf_op jit(solution)/shard_map/reduce_scatter | solution.py:437
  1140.6 20.9 %reduce-scatter.42.cloned.1.call-done = bf16[64,1]{1,0:T(8,128)(2,1)} async-done(((bf16[256,1]{1,0:T(8,128)(2,1)}), bf16[64,1]{1,0:T(8,128)(2,1)}) %reduce-scatter.42.cloned.1.call-update) | async-done | bytes 144
  1162.3 18.5 %reduce-scatter.44.cloned.1.call-done = bf16[64,1]{1,0:T(8,128)(2,1)} async-done(((bf16[256,1]{1,0:T(8,128)(2,1)}), bf16[64,1]{1,0:T(8,128)(2,1)}) %reduce-scatter.44.cloned.1.call-update) | async-done | bytes 144
  1181.7 19.4 %reduce-scatter.40.cloned.1.call-done = bf16[160,1]{1,0:T(8,128)(2,1)} async-done(((bf16[640,1]{1,0:T(8,128)(2,1)}), bf16[160,1]{1,0:T(8,128)(2,1)}) %reduce-scatter.40.cloned.1.call-update) | async-done | bytes 336
  1201.9 19.4 %reduce-scatter.46.cloned.1.call-done = bf16[160,1]{1,0:T(8,128)(2,1)} async-done(((bf16[640,1]{1,0:T(8,128)(2,1)}), bf16[160,1]{1,0:T(8,128)(2,1)}) %reduce-scatter.46.cloned.1.call-update) | async-done | bytes 336
  1222.2 19.3 %reduce-scatter.48.cloned.1.call-done = bf16[160,1]{1,0:T(8,128)(2,1)} async-done(((bf16[640,1]{1,0:T(8,128)(2,1)}), bf16[160,1]{1,0:T(8,128)(2,1)}) %reduce-scatter.48.cloned.1.call-update) | async-done | bytes 336
  1242.3 18.8 %reduce-scatter.50.cloned.1.call-done = bf16[160,1]{1,0:T(8,128)(2,1)} async-done(((bf16[640,1]{1,0:T(8,128)(2,1)}), bf16[160,1]{1,0:T(8,128)(2,1)}) %reduce-scatter.50.cloned.1.call-update) | async-done | bytes 336
  1261.9 10.1 all-reduce.10
  1275.3 70.5 %all-reduce.15.cloned.1.call-done = (bf16[1,160,1024]{2,1,0:T(8,128)(2,1)}, bf16[1,160,256]{2,1,0:T(8,128)(2,1)}, bf16[1,160,256]{2,1,0:T(8,128)(2,1)}, bf16[1,2...) async-done(((bf16[1,160,1024]{2,1,0:T(8,128)(2,1)}, bf16[1,160,256]{2,1,0:T(8,128)(2,1)}, ...) | async-done | bytes 2785296 | tf_op jit(solution)/shard_map/psum | solution.py:440
  (1265 shorter events, 504.0 us)
Async XLA Ops:
  7.3 21.9 %copy-start.102 = (bf16[1,160,256]{2,1,0:T(8,128)(2,1)S(1)}, bf16[1,160,256]{2,1,0:T(8,128)(2,1)}, u32[]{:S(2)}) copy-start(bf16[1,160,256]{2,1,0:T(8,128)(2,1)} %param.42) | copy-start | bytes 245764
  7.3 39.5 %copy-start.103 = (bf16[1,160,256]{2,1,0:T(8,128)(2,1)S(1)}, bf16[1,160,256]{2,1,0:T(8,128)(2,1)}, u32[]{:S(2)}) copy-start(bf16[1,160,256]{2,1,0:T(8,128)(2,1)} %param.41) | copy-start | bytes 245764
  7.3 54.3 %all-gather.6.cloned.1.call-start = ((), (), s32[]{:S(2)}) async-start(), calls=%async_computation.13 | async-start | bytes 1638400 | tf_op jit(solution)/shard_map/all_gather | solution.py:357
  8.0 77.9 %all-gather.8.cloned.1.call-start = ((), (), s32[]{:S(2)}) async-start(), calls=%async_computation.14 | async-start | bytes 1638400 | tf_op jit(solution)/shard_map/all_gather | solution.py:362
  8.8 132.6 %all-gather.10.cloned.1.call-start = ((), (), s32[]{:S(2)}) async-start(), calls=%async_computation.15 | async-start | bytes 3276800 | tf_op jit(solution)/shard_map/all_gather | solution.py:365
  9.5 186.9 %all-gather.12.cloned.1.call-start = ((), (), s32[]{:S(2)}) async-start(), calls=%async_computation.16 | async-start | bytes 3276800 | tf_op jit(solution)/shard_map/all_gather | solution.py:366
  10.1 241.3 %all-gather.14.cloned.1.call-start = ((), (), s32[]{:S(2)}) async-start(), calls=%async_computation.17 | async-start | bytes 3276800 | tf_op jit(solution)/shard_map/all_gather | solution.py:367
  10.7 882.3 %reduce-scatter.28.cloned.1.call-start = ((), (), s32[]{:S(2)}) async-start(), calls=%async_computation.19 | async-start | bytes 409600 | tf_op jit(solution)/shard_map/reduce_scatter | solution.py:437
  292.3 13.3 copy-start.42
  294.9 35.4 %collective-permute-start = (bf16[512,256]{0,1:T(8,128)(2,1)}, bf16[512,256]{0,1:T(8,128)(2,1)}, u32[]{:S(2)}, u32[]{:S(2)}) collective-permute-start(bf16[512,256]{0,1:T(8,128)(2,1)} %pad_maximum_fusion.4), channel_id=1, source_target_pairs={{0,1},{1,2},{2,3},{4,5},{5,6},{6,7},{8,9},{9,10},{10,11},{12,13},{... | collective-permute-start | bytes 786440 | tf_op jit(solution)/shard_map/while/body/eval_jaxpr/ppermute | solution.py:18
  301.1 33.8 %collective-permute-start.1 = (bf16[512,256]{1,0:T(8,128)(2,1)}, bf16[512,256]{1,0:T(8,128)(2,1)}, u32[]{:S(2)}, u32[]{:S(2)}) collective-permute-start(bf16[512,256]{1,0:T(8,128)(2,1)} %convolution_convert_fusion.4), channel_id=1, source_target_pairs={{0,1},{1,2},{2,3},{4,5},{5,6},{6,7},{8,9},{9,10},{10,11},{12,13},{... | collective-permute-start | bytes 786440 | tf_op jit(solution)/shard_map/while/body/eval_jaxpr/ppermute | solution.py:18
  351.8 9.8 collective-permute-start.2
  368.7 11.5 copy-start.42
  371.3 33.6 %collective-permute-start = (bf16[512,256]{0,1:T(8,128)(2,1)}, bf16[512,256]{0,1:T(8,128)(2,1)}, u32[]{:S(2)}, u32[]{:S(2)}) collective-permute-start(bf16[512,256]{0,1:T(8,128)(2,1)} %pad_maximum_fusion.4), channel_id=1, source_target_pairs={{0,1},{1,2},{2,3},{4,5},{5,6},{6,7},{8,9},{9,10},{10,11},{12,13},{... | collective-permute-start | bytes 786440 | tf_op jit(solution)/shard_map/while/body/eval_jaxpr/ppermute | solution.py:18
  376.8 32.7 %collective-permute-start.1 = (bf16[512,256]{1,0:T(8,128)(2,1)}, bf16[512,256]{1,0:T(8,128)(2,1)}, u32[]{:S(2)}, u32[]{:S(2)}) collective-permute-start(bf16[512,256]{1,0:T(8,128)(2,1)} %convolution_convert_fusion.4), channel_id=1, source_target_pairs={{0,1},{1,2},{2,3},{4,5},{5,6},{6,7},{8,9},{9,10},{10,11},{12,13},{... | collective-permute-start | bytes 786440 | tf_op jit(solution)/shard_map/while/body/eval_jaxpr/ppermute | solution.py:18
  426.4 9.6 collective-permute-start.2
  443.1 10.1 copy-start.42
  445.7 32.2 %collective-permute-start = (bf16[512,256]{0,1:T(8,128)(2,1)}, bf16[512,256]{0,1:T(8,128)(2,1)}, u32[]{:S(2)}, u32[]{:S(2)}) collective-permute-start(bf16[512,256]{0,1:T(8,128)(2,1)} %pad_maximum_fusion.4), channel_id=1, source_target_pairs={{0,1},{1,2},{2,3},{4,5},{5,6},{6,7},{8,9},{9,10},{10,11},{12,13},{... | collective-permute-start | bytes 786440 | tf_op jit(solution)/shard_map/while/body/eval_jaxpr/ppermute | solution.py:18
  449.8 32.7 %collective-permute-start.1 = (bf16[512,256]{1,0:T(8,128)(2,1)}, bf16[512,256]{1,0:T(8,128)(2,1)}, u32[]{:S(2)}, u32[]{:S(2)}) collective-permute-start(bf16[512,256]{1,0:T(8,128)(2,1)} %convolution_convert_fusion.4), channel_id=1, source_target_pairs={{0,1},{1,2},{2,3},{4,5},{5,6},{6,7},{8,9},{9,10},{10,11},{12,13},{... | collective-permute-start | bytes 786440 | tf_op jit(solution)/shard_map/while/body/eval_jaxpr/ppermute | solution.py:18
  499.4 9.7 collective-permute-start.2
  539.0 13.3 copy-start.9
  565.1 62.6 %collective-permute-start.4 = (bf16[512,256]{1,0:T(8,128)(2,1)}, bf16[512,256]{1,0:T(8,128)(2,1)}, u32[]{:S(2)}, u32[]{:S(2)}) collective-permute-start(bf16[512,256]{1,0:T(8,128)(2,1)} %slice.189), channel_id=1, source_target_pairs={{1,0},{2,1},{3,2},{5,4},{6,5},{7,6},{9,8},{10,9},{11,10},{13,12},{... | collective-permute-start | bytes 786440 | tf_op jit(solution)/shard_map/while/body/eval_jaxpr/ppermute | solution.py:18
  576.4 33.1 %collective-permute-start.3 = (bf16[512,256]{1,0:T(8,128)(2,1)}, bf16[512,256]{1,0:T(8,128)(2,1)}, u32[]{:S(2)}, u32[]{:S(2)}) collective-permute-start(bf16[512,256]{1,0:T(8,128)(2,1)} %slice.188), channel_id=1, source_target_pairs={{1,0},{2,1},{3,2},{5,4},{6,5},{7,6},{9,8},{10,9},{11,10},{13,12},{... | collective-permute-start | bytes 786440 | tf_op jit(solution)/shard_map/while/body/eval_jaxpr/ppermute | solution.py:18
  632.2 5.7 collective-permute-start.5
  644.6 13.3 copy-start.9
  670.8 66.7 %collective-permute-start.4 = (bf16[512,256]{1,0:T(8,128)(2,1)}, bf16[512,256]{1,0:T(8,128)(2,1)}, u32[]{:S(2)}, u32[]{:S(2)}) collective-permute-start(bf16[512,256]{1,0:T(8,128)(2,1)} %slice.189), channel_id=1, source_target_pairs={{1,0},{2,1},{3,2},{5,4},{6,5},{7,6},{9,8},{10,9},{11,10},{13,12},{... | collective-permute-start | bytes 786440 | tf_op jit(solution)/shard_map/while/body/eval_jaxpr/ppermute | solution.py:18
  682.0 37.2 %collective-permute-start.3 = (bf16[512,256]{1,0:T(8,128)(2,1)}, bf16[512,256]{1,0:T(8,128)(2,1)}, u32[]{:S(2)}, u32[]{:S(2)}) collective-permute-start(bf16[512,256]{1,0:T(8,128)(2,1)} %slice.188), channel_id=1, source_target_pairs={{1,0},{2,1},{3,2},{5,4},{6,5},{7,6},{9,8},{10,9},{11,10},{13,12},{... | collective-permute-start | bytes 786440 | tf_op jit(solution)/shard_map/while/body/eval_jaxpr/ppermute | solution.py:18
  708.8 9.4 copy-start.20
  708.8 9.4 copy-start.96
  742.0 5.7 collective-permute-start.5
  754.4 13.3 copy-start.9
  780.5 66.7 %collective-permute-start.4 = (bf16[512,256]{1,0:T(8,128)(2,1)}, bf16[512,256]{1,0:T(8,128)(2,1)}, u32[]{:S(2)}, u32[]{:S(2)}) collective-permute-start(bf16[512,256]{1,0:T(8,128)(2,1)} %slice.189), channel_id=1, source_target_pairs={{1,0},{2,1},{3,2},{5,4},{6,5},{7,6},{9,8},{10,9},{11,10},{13,12},{... | collective-permute-start | bytes 786440 | tf_op jit(solution)/shard_map/while/body/eval_jaxpr/ppermute | solution.py:18
  791.7 37.2 %collective-permute-start.3 = (bf16[512,256]{1,0:T(8,128)(2,1)}, bf16[512,256]{1,0:T(8,128)(2,1)}, u32[]{:S(2)}, u32[]{:S(2)}) collective-permute-start(bf16[512,256]{1,0:T(8,128)(2,1)} %slice.188), channel_id=1, source_target_pairs={{1,0},{2,1},{3,2},{5,4},{6,5},{7,6},{9,8},{10,9},{11,10},{13,12},{... | collective-permute-start | bytes 786440 | tf_op jit(solution)/shard_map/while/body/eval_jaxpr/ppermute | solution.py:18
  818.6 9.4 copy-start.20
  851.7 5.7 collective-permute-start.5
  864.2 49.9 %reduce-scatter.30.cloned.1.call-start = ((), (), s32[]{:S(2)}) async-start(), calls=%async_computation.20 | async-start | bytes 409600 | tf_op jit(solution)/shard_map/reduce_scatter | solution.py:437
  866.1 80.4 %reduce-scatter.26.cloned.1.call-start = ((), (), s32[]{:S(2)}) async-start(), calls=%async_computation.18 | async-start | bytes 1638400 | tf_op jit(solution)/shard_map/reduce_scatter | solution.py:437
  867.4 112.0 %reduce-scatter.32.cloned.1.call-start = ((), (), s32[]{:S(2)}) async-start(), calls=%async_computation.21 | async-start | bytes 1638400 | tf_op jit(solution)/shard_map/reduce_scatter | solution.py:437
  870.4 162.0 %reduce-scatter.34.cloned.1.call-start = ((), (), s32[]{:S(2)}) async-start(), calls=%async_computation.22 | async-start | bytes 3276800 | tf_op jit(solution)/shard_map/reduce_scatter | solution.py:437
  874.9 211.8 %reduce-scatter.36.cloned.1.call-start = ((), (), s32[]{:S(2)}) async-start(), calls=%async_computation.23 | async-start | bytes 3276800 | tf_op jit(solution)/shard_map/reduce_scatter | solution.py:437
  879.3 261.3 %reduce-scatter.38.cloned.1.call-start = ((), (), s32[]{:S(2)}) async-start(), calls=%async_computation.24 | async-start | bytes 3276800 | tf_op jit(solution)/shard_map/reduce_scatter | solution.py:437
  883.7 277.8 %reduce-scatter.42.cloned.1.call-start = ((), (), s32[]{:S(2)}) async-start(), calls=%async_computation.26 | async-start | bytes 81920
  885.1 295.8 %reduce-scatter.44.cloned.1.call-start = ((), (), s32[]{:S(2)}) async-start(), calls=%async_computation.27 | async-start | bytes 81920
  885.9 315.1 %reduce-scatter.40.cloned.1.call-start = ((), (), s32[]{:S(2)}) async-start(), calls=%async_computation.25 | async-start | bytes 204800
  886.8 334.5 %reduce-scatter.46.cloned.1.call-start = ((), (), s32[]{:S(2)}) async-start(), calls=%async_computation.28 | async-start | bytes 204800
  887.7 353.7 %reduce-scatter.48.cloned.1.call-start = ((), (), s32[]{:S(2)}) async-start(), calls=%async_computation.29 | async-start | bytes 204800
  888.6 372.5 %reduce-scatter.50.cloned.1.call-start = ((), (), s32[]{:S(2)}) async-start(), calls=%async_computation.30 | async-start | bytes 204800
  889.5 456.3 %all-reduce.15.cloned.1.call-start = ((), (), s32[]{:S(2)}) async-start(), calls=%async_computation.31 | async-start | bytes 5570560 | tf_op jit(solution)/shard_map/psum | solution.py:440
  (338 other events, 1175.3 us)
Sparse Core Ops, SparseCore 0:
  9.7 43.0 all-gather.5
  54.3 31.5 all-gather.7
  87.5 53.7 all-gather.9
  142.8 53.5 all-gather.11
  197.8 53.5 all-gather.13
  864.3 28.6 reduce-scatter.27
  895.8 18.2 reduce-scatter.29
  917.0 29.4 reduce-scatter.25
  949.3 29.9 reduce-scatter.31
  981.5 50.8 reduce-scatter.33
  1034.8 51.7 reduce-scatter.35
  1088.8 51.7 reduce-scatter.37
  1142.8 18.6 reduce-scatter.41
  1163.7 17.1 reduce-scatter.43
  1183.6 17.4 reduce-scatter.39
  1203.8 17.4 reduce-scatter.45
  1224.0 17.4 reduce-scatter.47
  1243.7 17.3 reduce-scatter.49
  1265.0 80.7 all-reduce.14
where the time goes:
time: 1370 us; the launch traced here: 1360 us
  waiting for transfers between devices  631 us (46%)
  matrix products  222 us (16%)
  other arithmetic  183 us (13%)
  local copies, waits for them, and re-layouts  182 us (13%)
  blocking collectives  57.5 us (4%)
  starting transfers between devices  37.6 us (3%)
  loops' own time  31.1 us (2%)
  between operations  15.9 us (1%)
    reduce_scatter x7, waiting for transfers between devices, per_device(): lax.psum_scatter(as_sent(stacked), 'fsdp', scatter_dimension=1, tiled=True)  251 us
    unnamed x25, waiting for transfers between devices  120 us
    psum x1, waiting for transfers between devices, per_device(): lax.psum(as_sent(shard_sums), 'ctx')  70.5 us
    all_gather x1, waiting for transfers between devices, per_device(): lax.all_gather(gate_weight, 'fsdp', axis=1, tiled=True)  55.4 us
    all_gather x1, waiting for transfers between devices, per_device(): lax.all_gather(up_weight, 'fsdp', axis=1, tiled=True)  55 us
    all_gather x1, waiting for transfers between devices, per_device(): lax.all_gather(down_weight, 'fsdp', axis=1, tiled=True)  55 us
    while x654, local copies, waits for them, and re-layouts  48.4 us
    ppermute x18, starting transfers between devices, passed_along(): return lax.ppermute(array, axis, pairs)  36.8 us
  transfers between devices with their start and end apart: 37, of which 18 were waited for; matrix products, arithmetic and copies ran while one was open for 24% of the time, Pallas kernels for 0%

commit v1 on v0

v1 whole, which is shorter than its diff:
```python
from functools import partial

import jax
import jax.numpy as jnp
from jax import lax
from jax.experimental import pallas as pl
from jax.experimental.pallas import tpu as pltpu
from jax.sharding import PartitionSpec as P

HD = 256
WINDOW = 512
EPS = 1e-06
LANES = 128
PARTS = 4
GAIN_ROWS = 16
QB = 128
F32 = jnp.float32
B16 = jnp.bfloat16
VMEM_LIMIT = 56 * 1024 * 1024
AXES = ("section", "fsdp", "ctx")


def rope_tables(offset):
    half_dim = HD // 2
    inv_freq = 10000.0 ** (-(jnp.arange(half_dim).astype(F32) * 2.0 / HD))
    angles = offset.astype(F32)[:, None] * inv_freq[None, :]
    return (jnp.cos(angles), jnp.sin(angles))


def layout_for(seq_lens, first_place, tok_count):
    seq_ends = jnp.cumsum(seq_lens)
    seq_starts = seq_ends - seq_lens
    places = first_place + jnp.arange(tok_count)
    segment = jnp.sum((places[:, None] >= seq_ends[None, :]).astype(jnp.int32), axis=1)
    labels = jnp.arange(seq_lens.shape[0])
    seg_hit = segment[:, None] == labels[None, :]
    start = jnp.sum(jnp.where(seg_hit, seq_starts[None, :], 0), axis=1)
    offset = places - start
    low = jnp.maximum(start, places - (WINDOW - 1)) - first_place + WINDOW
    return offset, low.astype(jnp.int32)


def dot(a, b):
    return lax.dot_general(a, b, (((1,), (0,)), ((), ())), preferred_element_type=F32)


def dot_nt(a, b):
    return lax.dot_general(a, b, (((1,), (1,)), ((), ())), preferred_element_type=F32)


def dot_tn(a, b):
    return lax.dot_general(a, b, (((0,), (0,)), ((), ())), preferred_element_type=F32)


def inv_rms(v):
    return lax.rsqrt(jnp.mean(v * v, axis=-1, keepdims=True) + EPS)


def rms_back(v, gain, grad):
    r = inv_rms(v)
    gg = grad * gain
    normed = v * r
    back = r * (gg - normed * jnp.mean(normed * gg, axis=-1, keepdims=True))
    return back, jnp.sum(grad * normed, axis=0, keepdims=True)


def rope(v, cos, sin):
    u, w = v[:, : HD // 2], v[:, HD // 2 :]
    return jnp.concatenate([u * cos - w * sin, w * cos + u * sin], axis=-1)


def rope_back(g, cos, sin):
    a, b = g[:, : HD // 2], g[:, HD // 2 :]
    return jnp.concatenate([a * cos + b * sin, b * cos - a * sin], axis=-1)


GELU_C = 0.7978845608028654
GELU_A = 0.044715


def gelu_parts(g):
    g2 = g * g
    t = jnp.tanh(GELU_C * g * (1.0 + GELU_A * g2))
    half = 0.5 * (1.0 + t)
    value = g * half
    slope = half + 0.5 * g * (1.0 - t * t) * (GELU_C * (1.0 + 3.0 * GELU_A * g2))
    return value, slope


def params(**kw):
    return pltpu.CompilerParams(vmem_limit_bytes=VMEM_LIMIT, **kw)


def cost(flops, nbytes):
    return pl.CostEstimate(flops=int(flops), bytes_accessed=int(nbytes), transcendentals=0)


def whole(shape):
    n = len(shape)
    return pl.BlockSpec(shape, lambda *i: (0,) * n)


def sds(shape, dtype):
    return jax.ShapeDtypeStruct(shape, dtype)


def kv_kernel(x_ref, gd_ref, gh_ref, cos_ref, sin_ref, w_ref, a_ref, pre_ref, kv_ref):
    x = x_ref[...].astype(F32)
    a = (x * inv_rms(x) * gd_ref[0:1, :]).astype(B16)
    a_ref[...] = a
    both = dot(a, w_ref[...])
    pre = both[:, :HD]
    pre_ref[...] = pre.astype(B16)
    keys = rope(pre * inv_rms(pre) * gh_ref[1:2, :], cos_ref[...], sin_ref[...])
    kv_ref[:, :HD] = keys.astype(B16)
    kv_ref[:, HD:] = both[:, HD:].astype(B16)


def kv_call(x, gd, gh, cos, sin, w_qkv):
    tok, width = x.shape
    q_width = w_qkv.shape[1] - 2 * HD
    return pl.pallas_call(
        kv_kernel,
        grid=(1,),
        in_specs=[
            whole(x.shape),
            whole(gd.shape),
            whole(gh.shape),
            whole(cos.shape),
            whole(sin.shape),
            pl.BlockSpec((width, 2 * HD), lambda j: (0, q_width // (2 * HD))),
        ],
        out_specs=[whole((tok, width)), whole((tok, HD)), whole((tok, 2 * HD))],
        out_shape=[sds((tok, width), B16), sds((tok, HD), B16), sds((tok, 2 * HD), B16)],
        compiler_params=params(),
        cost_estimate=cost(4 * tok * width * HD, 4e6),
        name="keys_values",
    )(x, gd, gh, cos, sin, w_qkv)


def q_kernel(a_ref, gh_ref, cos_ref, sin_ref, w_ref, pre_ref, q_ref):
    pre = dot(a_ref[...], w_ref[...])
    pre_ref[...] = pre.astype(B16)
    q_ref[...] = rope(pre * inv_rms(pre) * gh_ref[0:1, :], cos_ref[...], sin_ref[...]).astype(B16)


def q_call(a, gh, cos, sin, w_qkv):
    tok, width = a.shape
    q_width = w_qkv.shape[1] - 2 * HD
    block = pl.BlockSpec((tok, HD), lambda j: (0, j))
    return pl.pallas_call(
        q_kernel,
        grid=(q_width // HD,),
        in_specs=[
            whole(a.shape),
            whole(gh.shape),
            whole(cos.shape),
            whole(sin.shape),
            pl.BlockSpec((width, HD), lambda j: (0, j)),
        ],
        out_specs=[block, block],
        out_shape=[sds((tok, q_width), B16), sds((tok, q_width), B16)],
        compiler_params=params(),
        cost_estimate=cost(2 * tok * width * q_width, 5e6),
        name="queries",
    )(a, gh, cos, sin, w_qkv)


SCORE_SCALE = HD ** (-0.5)


def attn_kernel(q_ref, far_ref, near_ref, low_ref, o_ref, kv_scr):
    b = pl.program_id(0)

    @pl.when(b == 0)
    def _():
        kv_scr[:WINDOW, :] = far_ref[...]
        kv_scr[WINDOW:, :] = near_ref[...]

    span = WINDOW + QB
    first = pl.multiple_of(b * QB, QB)
    keys = kv_scr[pl.ds(first, span), :HD]
    vals = kv_scr[pl.ds(first, span), HD:]
    col = lax.broadcasted_iota(jnp.int32, (QB, span), 1)
    row = lax.broadcasted_iota(jnp.int32, (QB, span), 0)
    allowed = (col >= low_ref[...] - b * QB) & (col <= row + WINDOW)
    for h in range(q_ref.shape[1] // HD):
        scores = dot_nt(q_ref[:, h * HD : (h + 1) * HD], keys) * SCORE_SCALE
        e = jnp.where(allowed, jnp.exp(scores), 0.0)
        total = jnp.sum(e, axis=1, keepdims=True)
        o_ref[:, h * HD : (h + 1) * HD] = (dot(e.astype(B16), vals) / total).astype(B16)


def attn_call(q, far, near, low):
    tok, q_width = q.shape
    return pl.pallas_call(
        attn_kernel,
        grid=(tok // QB,),
        in_specs=[
            pl.BlockSpec((QB, q_width), lambda b: (b, 0)),
            whole(far.shape),
            whole(near.shape),
            pl.BlockSpec((QB, 1), lambda b: (b, 0)),
        ],
        out_specs=pl.BlockSpec((QB, q_width), lambda b: (b, 0)),
        out_shape=sds((tok, q_width), B16),
        scratch_shapes=[pltpu.VMEM((WINDOW + tok, 2 * HD), B16)],
        compiler_params=params(),
        cost_estimate=cost(4 * tok * q_width * (WINDOW + QB), 3e6),
        name="attend",
    )(q, far, near, low)


FC = 512


def ffn_kernel(
    o_ref, x_ref, gd_ref, wo_ref, wg_ref, wu_ref, wd_ref,
    y_ref, h_ref, g_ref, u_ref, z_ref, out_ref, b_scr,
):
    j = pl.program_id(0)

    @pl.when(j == 0)
    def _():
        y = dot(o_ref[...], wo_ref[...])
        y_ref[...] = y
        h = x_ref[...].astype(F32) + y * inv_rms(y) * gd_ref[1:2, :]
        h_ref[...] = h
        b_scr[...] = (h * inv_rms(h) * gd_ref[2:3, :]).astype(B16)

    b = b_scr[...]
    g = dot(b, wg_ref[...])
    u = dot(b, wu_ref[...])
    g_ref[...] = g.astype(B16)
    u_ref[...] = u.astype(B16)
    value = g * 0.5 * (1.0 + jnp.tanh(GELU_C * g * (1.0 + GELU_A * g * g)))
    z = dot((value * u).astype(B16), wd_ref[...])

    @pl.when(j == 0)
    def _():
        z_ref[...] = z

    @pl.when(j > 0)
    def _():
        z_ref[...] += z

    @pl.when(j == pl.num_programs(0) - 1)
    def _():
        zz = z_ref[...]
        out_ref[...] = (h_ref[...] + zz * inv_rms(zz) * gd_ref[3:4, :]).astype(B16)


def ffn_call(o, x, gd, w_out, w_gate, w_up, w_down):
    tok, width = x.shape
    ff = w_gate.shape[1]
    cols = pl.BlockSpec((tok, FC), lambda j: (0, j))
    tw = whole((tok, width))
    return pl.pallas_call(
        ffn_kernel,
        grid=(ff // FC,),
        in_specs=[
            whole(o.shape),
            tw,
            whole(gd.shape),
            whole(w_out.shape),
            pl.BlockSpec((width, FC), lambda j: (0, j)),
            pl.BlockSpec((width, FC), lambda j: (0, j)),
            pl.BlockSpec((FC, width), lambda j: (j, 0)),
        ],
        out_specs=[tw, tw, cols, cols, tw, tw],
        out_shape=[
            sds((tok, width), F32),
            sds((tok, width), F32),
            sds((tok, ff), B16),
            sds((tok, ff), B16),
            sds((tok, width), F32),
            sds((tok, width), B16),
        ],
        scratch_shapes=[pltpu.VMEM((tok, width), B16)],
        compiler_params=params(),
        cost_estimate=cost(2 * tok * width * (o.shape[1] + 3 * ff), 22e6),
        name="feed_forward",
    )(o, x, gd, w_out, w_gate, w_up, w_down)


def ffn_back_kernel(
    c_ref, z_ref, h_ref, y_ref, o_ref, gd_ref, g_ref, u_ref, wo_ref, wg_ref, wu_ref, wd_ref,
    pack_ref, dh_ref, do_ref, gg_ref, dz_scr, bt_scr, db_scr,
):
    j = pl.program_id(0)
    tok, width = c_ref.shape
    part = width // PARTS
    n_gate = PARTS * part
    n_down = (width // LANES) * (FC // PARTS)
    out_rows = o_ref.shape[1] // (PARTS * PARTS)

    @pl.when(j == 0)
    def _():
        dz, post_grad = rms_back(z_ref[...], gd_ref[3:4, :], c_ref[...].astype(F32))
        dz_scr[...] = dz.astype(B16)
        gg_ref[...] = jnp.zeros(gg_ref.shape, F32)
        gg_ref[3:4, :] = post_grad
        h = h_ref[...]
        bt_scr[...] = (h * inv_rms(h) * gd_ref[2:3, :]).T.astype(B16)
        db_scr[...] = jnp.zeros(db_scr.shape, F32)

    dz = dz_scr[...]
    df = dot_nt(dz, wd_ref[...])
    value, slope = gelu_parts(g_ref[...].astype(F32))
    u = u_ref[...].astype(F32)
    f = (value * u).astype(B16)
    du = (df * value).astype(B16)
    dg = (df * u * slope).astype(B16)
    db_scr[...] += dot_nt(dg, wg_ref[...]) + dot_nt(du, wu_ref[...])
    bt = bt_scr[...]
    for first, term in ((0, dg), (n_gate, du)):
        grad = dot(bt, term).astype(B16)
        for p in range(PARTS):
            for t in range(FC // LANES):
                pack_ref[j, p, pl.ds(first + t * part, part), :] = grad[
                    p * part : (p + 1) * part, t * LANES : (t + 1) * LANES
                ]
    grad = dot_tn(f, dz).astype(B16)
    rows = FC // PARTS
    for p in range(PARTS):
        for t in range(width // LANES):
            pack_ref[p, j, pl.ds(2 * n_gate + t * rows, rows), :] = grad[
                p * rows : (p + 1) * rows, t * LANES : (t + 1) * LANES
            ]

    @pl.when(j == pl.num_programs(0) - 1)
    def _():
        add, ffn_grad = rms_back(h_ref[...], gd_ref[2:3, :], db_scr[...])
        dh = c_ref[...].astype(F32) + add
        dh_ref[...] = dh
        dy32, attn_grad = rms_back(y_ref[...], gd_ref[1:2, :], dh)
        dy = dy32.astype(B16)
        gg_ref[1:2, :] = attn_grad
        gg_ref[2:3, :] = ffn_grad
        do_ref[...] = dot_nt(dy, wo_ref[...]).astype(B16)
        og = dot_tn(o_ref[...], dy).astype(B16)
        for f_part in range(PARTS):
            for p in range(PARTS):
                at = (f_part * PARTS + p) * out_rows
                for t in range(width // LANES):
                    pack_ref[p, f_part, pl.ds(2 * n_gate + n_down + t * out_rows, out_rows), :] = (
                        og[at : at + out_rows, t * LANES : (t + 1) * LANES]
                    )


def pack_rows(width, ff, q_width):
    gate = width // PARTS * (ff // PARTS // LANES)
    down = ff // (PARTS * PARTS) * (width // LANES)
    out = q_width // (PARTS * PARTS) * (width // LANES)
    return gate, down, out


def ffn_back_call(c, z, h, y, o, gd, g, u, w_out, w_gate, w_up, w_down):
    tok, width = c.shape
    ff = w_gate.shape[1]
    q_width = o.shape[1]
    gate, down, out = pack_rows(width, ff, q_width)
    pack_shape = (PARTS, PARTS, 2 * gate + down + out, LANES)
    cols = pl.BlockSpec((tok, FC), lambda j: (0, j))
    tw = whole((tok, width))
    return pl.pallas_call(
        ffn_back_kernel,
        grid=(ff // FC,),
        in_specs=[
            tw,
            tw,
            tw,
            tw,
            whole(o.shape),
            whole(gd.shape),
            cols,
            cols,
            whole(w_out.shape),
            pl.BlockSpec((width, FC), lambda j: (0, j)),
            pl.BlockSpec((width, FC), lambda j: (0, j)),
            pl.BlockSpec((FC, width), lambda j: (j, 0)),
        ],
        out_specs=[whole(pack_shape), tw, whole(o.shape), whole(gd.shape)],
        out_shape=[
            sds(pack_shape, B16),
            sds((tok, width), F32),
            sds(o.shape, B16),
            sds(gd.shape, F32),
        ],
        scratch_shapes=[
            pltpu.VMEM((tok, width), B16),
            pltpu.VMEM((width, tok), B16),
            pltpu.VMEM((tok, width), F32),
        ],
        compiler_params=params(),
        cost_estimate=cost(4 * tok * width * (q_width + 3 * ff), 35e6),
        name="feed_forward_back",
    )(c, z, h, y, o, gd, g, u, w_out, w_gate, w_up, w_down)


def attn_back_kernel(
    q_ref, do_ref, qpre_ref, far_ref, near_ref, low_ref, gh_ref, cos_ref, sin_ref,
    dq_ref, dfar_ref, dnear_ref, gg_ref, kv_scr, dkv_scr,
):
    b = pl.program_id(0)

    @pl.when(b == 0)
    def _():
        kv_scr[:WINDOW, :] = far_ref[...]
        kv_scr[WINDOW:, :] = near_ref[...]
        dkv_scr[...] = jnp.zeros(dkv_scr.shape, F32)
        gg_ref[...] = jnp.zeros(gg_ref.shape, F32)

    span = WINDOW + QB
    first = pl.multiple_of(b * QB, QB)
    keys = kv_scr[pl.ds(first, span), :HD]
    vals = kv_scr[pl.ds(first, span), HD:]
    col = lax.broadcasted_iota(jnp.int32, (span, QB), 0)
    row = lax.broadcasted_iota(jnp.int32, (span, QB), 1)
    allowed = (col >= low_ref[...] - b * QB) & (col <= row + WINDOW)
    cos, sin = cos_ref[...], sin_ref[...]
    dkeys = jnp.zeros((span, HD), F32)
    dvals = jnp.zeros((span, HD), F32)
    gain_grad = jnp.zeros((1, HD), F32)
    for h in range(q_ref.shape[1] // HD):
        at = slice(h * HD, (h + 1) * HD)
        q = q_ref[:, at]
        do = do_ref[:, at]
        scores = dot_nt(keys, q) * SCORE_SCALE
        e = jnp.where(allowed, jnp.exp(scores), 0.0)
        p = e * (1.0 / jnp.sum(e, axis=0, keepdims=True))
        dp = dot_nt(vals, do)
        inner = jnp.sum(p * dp, axis=0, keepdims=True)
        ds = (p * (dp - inner)).astype(B16)
        dvals += dot(p.astype(B16), do)
        dkeys += dot(ds, q)
        dq = dot_tn(ds, keys) * SCORE_SCALE
        dq0, gain = rms_back(qpre_ref[:, at].astype(F32), gh_ref[0:1, :], rope_back(dq, cos, sin))
        gain_grad += gain
        dq_ref[:, at] = dq0.astype(B16)
    dkv_scr[pl.ds(first, span), :HD] += dkeys * SCORE_SCALE
    dkv_scr[pl.ds(first, span), HD:] += dvals
    gg_ref[0:1, :] += gain_grad

    @pl.when(b == pl.num_programs(0) - 1)
    def _():
        dfar_ref[...] = dkv_scr[:WINDOW, :].astype(B16)
        dnear_ref[...] = dkv_scr[WINDOW:, :]


def attn_back_call(q, do, qpre, far, near, low_row, gh, cos, sin):
    tok, q_width = q.shape
    block = pl.BlockSpec((QB, q_width), lambda b: (b, 0))
    table = pl.BlockSpec((QB, HD // 2), lambda b: (b, 0))
    return pl.pallas_call(
        attn_back_kernel,
        grid=(tok // QB,),
        in_specs=[
            block,
            block,
            block,
            whole(far.shape),
            whole(near.shape),
            pl.BlockSpec((1, QB), lambda b: (0, b)),
            whole(gh.shape),
            table,
            table,
        ],
        out_specs=[block, whole(far.shape), whole(near.shape), whole(gh.shape)],
        out_shape=[
            sds(q.shape, B16),
            sds(far.shape, B16),
            sds(near.shape, F32),
            sds(gh.shape, F32),
        ],
        scratch_shapes=[
            pltpu.VMEM((WINDOW + tok, 2 * HD), B16),
            pltpu.VMEM((WINDOW + tok, 2 * HD), F32),
        ],
        compiler_params=params(),
        cost_estimate=cost(10 * tok * q_width * (WINDOW + QB), 8e6),
        name="attend_back",
    )(q, do, qpre, far, near, low_row, gh, cos, sin)


def q_back_kernel(a_ref, dq_ref, w_ref, wq_grad_ref, da_ref):
    dq = dq_ref[...]
    wq_grad_ref[...] = dot_tn(a_ref[...], dq).astype(B16)
    da_ref[...] = dot_nt(dq, w_ref[...])


def q_back_call(a, dq, w_qkv):
    tok, width = a.shape
    q_width = dq.shape[1]
    return pl.pallas_call(
        q_back_kernel,
        grid=(1,),
        in_specs=[whole(a.shape), whole(dq.shape), whole((width, q_width))],
        out_specs=[whole((width, q_width)), whole((tok, width))],
        out_shape=[sds((width, q_width), B16), sds((tok, width), F32)],
        compiler_params=params(),
        cost_estimate=cost(4 * tok * width * q_width, 6e6),
        name="queries_back",
    )(a, dq, w_qkv)


def kv_back_kernel(
    a_ref, x_ref, dh_ref, da_ref, dnear_ref, dback_ref, kpre_ref, gd_ref, gh_ref,
    cos_ref, sin_ref, w_ref, wq_ref, pack_ref, dx_ref, gd_grad_ref, gh_grad_ref,
):
    width = x_ref.shape[1]
    part = width // PARTS
    dkv = dnear_ref[...]
    tail = dback_ref[...].astype(F32)
    dkv = dkv + tail
    dk0, k_grad = rms_back(
        kpre_ref[...].astype(F32),
        gh_ref[1:2, :],
        rope_back(dkv[:, :HD], cos_ref[...], sin_ref[...]),
    )
    both = jnp.concatenate([dk0.astype(B16), dkv[:, HD:].astype(B16)], axis=1)
    kv_grad = dot_tn(a_ref[...], both).astype(B16)
    da = da_ref[...] + dot_nt(both, w_ref[...])
    add, in_grad = rms_back(x_ref[...].astype(F32), gd_ref[0:1, :], da)
    dx_ref[...] = (dh_ref[...] + add).astype(B16)
    gd_grad_ref[...] = jnp.zeros(gd_grad_ref.shape, F32)
    gd_grad_ref[0:1, :] = in_grad
    gh_grad_ref[...] = jnp.zeros(gh_grad_ref.shape, F32)
    gh_grad_ref[1:2, :] = k_grad
    q_tiles = wq_ref.shape[1] // LANES
    tiles = q_tiles + 2 * HD // LANES
    each = tiles // PARTS
    for t in range(tiles):
        c_part, slot = t // each, t % each
        for p in range(PARTS):
            rows = slice(p * part, (p + 1) * part)
            if t < q_tiles:
                piece = wq_ref[rows, t * LANES : (t + 1) * LANES]
            else:
                piece = kv_grad[rows, (t - q_tiles) * LANES : (t - q_tiles + 1) * LANES]
            pack_ref[c_part, p, slot * part : (slot + 1) * part, :] = piece


def kv_back_call(a, x, dh, da, dnear, dback, kpre, gd, gh, cos, sin, w_qkv, wq_grad):
    tok, width = a.shape
    q_width = wq_grad.shape[1]
    part = width // PARTS
    pack_shape = (PARTS, PARTS, part * ((q_width + 2 * HD) // LANES // PARTS), LANES)
    tw = whole((tok, width))
    return pl.pallas_call(
        kv_back_kernel,
        grid=(1,),
        in_specs=[
            tw,
            tw,
            tw,
            tw,
            whole(dnear.shape),
            whole(dback.shape),
            whole(kpre.shape),
            whole(gd.shape),
            whole(gh.shape),
            whole(cos.shape),
            whole(sin.shape),
            pl.BlockSpec((width, 2 * HD), lambda j: (0, q_width // (2 * HD))),
            whole(wq_grad.shape),
        ],
        out_specs=[whole(pack_shape), tw, whole(gd.shape), whole(gh.shape)],
        out_shape=[
            sds(pack_shape, B16),
            sds((tok, width), B16),
            sds(gd.shape, F32),
            sds(gh.shape, F32),
        ],
        compiler_params=params(),
        cost_estimate=cost(8 * tok * width * HD, 10e6),
        name="keys_values_back",
    )(a, x, dh, da, dnear, dback, kpre, gd, gh, cos, sin, w_qkv, wq_grad)


def pack_own(qkv, gains, gate, up, down, out):
    def by_cols(w):
        rows, cols = w.shape
        tiles = cols // (PARTS * LANES)
        return (
            w.reshape(rows, PARTS, tiles, LANES)
            .transpose(1, 2, 0, 3)
            .reshape(PARTS, tiles * rows, LANES)
        )

    def by_rows(w):
        rows, cols = w.shape
        n = rows // PARTS
        return (
            w.reshape(PARTS, n, cols // LANES, LANES)
            .transpose(0, 2, 1, 3)
            .reshape(PARTS, cols // LANES * n, LANES)
        )

    gain_rows = jnp.broadcast_to(gains[None], (PARTS,) + gains.shape)
    return (
        jnp.concatenate([by_cols(qkv), gain_rows], axis=1),
        jnp.concatenate([by_cols(gate), by_cols(up), by_rows(down), by_rows(out)], axis=1),
    )


def pick(spot_ref, j):
    return lax.rem(spot_ref[0] - j + PARTS, PARTS)


def piece_specs(rows):
    def own_map(j, spot):
        return (jnp.where(spot[2] == 1, pick(spot, j), 0), 0, 0, 0)

    def other_map(j, spot):
        return (jnp.where(spot[2] == 1, 0, pick(spot, j)), 0, 0, 0)

    shape = (1, PARTS, rows, LANES)
    return [pl.BlockSpec(shape, own_map), pl.BlockSpec(shape, other_map)]


def unpack_qkv_kernel(spot, own_ref, other_ref, w_ref, gain_ref):
    part = w_ref.shape[0] // PARTS

    def take(ref):
        for p in range(PARTS):
            d = lax.rem(spot[1] - p + PARTS, PARTS)
            for t in range(w_ref.shape[1] // LANES):
                w_ref[p * part : (p + 1) * part, t * LANES : (t + 1) * LANES] = ref[
                    0, d, t * part : (t + 1) * part, :
                ]
            gain_ref[p] = ref[0, d, ref.shape[2] - GAIN_ROWS :, :]

    pl.when(spot[2] == 1)(lambda: take(own_ref))
    pl.when(spot[2] == 0)(lambda: take(other_ref))


def unpack_qkv(spot, own, other, width, cols):
    return pl.pallas_call(
        unpack_qkv_kernel,
        grid_spec=pltpu.PrefetchScalarGridSpec(
            num_scalar_prefetch=1,
            grid=(PARTS,),
            in_specs=piece_specs(own.shape[2]),
            out_specs=[
                pl.BlockSpec((width, cols // PARTS), lambda j, spot: (0, j)),
                pl.BlockSpec((PARTS, GAIN_ROWS, LANES), lambda j, spot: (0, 0, 0)),
            ],
        ),
        out_shape=[sds((width, cols), B16), sds((PARTS, GAIN_ROWS, LANES), B16)],
        compiler_params=params(),
        cost_estimate=cost(0, 6e6),
        name="place_qkv",
    )(spot, own, other)


def unpack_ffn_kernel(spot, own_ref, other_ref, gate_ref, up_ref, down_ref, out_ref):
    width, cols = gate_ref.shape
    part = width // PARTS
    tiles = cols // LANES
    n_gate = tiles * part

    def take(ref):
        for p in range(PARTS):
            d = lax.rem(spot[1] - p + PARTS, PARTS)
            for n, w_ref in enumerate((gate_ref, up_ref)):
                for t in range(tiles):
                    at = n * n_gate + t * part
                    w_ref[p * part : (p + 1) * part, t * LANES : (t + 1) * LANES] = ref[
                        0, d, at : at + part, :
                    ]
            at = 2 * n_gate
            for w_ref in (down_ref, out_ref):
                rows = w_ref.shape[2]
                for t in range(width // LANES):
                    w_ref[p, 0, :, t * LANES : (t + 1) * LANES] = ref[0, d, at : at + rows, :]
                    at += rows

    pl.when(spot[2] == 1)(lambda: take(own_ref))
    pl.when(spot[2] == 0)(lambda: take(other_ref))


def unpack_ffn(spot, own, other, width, ff, q_width):
    cols = pl.BlockSpec((width, ff // PARTS), lambda j, spot: (0, j))

    def rows(n):
        return pl.BlockSpec((PARTS, 1, n // PARTS**2, width), lambda j, spot: (0, j, 0, 0))

    gate, up, down, out = pl.pallas_call(
        unpack_ffn_kernel,
        grid_spec=pltpu.PrefetchScalarGridSpec(
            num_scalar_prefetch=1,
            grid=(PARTS,),
            in_specs=piece_specs(own.shape[2]),
            out_specs=[cols, cols, rows(ff), rows(q_width)],
        ),
        out_shape=[
            sds((width, ff), B16),
            sds((width, ff), B16),
            sds((PARTS, PARTS, ff // PARTS**2, width), B16),
            sds((PARTS, PARTS, q_width // PARTS**2, width), B16),
        ],
        compiler_params=params(),
        cost_estimate=cost(0, 22e6),
        name="place_ffn",
    )(spot, own, other)
    return gate, up, down.reshape(ff, width), out.reshape(q_width, width)


def split_pack(pack, width, ff, q_width):
    gate, down, out = pack_rows(width, ff, q_width)
    part = width // PARTS

    def cols(p):
        tiles = p.shape[2] // part
        return (
            p.reshape(PARTS, PARTS, tiles, part, LANES)
            .transpose(1, 3, 0, 2, 4)
            .reshape(width, PARTS * tiles * LANES)
        )

    def rows(p):
        n = p.shape[2] // (width // LANES)
        return (
            p.reshape(PARTS, PARTS, width // LANES, n, LANES)
            .transpose(1, 0, 3, 2, 4)
            .reshape(PARTS * PARTS * n, width)
        )

    return (
        cols(pack[:, :, :gate]),
        cols(pack[:, :, gate : 2 * gate]),
        rows(pack[:, :, 2 * gate : 2 * gate + down]),
        rows(pack[:, :, 2 * gate + down :]),
    )


def moved(array, axis, by, layer):
    sizes = [lax.axis_size(name) for name in AXES]
    pairs = []
    for f in range(sizes[1]):
        for c in range(sizes[2]):
            f2 = (f + by) % sizes[1] if axis == "fsdp" else f
            c2 = (c + by) % sizes[2] if axis == "ctx" else c
            pairs.append(
                ((layer * sizes[1] + f) * sizes[2] + c, (layer * sizes[1] + f2) * sizes[2] + c2)
            )
    return lax.ppermute(array, AXES, pairs)


def handed(array, to):
    return lax.ppermute(array, "section", [(1 - to, to)])


def passed_along(array, by):
    devices = lax.axis_size("ctx")
    pairs = [(i, i + by) for i in range(devices) if 0 <= i + by < devices]
    return lax.ppermute(array, "ctx", pairs)


def gathered_pieces(own, layer):
    shards = [own[0]] + [moved(own[0], "fsdp", d, layer) for d in range(1, PARTS)]
    travelling = jnp.stack(shards[1:])
    quarters = [jnp.stack(shards)]
    for e in range(1, PARTS):
        quarters.append(jnp.concatenate([own[e][None], moved(travelling, "ctx", e, layer)]))
    return jnp.stack(quarters)


def at(array, index):
    return lax.dynamic_index_in_dim(array, lax.rem(index, PARTS), 0, keepdims=False)


def reduced_pieces(pack, layer, fsdp_index, ctx_index):
    other = handed(pack, layer)

    def both(index):
        return at(pack, index).astype(F32) + at(other, index).astype(F32)

    total = both(ctx_index)
    for e in range(1, PARTS):
        total += moved(both(ctx_index + e).astype(B16), "ctx", e, layer).astype(F32)
    rounded = total.astype(B16)
    piece = at(total, fsdp_index)
    for d in range(1, PARTS):
        piece += moved(at(rounded, fsdp_index + d), "fsdp", d, layer).astype(F32)
    piece = piece.astype(B16)
    ring = jnp.stack([piece] + [moved(piece, "ctx", e, layer) for e in range(1, PARTS)])
    return jnp.stack([at(ring, ctx_index - p + PARTS) for p in range(PARTS)])


def per_device(
    inputs,
    grad_out,
    lengths,
    in_gain,
    query_weight,
    key_weight,
    value_weight,
    query_gain,
    key_gain,
    out_weight,
    attn_gain,
    ffn_gain,
    gate_weight,
    up_weight,
    down_weight,
    post_gain,
):
    section = lax.axis_index("section")
    fsdp_index = lax.axis_index("fsdp")
    ctx_index = lax.axis_index("ctx")
    shards = lax.axis_size("fsdp")
    in_pieces = shards == PARTS and lax.axis_size("ctx") == PARTS
    tok = inputs.shape[2]
    width = inputs.shape[3]
    q_width = query_weight.shape[2]
    ff = gate_weight.shape[2]
    first_layer = section == 0

    qkv_own = jnp.concatenate([query_weight[0], key_weight[0], value_weight[0]], axis=1)
    gain_own = jnp.concatenate(
        [in_gain[0], attn_gain[0], ffn_gain[0], post_gain[0], query_gain[0], key_gain[0]]
    )

    def as_gains(raw):
        n, m = width // shards, HD // shards
        gd = [raw[:, i * n : (i + 1) * n].reshape(1, width) for i in range(4)]
        gh = [raw[:, 4 * n + i * m : 4 * n + (i + 1) * m].reshape(1, HD) for i in range(2)]
        gd = jnp.concatenate(gd + [jnp.zeros((4, width), raw.dtype)]).astype(F32)
        gh = jnp.concatenate(gh + [jnp.zeros((6, HD), raw.dtype)]).astype(F32)
        return gd, gh

    layers = []
    if in_pieces:
        gain_rows = jnp.pad(gain_own, (0, GAIN_ROWS * LANES - gain_own.shape[0]))
        packs = pack_own(
            qkv_own,
            gain_rows.reshape(GAIN_ROWS, LANES),
            gate_weight[0],
            up_weight[0],
            down_weight[0],
            out_weight[0],
        )

        def own_first(pack):
            back = pack[::-1]
            return lax.dynamic_slice_in_dim(
                jnp.concatenate([back, back]), PARTS - 1 - ctx_index, PARTS, 0
            )

        packs = [own_first(pack) for pack in packs]
        for layer in range(2):
            spot = jnp.stack([ctx_index, fsdp_index, (section == layer).astype(jnp.int32)])
            spot = spot.astype(jnp.int32)
            pieces = gathered_pieces(packs[0], layer)
            other = handed(pieces, 1 - layer)
            w_qkv, raw = unpack_qkv(spot, pieces, other, width, qkv_own.shape[1])
            gains = as_gains(raw.reshape(PARTS, GAIN_ROWS * LANES))
            pieces = gathered_pieces(packs[1], layer)
            other = handed(pieces, 1 - layer)
            gate, up, down, out = unpack_ffn(spot, pieces, other, width, ff, q_width)
            layers.append((w_qkv, out, gate, up, down) + gains)
    else:

        def whole_weight(own):
            full = lax.all_gather(own, "fsdp", axis=0, tiled=True)
            return lax.all_gather(full, "section", axis=0)

        full = [
            whole_weight(w)
            for w in (qkv_own, out_weight[0], gate_weight[0], up_weight[0], down_weight[0])
        ]
        raw = whole_weight(gain_own[None])
        for layer in range(2):
            layers.append(tuple(w[layer] for w in full) + as_gains(raw[layer]))

    def own_row(array):
        return lax.dynamic_index_in_dim(array[:, 0], section, 0, keepdims=False)

    offset, low = layout_for(own_row(lengths), ctx_index * tok, tok)
    cos, sin = rope_tables(offset)
    low_col, low_row = low[:, None], low[None, :]

    x = own_row(inputs)
    kept = []
    for w_qkv, w_out, w_gate, w_up, w_down, gd, gh in layers:
        a, kpre, near = kv_call(x, gd, gh, cos, sin, w_qkv)
        far = passed_along(near, 1)
        qpre, q = q_call(a, gh, cos, sin, w_qkv)
        o = attn_call(q, far, near, low_col)
        y, h, g, u, z, result = ffn_call(o, x, gd, w_out, w_gate, w_up, w_down)
        kept.append((x, a, kpre, near, far, qpre, q, o, y, h, g, u, z, result))
        x = result

    cot = own_row(grad_out)
    packs, in_grads, gain_grads = [None] * 2, [None] * 2, [None] * 2
    for layer in (1, 0):
        w_qkv, w_out, w_gate, w_up, w_down, gd, gh = layers[layer]
        x, a, kpre, near, far, qpre, q, o, y, h, g, u, z, result = kept[layer]
        ffn_pack, dh, do, gd_one = ffn_back_call(
            cot, z, h, y, o, gd, g, u, w_out, w_gate, w_up, w_down
        )
        dq, dfar, dnear, gh_one = attn_back_call(q, do, qpre, far, near, low_row, gh, cos, sin)
        dback = passed_along(dfar, -1)
        if tok > WINDOW:
            dback = jnp.pad(dback, ((tok - WINDOW, 0), (0, 0)))
        wq_grad, da = q_back_call(a, dq, w_qkv)
        qkv_pack, cot, gd_two, gh_two = kv_back_call(
            a, x, dh, da, dnear, dback, kpre, gd, gh, cos, sin, w_qkv, wq_grad
        )
        in_grads[layer] = cot
        packs[layer] = (ffn_pack, qkv_pack)
        gain_grads[layer] = jnp.concatenate(
            [(gd_one + gd_two)[:4].reshape(-1), (gh_one + gh_two)[:2].reshape(-1)]
        )

    def by_layer(first, second):
        own = jnp.where(first_layer, first, second)
        got = lax.ppermute(jnp.where(first_layer, second, first), "section", [(0, 1), (1, 0)])
        return jnp.stack([jnp.where(first_layer, own, got), jnp.where(first_layer, got, own)])

    activations = by_layer(kept[0][-1], kept[1][-1])
    input_grads = by_layer(in_grads[0], in_grads[1])

    gain_sums = lax.psum(jnp.stack(gain_grads), AXES)
    gain_sums = lax.dynamic_index_in_dim(gain_sums, section, 0, keepdims=False)

    def gain_shard(first, n):
        return lax.dynamic_slice_in_dim(gain_sums, first + fsdp_index * n, n, 0)[None]

    dn, hn = width // shards, HD // shards
    d_gains = [gain_shard(i * width, dn) for i in range(4)]
    h_gains = [gain_shard(4 * width + i * HD, hn) for i in range(2)]

    if in_pieces:
        done = [None] * 2
        for layer in (1, 0):
            done[layer] = tuple(
                reduced_pieces(p, layer, fsdp_index, ctx_index) for p in packs[layer]
            )
        ffn_own, qkv_own = (jnp.where(first_layer, p, r) for p, r in zip(*done))
        n_gate, n_down, n_out = pack_rows(width, ff, q_width)
        part = width // PARTS

        def cols(p):
            tiles = p.shape[1] // part
            return p.reshape(PARTS, tiles, part, LANES).transpose(2, 0, 1, 3).reshape(part, -1)

        def rows(p):
            n = p.shape[1] // (width // LANES)
            return (
                p.reshape(PARTS, width // LANES, n, LANES).transpose(0, 2, 1, 3).reshape(-1, width)
            )

        gate_g = cols(ffn_own[:, :n_gate])
        up_g = cols(ffn_own[:, n_gate : 2 * n_gate])
        down_g = rows(ffn_own[:, 2 * n_gate : 2 * n_gate + n_down])
        out_g = rows(ffn_own[:, 2 * n_gate + n_down :])
        qkv_g = cols(qkv_own)
    else:
        sums = []
        for ffn_pack, qkv_pack in packs:
            gate, up, down, out = split_pack(ffn_pack, width, ff, q_width)
            part = width // PARTS
            tiles = qkv_pack.shape[2] // part
            qkv = (
                qkv_pack.reshape(PARTS, PARTS, tiles, part, LANES)
                .transpose(1, 3, 0, 2, 4)
                .reshape(width, -1)
            )
            sums.append((gate, up, down, out, qkv))
        shard = [
            lax.psum_scatter(
                lax.psum_scatter(jnp.stack(pair), "section", scatter_dimension=0, tiled=True)[0],
                "fsdp",
                scatter_dimension=0,
                tiled=True,
            )
            for pair in zip(*sums)
        ]
        gate_g, up_g, down_g, out_g, qkv_g = lax.psum(tuple(shard), "ctx")

    gate_g, up_g, down_g, out_g, qkv_g = (
        w.astype(F32)[None] for w in (gate_g, up_g, down_g, out_g, qkv_g)
    )
    return (
        activations[None, :, None],
        input_grads[None, :, None],
        d_gains[0],
        qkv_g[:, :, :q_width],
        qkv_g[:, :, q_width : q_width + HD],
        qkv_g[:, :, q_width + HD :],
        h_gains[0],
        h_gains[1],
        out_g,
        d_gains[1],
        d_gains[2],
        gate_g,
        up_g,
        down_g,
        d_gains[3],
    )


def solution(mesh):
    return jax.shard_map(
        per_device,
        mesh=mesh,
        in_specs=(
            P(None, "fsdp", "ctx", None),
            P(None, "fsdp", "ctx", None),
            P(None, "fsdp", None),
            P("section", "fsdp"),
            P("section", "fsdp", None),
            P("section", "fsdp", None),
            P("section", "fsdp", None),
            P("section", "fsdp"),
            P("section", "fsdp"),
            P("section", "fsdp", None),
            P("section", "fsdp"),
            P("section", "fsdp"),
            P("section", "fsdp", None),
            P("section", "fsdp", None),
            P("section", "fsdp", None),
            P("section", "fsdp"),
        ),
        out_specs=(
            P("section", None, "fsdp", "ctx", None),
            P("section", None, "fsdp", "ctx", None),
            P("section", "fsdp"),
            P("section", "fsdp", None),
            P("section", "fsdp", None),
            P("section", "fsdp", None),
            P("section", "fsdp"),
            P("section", "fsdp"),
            P("section", "fsdp", None),
            P("section", "fsdp"),
            P("section", "fsdp"),
            P("section", "fsdp", None),
            P("section", "fsdp", None),
            P("section", "fsdp", None),
            P("section", "fsdp"),
        ),
        check_vma=False,
    )
```

time: 1370 us -> 814 us (0.59)
  waiting for transfers between devices: 631 us -> 222 us
  matrix products: 222 us -> 0 us
  Pallas kernels: 0 us -> 185 us
  starting transfers between devices: 37.6 us -> 191 us
  local copies, waits for them, and re-layouts: 182 us -> 38.2 us
  other arithmetic: 183 us -> 76.9 us
  loops' own time: 31.1 us -> 0 us
  blocking collectives: 57.5 us -> 87.1 us
    reduce_scatter x7 -> x0, waiting for transfers between devices: 251 us -> none  [per_device(): lax.psum_scatter(as_sent(stacked), 'fsdp', scatter_dimension=1, tiled=True)]
    dot_general x84 -> x0, matrix products: 222 us -> none  [the longest x3 22.6 us: layer_back(): jnp.einsum('td,fd->tf', d_down, down_weight, preferred_element_type=jnp.f...]
    ppermute x18 -> x74, waiting for transfers between devices: 0.05 us -> 222 us  [the longest x60 201 us: moved(): return lax.ppermute(array, AXES, pairs)]
    all_gather x5 -> x0, waiting for transfers between devices: 190 us -> none  [the longest x1 55.4 us: per_device(): lax.all_gather(gate_weight, 'fsdp', axis=1, tiled=True)]
    pallas_call x0 -> x20, Pallas kernels: none -> 185 us  [the longest x2 49.5 us: ffn_back_call(): pl.pallas_call(ffn_back_kernel, grid=(ff // FC,), in_specs=[tw, tw, tw, t...]
    ppermute x18 -> x74, starting transfers between devices: 36.8 us -> 191 us  [the longest x60 145 us: moved(): return lax.ppermute(array, AXES, pairs)]
    unnamed x25 -> x0, waiting for transfers between devices: 120 us -> none
    psum x1, blocking collectives: 10.1 us -> 87.1 us  [per_device(): gain_sums = lax.psum(jnp.stack(gain_grads), AXES)]
  transfers between devices with their start and end apart: 37 -> 74, of which waited for: 18 -> 22; matrix products, arithmetic and copies ran while one was open for 24% -> 9% of each run, Pallas kernels for 0% -> 17%
where the time goes in v1:
time: 814 us; the launch traced here: 803 us
  waiting for transfers between devices  222 us (27%)
  starting transfers between devices  191 us (23%)
  Pallas kernels  185 us (23%)
  blocking collectives  87.1 us (11%)
  other arithmetic  76.9 us (9%)
  local copies, waits for them, and re-layouts  38.2 us (5%)
    ppermute x60, waiting for transfers between devices, moved(): return lax.ppermute(array, AXES, pairs)  201 us
    ppermute x60, starting transfers between devices, moved(): return lax.ppermute(array, AXES, pairs)  145 us
    psum x1, blocking collectives, per_device(): gain_sums = lax.psum(jnp.stack(gain_grads), AXES)  87.1 us
    pallas_call x2, Pallas kernels, ffn_back_call(): pl.pallas_call(ffn_back_kernel, grid=(ff // FC,), in_specs=[tw, tw, tw, t...  49.5 us
    ppermute x8, starting transfers between devices, handed(): return lax.ppermute(array, 'section', [(1 - to, to)])  36.3 us
    pallas_call x2, Pallas kernels, attn_back_call(): pl.pallas_call(attn_back_kernel, grid=(tok // QB,), in_specs=[block, bloc...  29 us
    pallas_call x2, Pallas kernels, ffn_call(): pl.pallas_call(ffn_kernel, grid=(ff // FC,), in_specs=[whole(o.shape), tw...  27.3 us
    convert_element_type x4, other arithmetic, reduced_pieces(): total += moved(both(ctx_index + e).astype(B16), 'ctx', e, layer).astype(F32)  23.6 us
  transfers between devices with their start and end apart: 74, of which 22 were waited for; matrix products, arithmetic and copies ran while one was open for 9% of the time, Pallas kernels for 17%

profile of v1, /device:TPU:0, one launch (start us, length us, event | category | flops | bytes accessed | tf_op | source)
XLA Modules:
  0.0 803.0 jit_solution(4257273623143794541)
XLA Ops:
  22.0 7.0 collective-permute-start.10
  34.8 7.6 collective-permute-done.10
  42.4 33.4 %collective-permute-done.9 = bf16[2240,128]{1,0:T(8,128)(2,1)S(1)} collective-permute-done((bf16[2240,128]{1,0:T(8,128)(2,1)S(1)}, bf16[2240,128]{1,0:T(8,128)(2,1)S(1)}, u32[]{:S(2)}, u32[]{:S(2)}) %collective-permute-start.9) | collective-permute-done | bytes 573472 | tf_op jit(solution)/shard_map/ppermute | solution.py:748
  87.4 31.0 %collective-permute-done.13 = bf16[3,2240,128]{2,1,0:T(8,128)(2,1)S(1)} collective-permute-done((bf16[3,2240,128]{2,1,0:T(8,128)(2,1)S(1)}, bf16[3,2240,128]{2,1,0:T(8,128)(2,1)S(1)}, u32[]{:S(2)}, u32[]{:S(2)}) %collective-permute-start.13) | collective-permute-done | bytes 1720352 | tf_op jit(solution)/shard_map/ppermute | solution.py:748
  118.8 37.3 %collective-permute-done.12 = bf16[3,2240,128]{2,1,0:T(8,128)(2,1)S(1)} collective-permute-done((bf16[3,2240,128]{2,1,0:T(8,128)(2,1)S(1)}, bf16[3,2240,128]{2,1,0:T(8,128)(2,1)S(1)}, u32[]{:S(2)}, u32[]{:S(2)}) %collective-permute-start.12) | collective-permute-done | bytes 1720352 | tf_op jit(solution)/shard_map/ppermute | solution.py:748
  156.9 4.5 pad_maximum_fusion.own_ref
  161.4 4.9 collective-permute-start.14
  166.3 4.6 pad_maximum_fusion.1.own_ref
  177.4 8.7 %collective-permute-start.1 = (bf16[496,128]{1,0:T(8,128)(2,1)S(1)}, bf16[496,128]{1,0:T(8,128)(2,1)S(1)}, u32[]{:S(2)}, u32[]{:S(2)}) collective-permute-start(bf16[496,128]{1,0:T(8,128)(2,1)S(1)} %get-tuple-element.271), channel_id=1, source_target_pairs={{0,8},{1,9},{2,10},{3,11},{4,12},{5,13},{6,14},{7,15},{8,0},{9,1},... | collective-permute-start | bytes 380936 | tf_op jit(solution)/shard_map/ppermute | solution.py:748
  200.0 6.0 collective-permute-done.5
  210.6 5.9 collective-permute-done.3
  218.9 11.3 %collective-permute-start.6 = (bf16[4,4,496,128]{3,2,1,0:T(8,128)(2,1)}, bf16[4,4,496,128]{3,2,1,0:T(8,128)(2,1)}, u32[]{:S(2)}, u32[]{:S(2)}) collective-permute-start(bf16[4,4,496,128]{3,2,1,0:T(8,128)(2,1)} %pad_maximum_fusion.13.own_ref), channel_id=1, source_target_pairs={{0,16},{1,17},{2,18},{3,19},{4,20},{5,21},{6,22},{7,23},{8,24},{9,... | collective-permute-start | bytes 6094856 | tf_op jit(solution)/shard_map/ppermute | solution.py:752
  238.4 4.8 place_qkv.2
  245.3 4.8 place_qkv.3
  259.4 4.8 queries.2
  269.4 6.4 attend.2.o_ref
  275.8 9.3 %place_ffn.2 = (bf16[640,2048]{1,0:T(8,128)(2,1)}, bf16[640,2048]{1,0:T(8,128)(2,1)}, bf16[4,4,128,640]{3,2,1,0:T(8,128)(2,1)}, bf16[4,4,64,640]{3,2,1,0:T(8,128)(2,1)}) custom-call(s32[3]{0:T(128)} %pad_add_fusion.spot, bf16[4,4,2240,128]{3,2,1,0:T(8,128)(2,1)} %pad_maximum_fusion.own_ref, bf16[4,4,2240,128]{3,2,1,0:T(8,128)(2,1)} %collective-permute-done.14.other_ref), custom_call_target="tpu_custom_call" | custom-call | bytes 22000000 | tf_op jit(solution)/shard_map/place_ffn/pallas_call | solution.py:689
  285.1 13.7 %feed_forward.2 = (f32[512,640]{1,0:T(8,128)}, f32[512,640]{1,0:T(8,128)}, bf16[512,2048]{1,0:T(8,128)(2,1)}, bf16[512,2048]{1,0:T(8,128)(2,1)}, f32[512,640]{1,0:T(8,128)}, /*index=5*/bf16[512,640]{1,0:T(8,128)(2,1)}) custom-call(bf16[512,1024]{1,0:T(8,128)(2,1)} %attend.2.o_ref, bf16[512,640]{1,0:T(8,128)(2,1)} %dynamic-slice_bitcast_fusion.1.x_ref, ...), custom_call_target="tpu_custom_call" | custom-call | flops 4697620480 | bytes 22000000 | tf_op jit(solution)/shard_map/feed_forward/pallas_call | solution.py:258
  302.0 4.5 collective-permute-start.22
  307.4 9.3 %place_ffn.3 = (bf16[640,2048]{1,0:T(8,128)(2,1)}, bf16[640,2048]{1,0:T(8,128)(2,1)}, bf16[4,4,128,640]{3,2,1,0:T(8,128)(2,1)}, bf16[4,4,64,640]{3,2,1,0:T(8,128)(2,1)}) custom-call(s32[3]{0:T(128)} %pad_add_fusion.2.spot, bf16[4,4,2240,128]{3,2,1,0:T(8,128)(2,1)} %pad_maximum_fusion.1.own_ref, bf16[4,4,2240,128]{3,2,1,0:T(8,128)(2,1)} %collective-permute-done.29.other_ref), custom_call_target="tpu_custom_call" | custom-call | bytes 22000000 | tf_op jit(solution)/shard_map/place_ffn/pallas_call | solution.py:689
  316.7 4.8 queries.3
  322.3 6.4 attend.3.o_ref
  328.7 13.6 %feed_forward.3 = (f32[512,640]{1,0:T(8,128)}, f32[512,640]{1,0:T(8,128)}, bf16[512,2048]{1,0:T(8,128)(2,1)}, bf16[512,2048]{1,0:T(8,128)(2,1)}, f32[512,640]{1,0:T(8,128)}, /*index=5*/bf16[512,640]{1,0:T(8,128)(2,1)}) custom-call(bf16[512,1024]{1,0:T(8,128)(2,1)} %attend.3.o_ref, bf16[512,640]{1,0:T(8,128)(2,1)} %get-tuple-element.86.x_ref, ...), custom_call_target="tpu_custom_call" | custom-call | flops 4697620480 | bytes 22000000 | tf_op jit(solution)/shard_map/feed_forward/pallas_call | solution.py:258
  342.4 24.6 %feed_forward_back.2 = (bf16[4,4,2240,128]{3,2,1,0:T(8,128)(2,1)}, f32[512,640]{1,0:T(8,128)}, bf16[512,1024]{1,0:T(8,128)(2,1)}, f32[8,640]{1,0:T(8,128)}) custom-call(bf16[512,640]{1,0:T(8,128)(2,1)} %dynamic-slice_bitcast_fusion.c_ref, f32[512,640]{1,0:T(8,128)} %get-tuple-element.97.z_ref, f32[512,640]{1,0:T(8,128)} %get-tuple-element.98.h_ref, ...), custom_call_target="tpu_custom_call" | custom-call | flops 9395240960 | bytes 35000000 | tf_op jit(solution)/shard_map/feed_forward_back/pallas_call | solution.py:366
  367.0 6.9 collective-permute-start.64
  374.4 14.5 %attend_back.2 = (bf16[512,1024]{1,0:T(8,128)(2,1)}, bf16[512,512]{1,0:T(8,128)(2,1)}, f32[512,512]{1,0:T(8,128)}, f32[8,256]{1,0:T(8,128)}) custom-call(bf16[512,1024]{1,0:T(8,128)(2,1)} %get-tuple-element.90.q_ref, bf16[512,1024]{1,0:T(8,128)(2,1)} %get-tuple-element.103.do_ref, bf16[512,1024]{1,0:T(8,128)(2,1)} %get-tuple-element.104.qpre_ref, ...), custom_call_target="tpu_custom_call" | custom-call | flops 3355443200 | bytes 8000000 | tf_op jit(solution)/shard_map/attend_back/pallas_call | solution.py:455
  390.2 4.6 queries_back.2
  394.8 6.3 collective-permute-done.31.dback_ref
  401.9 6.5 keys_values_back.2
  408.4 24.9 %feed_forward_back.3 = (bf16[4,4,2240,128]{3,2,1,0:T(8,128)(2,1)}, f32[512,640]{1,0:T(8,128)}, bf16[512,1024]{1,0:T(8,128)(2,1)}, f32[8,640]{1,0:T(8,128)}) custom-call(bf16[512,640]{1,0:T(8,128)(2,1)} %get-tuple-element.111.c_ref, f32[512,640]{1,0:T(8,128)} %get-tuple-element.112.z_ref, f32[512,640]{1,0:T(8,128)} %get-tuple-element.113.h_ref, ...), custom_call_target="tpu_custom_call" | custom-call | flops 9395240960 | bytes 35000000 | tf_op jit(solution)/shard_map/feed_forward_back/pallas_call | solution.py:366
  434.6 8.1 %collective-permute-start.44 = (bf16[4,4,480,128]{3,2,1,0:T(8,128)(2,1)}, bf16[4,4,480,128]{3,2,1,0:T(8,128)(2,1)}, u32[]{:S(2)}, u32[]{:S(2)}) collective-permute-start(bf16[4,4,480,128]{3,2,1,0:T(8,128)(2,1)} %get-tuple-element.136), channel_id=1, source_target_pairs={{0,16},{1,17},{2,18},{3,19},{4,20},{5,21},{6,22},{7,23},{8,24},{9,... | collective-permute-start | bytes 5898248 | tf_op jit(solution)/shard_map/ppermute | solution.py:752
  442.9 14.5 %attend_back.3 = (bf16[512,1024]{1,0:T(8,128)(2,1)}, bf16[512,512]{1,0:T(8,128)(2,1)}, f32[512,512]{1,0:T(8,128)}, f32[8,256]{1,0:T(8,128)}) custom-call(bf16[512,1024]{1,0:T(8,128)(2,1)} %get-tuple-element.80.q_ref, bf16[512,1024]{1,0:T(8,128)(2,1)} %get-tuple-element.118.do_ref, bf16[512,1024]{1,0:T(8,128)(2,1)} %get-tuple-element.119.qpre_ref, ...), custom_call_target="tpu_custom_call" | custom-call | flops 3355443200 | bytes 8000000 | tf_op jit(solution)/shard_map/attend_back/pallas_call | solution.py:455
  459.5 4.6 queries_back.3
  464.1 10.7 %collective-permute-done.32.dback_ref = bf16[512,512]{1,0:T(8,128)(2,1)S(1)} collective-permute-done((bf16[512,512]{1,0:T(8,128)(2,1)}, bf16[512,512]{1,0:T(8,128)(2,1)S(1)}, u32[]{:S(2)}, u32[]{:S(2)}) %collective-permute-start.32) | collective-permute-done | bytes 524320 | tf_op jit(solution)/shard_map/ppermute | solution.py:758
  475.5 6.6 keys_values_back.3
  497.5 4.7 collective-permute-start.35
  502.1 8.9 %fusion.19 = (bf16[4,2240,128]{2,1,0:T(8,128)(2,1)}, bf16[4,2240,128]{2,1,0:T(8,128)(2,1)}, bf16[4,2240,128]{2,1,0:T(8,128)(2,1)}) fusion(bf16[4,4,2240,128]{3,2,1,0:T(8,128)(2,1)} %collective-permute-done.64, s32[]{:T(128)S(6)} %select_n.207, bf16[4,4,2240,128]{3,2,1,0:T(8,128)(2,1)} %get-tuple-element.138, s32[]{:T(128)S(6)} %select_n.209, s32[]{:T(128)S(6)} %select_n.208), kind=kLoop, calls=%fused_computation.39 | loop fusion | flops 13762560 | bytes 20643852 | tf_op jit(solution)/shard_map/convert_element_type | solution.py:782
  518.4 87.1 %psum.7 = f32[2,3072]{1,0:T(2,128)S(1)} all-reduce(f32[2,3072]{1,0:T(2,128)S(1)} %pad_maximum_fusion.31), channel_id=1, replica_groups=mesh['section'=2,'fsdp'=4,'ctx'=4] {'section','fsdp','ctx'}, use_global_device_ids=true, to_apply=%region_3.4 | all-reduce | flops 6144 | bytes 49152 | tf_op jit(solution)/shard_map/psum | solution.py:926
  617.7 4.5 collective-permute-start.40
  648.4 8.9 %fusion.16 = (bf16[4,2240,128]{2,1,0:T(8,128)(2,1)}, bf16[4,2240,128]{2,1,0:T(8,128)(2,1)}, bf16[4,2240,128]{2,1,0:T(8,128)(2,1)}) fusion(bf16[4,4,2240,128]{3,2,1,0:T(8,128)(2,1)} %collective-permute-done.54, s32[]{:T(128)S(6)} %select_n.207, bf16[4,4,2240,128]{3,2,1,0:T(8,128)(2,1)} %get-tuple-element.137, s32[]{:T(128)S(6)} %select_n.209, s32[]{:T(128)S(6)} %select_n.208), kind=kLoop, calls=%fused_computation.36 | loop fusion | flops 13762560 | bytes 20643852 | tf_op jit(solution)/shard_map/convert_element_type | solution.py:782
  671.0 5.8 fusion.61
  678.3 10.3 %collective-permute-done.55 = bf16[4,2240,128]{2,1,0:T(8,128)(2,1)} collective-permute-done((bf16[4,2240,128]{2,1,0:T(8,128)(2,1)}, bf16[4,2240,128]{2,1,0:T(8,128)(2,1)}, u32[]{:S(2)}, u32[]{:S(2)}) %collective-permute-start.55) | collective-permute-done | bytes 2293792 | tf_op jit(solution)/shard_map/ppermute | solution.py:748
  689.3 24.2 %collective-permute-done.57 = bf16[4,2240,128]{2,1,0:T(8,128)(2,1)} collective-permute-done((bf16[4,2240,128]{2,1,0:T(8,128)(2,1)}, bf16[4,2240,128]{2,1,0:T(8,128)(2,1)}, u32[]{:S(2)}, u32[]{:S(2)}) %collective-permute-start.57) | collective-permute-done | bytes 2293792 | tf_op jit(solution)/shard_map/ppermute | solution.py:748
  713.5 5.8 fusion.63
  734.1 5.3 collective-permute-done.60
  739.4 12.3 %collective-permute-done.59 = bf16[2240,128]{1,0:T(8,128)(2,1)S(1)} collective-permute-done((bf16[2240,128]{1,0:T(8,128)(2,1)S(1)}, bf16[2240,128]{1,0:T(8,128)(2,1)S(1)}, u32[]{:S(2)}, u32[]{:S(2)}) %collective-permute-start.59) | collective-permute-done | bytes 573472 | tf_op jit(solution)/shard_map/ppermute | solution.py:748
  752.0 20.5 %collective-permute-start.63 = (bf16[2240,128]{1,0:T(8,128)(2,1)S(1)}, bf16[2240,128]{1,0:T(8,128)(2,1)S(1)}, u32[]{:S(2)}, u32[]{:S(2)}) collective-permute-start(bf16[2240,128]{1,0:T(8,128)(2,1)S(1)} %fusion.28), channel_id=1, source_target_pairs={{0,3},{1,0},{2,1},{3,2},{4,7},{5,4},{6,5},{7,6},{8,11},{9,8},{10,9... | collective-permute-start | bytes 1720328 | tf_op jit(solution)/shard_map/ppermute | solution.py:748
  779.8 10.5 %collective-permute-done.62 = bf16[2240,128]{1,0:T(8,128)(2,1)S(1)} collective-permute-done((bf16[2240,128]{1,0:T(8,128)(2,1)S(1)}, bf16[2240,128]{1,0:T(8,128)(2,1)S(1)}, u32[]{:S(2)}, u32[]{:S(2)}) %collective-permute-start.62) | collective-permute-done | bytes 573472 | tf_op jit(solution)/shard_map/ppermute | solution.py:748
  (325 shorter events, 214.2 us)
Async XLA Ops:
  22.0 20.4 %collective-permute-start.10 = (bf16[2240,128]{1,0:T(8,128)(2,1)S(1)}, bf16[2240,128]{1,0:T(8,128)(2,1)S(1)}, u32[]{:S(2)}, u32[]{:S(2)}) collective-permute-start(bf16[2240,128]{1,0:T(8,128)(2,1)S(1)} %get-tuple-element.252), channel_id=1, source_target_pairs={{0,12},{1,13},{2,14},{3,15},{4,0},{5,1},{6,2},{7,3},{8,4},{9,5},{1... | collective-permute-start | bytes 1720328 | tf_op jit(solution)/shard_map/ppermute | solution.py:748
  29.0 46.9 %collective-permute-start.9 = (bf16[2240,128]{1,0:T(8,128)(2,1)S(1)}, bf16[2240,128]{1,0:T(8,128)(2,1)S(1)}, u32[]{:S(2)}, u32[]{:S(2)}) collective-permute-start(bf16[2240,128]{1,0:T(8,128)(2,1)S(1)} %get-tuple-element.252), channel_id=1, source_target_pairs={{0,8},{1,9},{2,10},{3,11},{4,12},{5,13},{6,14},{7,15},{8,0},{9,1},... | collective-permute-start | bytes 1720328 | tf_op jit(solution)/shard_map/ppermute | solution.py:748
  30.9 44.9 %collective-permute-start.8 = (bf16[2240,128]{1,0:T(8,128)(2,1)S(1)}, bf16[2240,128]{1,0:T(8,128)(2,1)S(1)}, u32[]{:S(2)}, u32[]{:S(2)}) collective-permute-start(bf16[2240,128]{1,0:T(8,128)(2,1)S(1)} %get-tuple-element.252), channel_id=1, source_target_pairs={{0,4},{1,5},{2,6},{3,7},{4,8},{5,9},{6,10},{7,11},{8,12},{9,13},{1... | collective-permute-start | bytes 1720328 | tf_op jit(solution)/shard_map/ppermute | solution.py:748
  34.0 50.3 %collective-permute-start.28 = (bf16[3,2240,128]{2,1,0:T(8,128)(2,1)S(1)}, bf16[3,2240,128]{2,1,0:T(8,128)(2,1)S(1)}, u32[]{:S(2)}, u32[]{:S(2)}) collective-permute-start(bf16[3,2240,128]{2,1,0:T(8,128)(2,1)S(1)} %pad_maximum_fusion.16), channel_id=1, source_target_pairs={{16,19},{17,16},{18,17},{19,18},{20,23},{21,20},{22,21},{23,22},{2... | collective-permute-start | bytes 5160968 | tf_op jit(solution)/shard_map/ppermute | solution.py:748
  76.0 42.4 %collective-permute-start.13 = (bf16[3,2240,128]{2,1,0:T(8,128)(2,1)S(1)}, bf16[3,2240,128]{2,1,0:T(8,128)(2,1)S(1)}, u32[]{:S(2)}, u32[]{:S(2)}) collective-permute-start(bf16[3,2240,128]{2,1,0:T(8,128)(2,1)S(1)} %pad_maximum_fusion.15), channel_id=1, source_target_pairs={{0,3},{1,0},{2,1},{3,2},{4,7},{5,4},{6,5},{7,6},{8,11},{9,8},{10,9... | collective-permute-start | bytes 5160968 | tf_op jit(solution)/shard_map/ppermute | solution.py:748
  80.4 38.4 %collective-permute-start.27 = (bf16[3,2240,128]{2,1,0:T(8,128)(2,1)S(1)}, bf16[3,2240,128]{2,1,0:T(8,128)(2,1)S(1)}, u32[]{:S(2)}, u32[]{:S(2)}) collective-permute-start(bf16[3,2240,128]{2,1,0:T(8,128)(2,1)S(1)} %pad_maximum_fusion.16), channel_id=1, source_target_pairs={{16,18},{17,19},{18,16},{19,17},{20,22},{21,23},{22,20},{23,21},{2... | collective-permute-start | bytes 5160968 | tf_op jit(solution)/shard_map/ppermute | solution.py:748
  81.2 75.0 %collective-permute-start.12 = (bf16[3,2240,128]{2,1,0:T(8,128)(2,1)S(1)}, bf16[3,2240,128]{2,1,0:T(8,128)(2,1)S(1)}, u32[]{:S(2)}, u32[]{:S(2)}) collective-permute-start(bf16[3,2240,128]{2,1,0:T(8,128)(2,1)S(1)} %pad_maximum_fusion.15), channel_id=1, source_target_pairs={{0,2},{1,3},{2,0},{3,1},{4,6},{5,7},{6,4},{7,5},{8,10},{9,11},{10,... | collective-permute-start | bytes 5160968 | tf_op jit(solution)/shard_map/ppermute | solution.py:748
  83.6 73.0 %collective-permute-start.26 = (bf16[3,2240,128]{2,1,0:T(8,128)(2,1)S(1)}, bf16[3,2240,128]{2,1,0:T(8,128)(2,1)S(1)}, u32[]{:S(2)}, u32[]{:S(2)}) collective-permute-start(bf16[3,2240,128]{2,1,0:T(8,128)(2,1)S(1)} %pad_maximum_fusion.16), channel_id=1, source_target_pairs={{16,17},{17,18},{18,19},{19,16},{20,21},{21,22},{22,23},{23,20},{2... | collective-permute-start | bytes 5160968 | tf_op jit(solution)/shard_map/ppermute | solution.py:748
  84.3 72.2 %collective-permute-start.11 = (bf16[3,2240,128]{2,1,0:T(8,128)(2,1)S(1)}, bf16[3,2240,128]{2,1,0:T(8,128)(2,1)S(1)}, u32[]{:S(2)}, u32[]{:S(2)}) collective-permute-start(bf16[3,2240,128]{2,1,0:T(8,128)(2,1)S(1)} %pad_maximum_fusion.15), channel_id=1, source_target_pairs={{0,1},{1,2},{2,3},{3,0},{4,5},{5,6},{6,7},{7,4},{8,9},{9,10},{10,1... | collective-permute-start | bytes 5160968 | tf_op jit(solution)/shard_map/ppermute | solution.py:748
  161.4 114.4 %collective-permute-start.14 = (bf16[4,4,2240,128]{3,2,1,0:T(8,128)(2,1)}, bf16[4,4,2240,128]{3,2,1,0:T(8,128)(2,1)}, u32[]{:S(2)}, u32[]{:S(2)}) collective-permute-start(bf16[4,4,2240,128]{3,2,1,0:T(8,128)(2,1)} %pad_maximum_fusion.own_ref), channel_id=1, source_target_pairs={{0,16},{1,17},{2,18},{3,19},{4,20},{5,21},{6,22},{7,23},{8,24},{9,... | collective-permute-start | bytes 27525128 | tf_op jit(solution)/shard_map/ppermute | solution.py:752
  170.9 136.5 %collective-permute-start.29 = (bf16[4,4,2240,128]{3,2,1,0:T(8,128)(2,1)}, bf16[4,4,2240,128]{3,2,1,0:T(8,128)(2,1)}, u32[]{:S(2)}, u32[]{:S(2)}) collective-permute-start(bf16[4,4,2240,128]{3,2,1,0:T(8,128)(2,1)} %pad_maximum_fusion.1.own_ref), channel_id=1, source_target_pairs={{16,0},{17,1},{18,2},{19,3},{20,4},{21,5},{22,6},{23,7},{24,8},{25... | collective-permute-start | bytes 27525128 | tf_op jit(solution)/shard_map/ppermute | solution.py:752
  175.5 14.8 %collective-permute-start.2 = (bf16[496,128]{1,0:T(8,128)(2,1)S(1)}, bf16[496,128]{1,0:T(8,128)(2,1)S(1)}, u32[]{:S(2)}, u32[]{:S(2)}) collective-permute-start(bf16[496,128]{1,0:T(8,128)(2,1)S(1)} %get-tuple-element.271), channel_id=1, source_target_pairs={{0,12},{1,13},{2,14},{3,15},{4,0},{5,1},{6,2},{7,3},{8,4},{9,5},{1... | collective-permute-start | bytes 380936 | tf_op jit(solution)/shard_map/ppermute | solution.py:748
  177.4 15.6 %collective-permute-start.1 = (bf16[496,128]{1,0:T(8,128)(2,1)S(1)}, bf16[496,128]{1,0:T(8,128)(2,1)S(1)}, u32[]{:S(2)}, u32[]{:S(2)}) collective-permute-start(bf16[496,128]{1,0:T(8,128)(2,1)S(1)} %get-tuple-element.271), channel_id=1, source_target_pairs={{0,8},{1,9},{2,10},{3,11},{4,12},{5,13},{6,14},{7,15},{8,0},{9,1},... | collective-permute-start | bytes 380936 | tf_op jit(solution)/shard_map/ppermute | solution.py:748
  218.9 19.6 %collective-permute-start.6 = (bf16[4,4,496,128]{3,2,1,0:T(8,128)(2,1)}, bf16[4,4,496,128]{3,2,1,0:T(8,128)(2,1)}, u32[]{:S(2)}, u32[]{:S(2)}) collective-permute-start(bf16[4,4,496,128]{3,2,1,0:T(8,128)(2,1)} %pad_maximum_fusion.13.own_ref), channel_id=1, source_target_pairs={{0,16},{1,17},{2,18},{3,19},{4,20},{5,21},{6,22},{7,23},{8,24},{9,... | collective-permute-start | bytes 6094856 | tf_op jit(solution)/shard_map/ppermute | solution.py:752
  231.9 13.4 %collective-permute-start.21 = (bf16[4,4,496,128]{3,2,1,0:T(8,128)(2,1)S(1)}, bf16[4,4,496,128]{3,2,1,0:T(8,128)(2,1)}, u32[]{:S(2)}, u32[]{:S(2)}) collective-permute-start(bf16[4,4,496,128]{3,2,1,0:T(8,128)(2,1)S(1)} %pad_maximum_fusion.14.own_ref), channel_id=1, source_target_pairs={{16,0},{17,1},{18,2},{19,3},{20,4},{21,5},{22,6},{23,7},{24,8},{25... | collective-permute-start | bytes 6094856 | tf_op jit(solution)/shard_map/ppermute | solution.py:752
  254.8 13.7 %collective-permute-start.7 = (bf16[512,512]{1,0:T(8,128)(2,1)}, bf16[512,512]{1,0:T(8,128)(2,1)S(1)}, u32[]{:S(2)}, u32[]{:S(2)}) collective-permute-start(bf16[512,512]{1,0:T(8,128)(2,1)} %get-tuple-element.81.near_ref), channel_id=1, source_target_pairs={{0,1},{1,2},{2,3},{4,5},{5,6},{6,7},{8,9},{9,10},{10,11},{12,13},{... | collective-permute-start | bytes 1572872 | tf_op jit(solution)/shard_map/ppermute | solution.py:758
  302.0 19.5 %collective-permute-start.22 = (bf16[512,512]{1,0:T(8,128)(2,1)}, bf16[512,512]{1,0:T(8,128)(2,1)S(1)}, u32[]{:S(2)}, u32[]{:S(2)}) collective-permute-start(bf16[512,512]{1,0:T(8,128)(2,1)} %get-tuple-element.91.near_ref), channel_id=1, source_target_pairs={{0,1},{1,2},{2,3},{4,5},{5,6},{6,7},{8,9},{9,10},{10,11},{12,13},{... | collective-permute-start | bytes 1572872 | tf_op jit(solution)/shard_map/ppermute | solution.py:758
  367.0 130.5 %collective-permute-start.64 = (bf16[4,4,2240,128]{3,2,1,0:T(8,128)(2,1)}, bf16[4,4,2240,128]{3,2,1,0:T(8,128)(2,1)}, u32[]{:S(2)}, u32[]{:S(2)}) collective-permute-start(bf16[4,4,2240,128]{3,2,1,0:T(8,128)(2,1)} %get-tuple-element.138), channel_id=1, source_target_pairs={{0,16},{1,17},{2,18},{3,19},{4,20},{5,21},{6,22},{7,23},{8,24},{9,... | collective-permute-start | bytes 27525128 | tf_op jit(solution)/shard_map/ppermute | solution.py:752
  433.3 212.1 %collective-permute-start.54 = (bf16[4,4,2240,128]{3,2,1,0:T(8,128)(2,1)}, bf16[4,4,2240,128]{3,2,1,0:T(8,128)(2,1)}, u32[]{:S(2)}, u32[]{:S(2)}) collective-permute-start(bf16[4,4,2240,128]{3,2,1,0:T(8,128)(2,1)} %get-tuple-element.137), channel_id=1, source_target_pairs={{16,0},{17,1},{18,2},{19,3},{20,4},{21,5},{22,6},{23,7},{24,8},{25... | collective-permute-start | bytes 27525128 | tf_op jit(solution)/shard_map/ppermute | solution.py:752
  434.6 48.9 %collective-permute-start.44 = (bf16[4,4,480,128]{3,2,1,0:T(8,128)(2,1)}, bf16[4,4,480,128]{3,2,1,0:T(8,128)(2,1)}, u32[]{:S(2)}, u32[]{:S(2)}) collective-permute-start(bf16[4,4,480,128]{3,2,1,0:T(8,128)(2,1)} %get-tuple-element.136), channel_id=1, source_target_pairs={{0,16},{1,17},{2,18},{3,19},{4,20},{5,21},{6,22},{7,23},{8,24},{9,... | collective-permute-start | bytes 5898248 | tf_op jit(solution)/shard_map/ppermute | solution.py:752
  442.8 44.6 %collective-permute-start.30 = (bf16[512,640]{1,0:T(8,128)(2,1)S(1)}, bf16[512,640]{1,0:T(8,128)(2,1)S(1)}, u32[]{:S(2)}, u32[]{:S(2)}) collective-permute-start(bf16[512,640]{1,0:T(8,128)(2,1)S(1)} %broadcast_select_fusion.2), channel_id=1, source_target_pairs={{0,16},{16,0},{1,17},{17,1},{2,18},{18,2},{3,19},{19,3},{4,20},{20... | collective-permute-start | bytes 1966088 | tf_op jit(solution)/shard_map/ppermute | solution.py:920
  457.5 17.3 %collective-permute-start.32 = (bf16[512,512]{1,0:T(8,128)(2,1)}, bf16[512,512]{1,0:T(8,128)(2,1)S(1)}, u32[]{:S(2)}, u32[]{:S(2)}) collective-permute-start(bf16[512,512]{1,0:T(8,128)(2,1)} %get-tuple-element.123), channel_id=1, source_target_pairs={{1,0},{2,1},{3,2},{5,4},{6,5},{7,6},{9,8},{10,9},{11,10},{13,12},{... | collective-permute-start | bytes 1572872 | tf_op jit(solution)/shard_map/ppermute | solution.py:758
  492.7 18.3 %collective-permute-start.48 = (bf16[480,128]{1,0:T(8,128)(2,1)S(1)}, bf16[480,128]{1,0:T(8,128)(2,1)S(1)}, u32[]{:S(2)}, u32[]{:S(2)}) collective-permute-start(bf16[480,128]{1,0:T(8,128)(2,1)S(1)} %get-tuple-element.279), channel_id=1, source_target_pairs={{16,20},{17,21},{18,22},{19,23},{20,24},{21,25},{22,26},{23,27},{2... | collective-permute-start | bytes 368648 | tf_op jit(solution)/shard_map/ppermute | solution.py:748
  493.4 19.8 %collective-permute-start.50 = (bf16[480,128]{1,0:T(8,128)(2,1)S(1)}, bf16[480,128]{1,0:T(8,128)(2,1)S(1)}, u32[]{:S(2)}, u32[]{:S(2)}) collective-permute-start(bf16[480,128]{1,0:T(8,128)(2,1)S(1)} %get-tuple-element.280), channel_id=1, source_target_pairs={{16,28},{17,29},{18,30},{19,31},{20,16},{21,17},{22,18},{23,19},{2... | collective-permute-start | bytes 368648 | tf_op jit(solution)/shard_map/ppermute | solution.py:748
  494.1 22.3 %collective-permute-start.49 = (bf16[480,128]{1,0:T(8,128)(2,1)S(1)}, bf16[480,128]{1,0:T(8,128)(2,1)S(1)}, u32[]{:S(2)}, u32[]{:S(2)}) collective-permute-start(bf16[480,128]{1,0:T(8,128)(2,1)S(1)} %get-tuple-element.281), channel_id=1, source_target_pairs={{16,24},{17,25},{18,26},{19,27},{20,28},{21,29},{22,30},{23,31},{2... | collective-permute-start | bytes 368648 | tf_op jit(solution)/shard_map/ppermute | solution.py:748
  497.5 108.1 %collective-permute-start.35 = (bf16[4,480,128]{2,1,0:T(8,128)(2,1)}, bf16[4,480,128]{2,1,0:T(8,128)(2,1)}, u32[]{:S(2)}, u32[]{:S(2)}) collective-permute-start(bf16[4,480,128]{2,1,0:T(8,128)(2,1)} %get-tuple-element.231), channel_id=1, source_target_pairs={{0,1},{1,2},{2,3},{3,0},{4,5},{5,6},{6,7},{7,4},{8,9},{9,10},{10,1... | collective-permute-start | bytes 1474568 | tf_op jit(solution)/shard_map/ppermute | solution.py:748
  511.0 94.7 %collective-permute-start.37 = (bf16[4,480,128]{2,1,0:T(8,128)(2,1)}, bf16[4,480,128]{2,1,0:T(8,128)(2,1)}, u32[]{:S(2)}, u32[]{:S(2)}) collective-permute-start(bf16[4,480,128]{2,1,0:T(8,128)(2,1)} %get-tuple-element.232), channel_id=1, source_target_pairs={{0,3},{1,0},{2,1},{3,2},{4,7},{5,4},{6,5},{7,6},{8,11},{9,8},{10,9... | collective-permute-start | bytes 1474568 | tf_op jit(solution)/shard_map/ppermute | solution.py:748
  513.2 93.2 %collective-permute-start.36 = (bf16[4,480,128]{2,1,0:T(8,128)(2,1)}, bf16[4,480,128]{2,1,0:T(8,128)(2,1)}, u32[]{:S(2)}, u32[]{:S(2)}) collective-permute-start(bf16[4,480,128]{2,1,0:T(8,128)(2,1)} %get-tuple-element.233), channel_id=1, source_target_pairs={{0,2},{1,3},{2,0},{3,1},{4,6},{5,7},{6,4},{7,5},{8,10},{9,11},{10,... | collective-permute-start | bytes 1474568 | tf_op jit(solution)/shard_map/ppermute | solution.py:748
  516.3 147.7 %collective-permute-start.65 = (bf16[4,2240,128]{2,1,0:T(8,128)(2,1)}, bf16[4,2240,128]{2,1,0:T(8,128)(2,1)}, u32[]{:S(2)}, u32[]{:S(2)}) collective-permute-start(bf16[4,2240,128]{2,1,0:T(8,128)(2,1)} %get-tuple-element.222), channel_id=1, source_target_pairs={{16,17},{17,18},{18,19},{19,16},{20,21},{21,22},{22,23},{23,20},{2... | collective-permute-start | bytes 6881288 | tf_op jit(solution)/shard_map/ppermute | solution.py:748
  612.0 59.0 %collective-permute-start.67 = (bf16[4,2240,128]{2,1,0:T(8,128)(2,1)}, bf16[4,2240,128]{2,1,0:T(8,128)(2,1)}, u32[]{:S(2)}, u32[]{:S(2)}) collective-permute-start(bf16[4,2240,128]{2,1,0:T(8,128)(2,1)} %get-tuple-element.223), channel_id=1, source_target_pairs={{16,19},{17,16},{18,17},{19,18},{20,23},{21,20},{22,21},{23,22},{2... | collective-permute-start | bytes 6881288 | tf_op jit(solution)/shard_map/ppermute | solution.py:748
  614.1 56.9 %collective-permute-start.66 = (bf16[4,2240,128]{2,1,0:T(8,128)(2,1)}, bf16[4,2240,128]{2,1,0:T(8,128)(2,1)}, u32[]{:S(2)}, u32[]{:S(2)}) collective-permute-start(bf16[4,2240,128]{2,1,0:T(8,128)(2,1)} %get-tuple-element.224), channel_id=1, source_target_pairs={{16,18},{17,19},{18,16},{19,17},{20,22},{21,23},{22,20},{23,21},{2... | collective-permute-start | bytes 6881288 | tf_op jit(solution)/shard_map/ppermute | solution.py:748
  641.4 15.9 %collective-permute-start.42 = (bf16[480,128]{1,0:T(8,128)(2,1)S(1)}, bf16[480,128]{1,0:T(8,128)(2,1)S(1)}, u32[]{:S(2)}, u32[]{:S(2)}) collective-permute-start(bf16[480,128]{1,0:T(8,128)(2,1)S(1)} %fusion.57), channel_id=1, source_target_pairs={{0,2},{1,3},{2,0},{3,1},{4,6},{5,7},{6,4},{7,5},{8,10},{9,11},{10,... | collective-permute-start | bytes 368648 | tf_op jit(solution)/shard_map/ppermute | solution.py:748
  645.4 14.2 %collective-permute-start.41 = (bf16[480,128]{1,0:T(8,128)(2,1)S(1)}, bf16[480,128]{1,0:T(8,128)(2,1)S(1)}, u32[]{:S(2)}, u32[]{:S(2)}) collective-permute-start(bf16[480,128]{1,0:T(8,128)(2,1)S(1)} %fusion.57), channel_id=1, source_target_pairs={{0,1},{1,2},{2,3},{3,0},{4,5},{5,6},{6,7},{7,4},{8,9},{9,10},{10,1... | collective-permute-start | bytes 368648 | tf_op jit(solution)/shard_map/ppermute | solution.py:748
  657.3 31.3 %collective-permute-start.55 = (bf16[4,2240,128]{2,1,0:T(8,128)(2,1)}, bf16[4,2240,128]{2,1,0:T(8,128)(2,1)}, u32[]{:S(2)}, u32[]{:S(2)}) collective-permute-start(bf16[4,2240,128]{2,1,0:T(8,128)(2,1)} %get-tuple-element.225), channel_id=1, source_target_pairs={{0,1},{1,2},{2,3},{3,0},{4,5},{5,6},{6,7},{7,4},{8,9},{9,10},{10,1... | collective-permute-start | bytes 6881288 | tf_op jit(solution)/shard_map/ppermute | solution.py:748
  659.6 53.9 %collective-permute-start.57 = (bf16[4,2240,128]{2,1,0:T(8,128)(2,1)}, bf16[4,2240,128]{2,1,0:T(8,128)(2,1)}, u32[]{:S(2)}, u32[]{:S(2)}) collective-permute-start(bf16[4,2240,128]{2,1,0:T(8,128)(2,1)} %get-tuple-element.226), channel_id=1, source_target_pairs={{0,3},{1,0},{2,1},{3,2},{4,7},{5,4},{6,5},{7,6},{8,11},{9,8},{10,9... | collective-permute-start | bytes 6881288 | tf_op jit(solution)/shard_map/ppermute | solution.py:748
  664.1 49.4 %collective-permute-start.56 = (bf16[4,2240,128]{2,1,0:T(8,128)(2,1)}, bf16[4,2240,128]{2,1,0:T(8,128)(2,1)}, u32[]{:S(2)}, u32[]{:S(2)}) collective-permute-start(bf16[4,2240,128]{2,1,0:T(8,128)(2,1)} %get-tuple-element.227), channel_id=1, source_target_pairs={{0,2},{1,3},{2,0},{3,1},{4,6},{5,7},{6,4},{7,5},{8,10},{9,11},{10,... | collective-permute-start | bytes 6881288 | tf_op jit(solution)/shard_map/ppermute | solution.py:748
  676.9 50.6 %collective-permute-start.68 = (bf16[2240,128]{1,0:T(8,128)(2,1)S(1)}, bf16[2240,128]{1,0:T(8,128)(2,1)S(1)}, u32[]{:S(2)}, u32[]{:S(2)}) collective-permute-start(bf16[2240,128]{1,0:T(8,128)(2,1)S(1)} %get-tuple-element.241), channel_id=1, source_target_pairs={{16,20},{17,21},{18,22},{19,23},{20,24},{21,25},{22,26},{23,27},{2... | collective-permute-start | bytes 1720328 | tf_op jit(solution)/shard_map/ppermute | solution.py:748
  677.6 52.4 %collective-permute-start.70 = (bf16[2240,128]{1,0:T(8,128)(2,1)S(1)}, bf16[2240,128]{1,0:T(8,128)(2,1)S(1)}, u32[]{:S(2)}, u32[]{:S(2)}) collective-permute-start(bf16[2240,128]{1,0:T(8,128)(2,1)S(1)} %get-tuple-element.242), channel_id=1, source_target_pairs={{16,28},{17,29},{18,30},{19,31},{20,16},{21,17},{22,18},{23,19},{2... | collective-permute-start | bytes 1720328 | tf_op jit(solution)/shard_map/ppermute | solution.py:748
  688.6 41.4 %collective-permute-start.69 = (bf16[2240,128]{1,0:T(8,128)(2,1)S(1)}, bf16[2240,128]{1,0:T(8,128)(2,1)S(1)}, u32[]{:S(2)}, u32[]{:S(2)}) collective-permute-start(bf16[2240,128]{1,0:T(8,128)(2,1)S(1)} %get-tuple-element.243), channel_id=1, source_target_pairs={{16,24},{17,25},{18,26},{19,27},{20,28},{21,29},{22,30},{23,31},{2... | collective-permute-start | bytes 1720328 | tf_op jit(solution)/shard_map/ppermute | solution.py:748
  719.4 14.0 %collective-permute-start.58 = (bf16[2240,128]{1,0:T(8,128)(2,1)S(1)}, bf16[2240,128]{1,0:T(8,128)(2,1)S(1)}, u32[]{:S(2)}, u32[]{:S(2)}) collective-permute-start(bf16[2240,128]{1,0:T(8,128)(2,1)S(1)} %get-tuple-element.248), channel_id=1, source_target_pairs={{0,4},{1,5},{2,6},{3,7},{4,8},{5,9},{6,10},{7,11},{8,12},{9,13},{1... | collective-permute-start | bytes 1720328 | tf_op jit(solution)/shard_map/ppermute | solution.py:748
  723.2 16.2 %collective-permute-start.60 = (bf16[2240,128]{1,0:T(8,128)(2,1)S(1)}, bf16[2240,128]{1,0:T(8,128)(2,1)S(1)}, u32[]{:S(2)}, u32[]{:S(2)}) collective-permute-start(bf16[2240,128]{1,0:T(8,128)(2,1)S(1)} %get-tuple-element.249), channel_id=1, source_target_pairs={{0,12},{1,13},{2,14},{3,15},{4,0},{5,1},{6,2},{7,3},{8,4},{9,5},{1... | collective-permute-start | bytes 1720328 | tf_op jit(solution)/shard_map/ppermute | solution.py:748
  727.5 24.2 %collective-permute-start.59 = (bf16[2240,128]{1,0:T(8,128)(2,1)S(1)}, bf16[2240,128]{1,0:T(8,128)(2,1)S(1)}, u32[]{:S(2)}, u32[]{:S(2)}) collective-permute-start(bf16[2240,128]{1,0:T(8,128)(2,1)S(1)} %get-tuple-element.250), channel_id=1, source_target_pairs={{0,8},{1,9},{2,10},{3,11},{4,12},{5,13},{6,14},{7,15},{8,0},{9,1},... | collective-permute-start | bytes 1720328 | tf_op jit(solution)/shard_map/ppermute | solution.py:748
  730.3 45.4 %collective-permute-start.73 = (bf16[2240,128]{1,0:T(8,128)(2,1)S(1)}, bf16[2240,128]{1,0:T(8,128)(2,1)S(1)}, u32[]{:S(2)}, u32[]{:S(2)}) collective-permute-start(bf16[2240,128]{1,0:T(8,128)(2,1)S(1)} %fusion.25), channel_id=1, source_target_pairs={{16,19},{17,16},{18,17},{19,18},{20,23},{21,20},{22,21},{23,22},{2... | collective-permute-start | bytes 1720328 | tf_op jit(solution)/shard_map/ppermute | solution.py:748
  731.0 46.6 %collective-permute-start.72 = (bf16[2240,128]{1,0:T(8,128)(2,1)S(1)}, bf16[2240,128]{1,0:T(8,128)(2,1)S(1)}, u32[]{:S(2)}, u32[]{:S(2)}) collective-permute-start(bf16[2240,128]{1,0:T(8,128)(2,1)S(1)} %fusion.25), channel_id=1, source_target_pairs={{16,18},{17,19},{18,16},{19,17},{20,22},{21,23},{22,20},{23,21},{2... | collective-permute-start | bytes 1720328 | tf_op jit(solution)/shard_map/ppermute | solution.py:748
  733.4 44.2 %collective-permute-start.71 = (bf16[2240,128]{1,0:T(8,128)(2,1)S(1)}, bf16[2240,128]{1,0:T(8,128)(2,1)S(1)}, u32[]{:S(2)}, u32[]{:S(2)}) collective-permute-start(bf16[2240,128]{1,0:T(8,128)(2,1)S(1)} %fusion.25), channel_id=1, source_target_pairs={{16,17},{17,18},{18,19},{19,16},{20,21},{21,22},{22,23},{23,20},{2... | collective-permute-start | bytes 1720328 | tf_op jit(solution)/shard_map/ppermute | solution.py:748
  752.0 27.8 %collective-permute-start.63 = (bf16[2240,128]{1,0:T(8,128)(2,1)S(1)}, bf16[2240,128]{1,0:T(8,128)(2,1)S(1)}, u32[]{:S(2)}, u32[]{:S(2)}) collective-permute-start(bf16[2240,128]{1,0:T(8,128)(2,1)S(1)} %fusion.28), channel_id=1, source_target_pairs={{0,3},{1,0},{2,1},{3,2},{4,7},{5,4},{6,5},{7,6},{8,11},{9,8},{10,9... | collective-permute-start | bytes 1720328 | tf_op jit(solution)/shard_map/ppermute | solution.py:748
  772.5 17.7 %collective-permute-start.62 = (bf16[2240,128]{1,0:T(8,128)(2,1)S(1)}, bf16[2240,128]{1,0:T(8,128)(2,1)S(1)}, u32[]{:S(2)}, u32[]{:S(2)}) collective-permute-start(bf16[2240,128]{1,0:T(8,128)(2,1)S(1)} %fusion.28), channel_id=1, source_target_pairs={{0,2},{1,3},{2,0},{3,1},{4,6},{5,7},{6,4},{7,5},{8,10},{9,11},{10,... | collective-permute-start | bytes 1720328 | tf_op jit(solution)/shard_map/ppermute | solution.py:748
  775.7 14.6 %collective-permute-start.61 = (bf16[2240,128]{1,0:T(8,128)(2,1)S(1)}, bf16[2240,128]{1,0:T(8,128)(2,1)S(1)}, u32[]{:S(2)}, u32[]{:S(2)}) collective-permute-start(bf16[2240,128]{1,0:T(8,128)(2,1)S(1)} %fusion.28), channel_id=1, source_target_pairs={{0,1},{1,2},{2,3},{3,0},{4,5},{5,6},{6,7},{7,4},{8,9},{9,10},{10,1... | collective-permute-start | bytes 1720328 | tf_op jit(solution)/shard_map/ppermute | solution.py:748
  (54 other events, 682.4 us)

commit v2 on v1

--- a/solution.py
+++ b/solution.py
@@ -12,7 +12,7 @@
 EPS = 1e-06
 LANES = 128
 PARTS = 4
-GAIN_ROWS = 16
+GAIN_ROWS = 32
 QB = 128
 F32 = jnp.float32
 B16 = jnp.bfloat16
@@ -92,12 +92,19 @@
 
 
 def cost(flops, nbytes):
-    return pl.CostEstimate(flops=int(flops), bytes_accessed=int(nbytes), transcendentals=0)
+    return pl.CostEstimate(flops=int(flops) * 30, bytes_accessed=int(nbytes), transcendentals=0)
 
 
 def whole(shape):
     n = len(shape)
     return pl.BlockSpec(shape, lambda *i: (0,) * n)
+
+
+def held_back(kernel, first, n):
+    def body(*refs):
+        kernel(*refs[:first], *refs[first + n :])
+
+    return body
 
 
 def sds(shape, dtype):
@@ -116,9 +123,9 @@
     kv_ref[:, HD:] = both[:, HD:].astype(B16)
 
 
-def kv_call(x, gd, gh, cos, sin, w_qkv):
+def kv_call(layer, x, gd, gh, cos, sin, w_qkv):
     tok, width = x.shape
-    q_width = w_qkv.shape[1] - 2 * HD
+    q_width = w_qkv.shape[2] - 2 * HD
     return pl.pallas_call(
         kv_kernel,
         grid=(1,),
@@ -128,7 +135,7 @@
             whole(gh.shape),
             whole(cos.shape),
             whole(sin.shape),
-            pl.BlockSpec((width, 2 * HD), lambda j: (0, q_width // (2 * HD))),
+            pl.BlockSpec((None, width, 2 * HD), lambda j: (layer, 0, q_width // (2 * HD))),
         ],
         out_specs=[whole((tok, width)), whole((tok, HD)), whole((tok, 2 * HD))],
         out_shape=[sds((tok, width), B16), sds((tok, HD), B16), sds((tok, 2 * HD), B16)],
@@ -144,9 +151,9 @@
     q_ref[...] = rope(pre * inv_rms(pre) * gh_ref[0:1, :], cos_ref[...], sin_ref[...]).astype(B16)
 
 
-def q_call(a, gh, cos, sin, w_qkv):
+def q_call(layer, a, gh, cos, sin, w_qkv):
     tok, width = a.shape
-    q_width = w_qkv.shape[1] - 2 * HD
+    q_width = w_qkv.shape[2] - 2 * HD
     block = pl.BlockSpec((tok, HD), lambda j: (0, j))
     return pl.pallas_call(
         q_kernel,
@@ -156,7 +163,7 @@
             whole(gh.shape),
             whole(cos.shape),
             whole(sin.shape),
-            pl.BlockSpec((width, HD), lambda j: (0, j)),
+            pl.BlockSpec((None, width, HD), lambda j: (layer, 0, j)),
         ],
         out_specs=[block, block],
         out_shape=[sds((tok, q_width), B16), sds((tok, q_width), B16)],
@@ -284,10 +291,21 @@
 
 
 def ffn_back_kernel(
-    c_ref, z_ref, h_ref, y_ref, o_ref, gd_ref, g_ref, u_ref, wo_ref, wg_ref, wu_ref, wd_ref,
-    pack_ref, dh_ref, do_ref, gg_ref, dz_scr, bt_scr, db_scr,
+    spot, c_ref, z_ref, h_ref, y_ref, o_ref, gd_ref, g_ref, u_ref, wo_ref, wg_ref, wu_ref, wd_ref,
+    keep_ref, send_ref, dh_ref, do_ref, gg_ref, dz_scr, bt_scr, db_scr,
 ):
     j = pl.program_id(0)
+    half = keep_ref.shape[2]
+
+    def put(blocks):
+        for section in range(2):
+
+            @pl.when(spot[2] == section)
+            def _():
+                for c_part, p, row, block in blocks:
+                    ref = keep_ref if row // half == section else send_ref
+                    ref[c_part, p, pl.ds(row % half, block.shape[0]), :] = block
+
     tok, width = c_ref.shape
     part = width // PARTS
     n_gate = PARTS * part
@@ -313,20 +331,20 @@
     dg = (df * u * slope).astype(B16)
     db_scr[...] += dot_nt(dg, wg_ref[...]) + dot_nt(du, wu_ref[...])
     bt = bt_scr[...]
+    blocks = []
     for first, term in ((0, dg), (n_gate, du)):
         grad = dot(bt, term).astype(B16)
         for p in range(PARTS):
             for t in range(FC // LANES):
-                pack_ref[j, p, pl.ds(first + t * part, part), :] = grad[
-                    p * part : (p + 1) * part, t * LANES : (t + 1) * LANES
-                ]
+                block = grad[p * part : (p + 1) * part, t * LANES : (t + 1) * LANES]
+                blocks.append((j, p, first + t * part, block))
     grad = dot_tn(f, dz).astype(B16)
     rows = FC // PARTS
     for p in range(PARTS):
         for t in range(width // LANES):
-            pack_ref[p, j, pl.ds(2 * n_gate + t * rows, rows), :] = grad[
-                p * rows : (p + 1) * rows, t * LANES : (t + 1) * LANES
-            ]
+            block = grad[p * rows : (p + 1) * rows, t * LANES : (t + 1) * LANES]
+            blocks.append((p, j, 2 * n_gate + t * rows, block))
+    put(blocks)
 
     @pl.when(j == pl.num_programs(0) - 1)
     def _():
@@ -339,13 +357,14 @@
         gg_ref[2:3, :] = ffn_grad
         do_ref[...] = dot_nt(dy, wo_ref[...]).astype(B16)
         og = dot_tn(o_ref[...], dy).astype(B16)
+        out_blocks = []
         for f_part in range(PARTS):
             for p in range(PARTS):
                 at = (f_part * PARTS + p) * out_rows
                 for t in range(width // LANES):
-                    pack_ref[p, f_part, pl.ds(2 * n_gate + n_down + t * out_rows, out_rows), :] = (
-                        og[at : at + out_rows, t * LANES : (t + 1) * LANES]
-                    )
+                    block = og[at : at + out_rows, t * LANES : (t + 1) * LANES]
+                    out_blocks.append((p, f_part, 2 * n_gate + n_down + t * out_rows, block))
+        put(out_blocks)
 
 
 def pack_rows(width, ff, q_width):
@@ -355,47 +374,51 @@
     return gate, down, out
 
 
-def ffn_back_call(c, z, h, y, o, gd, g, u, w_out, w_gate, w_up, w_down):
+def ffn_back_call(spot, c, z, h, y, o, gd, g, u, w_out, w_gate, w_up, w_down):
     tok, width = c.shape
     ff = w_gate.shape[1]
     q_width = o.shape[1]
     gate, down, out = pack_rows(width, ff, q_width)
-    pack_shape = (PARTS, PARTS, 2 * gate + down + out, LANES)
-    cols = pl.BlockSpec((tok, FC), lambda j: (0, j))
+    pack_shape = (PARTS, PARTS, (2 * gate + down + out) // 2, LANES)
+    cols = pl.BlockSpec((tok, FC), lambda j, *_: (0, j))
     tw = whole((tok, width))
     return pl.pallas_call(
         ffn_back_kernel,
-        grid=(ff // FC,),
-        in_specs=[
-            tw,
-            tw,
-            tw,
-            tw,
-            whole(o.shape),
-            whole(gd.shape),
-            cols,
-            cols,
-            whole(w_out.shape),
-            pl.BlockSpec((width, FC), lambda j: (0, j)),
-            pl.BlockSpec((width, FC), lambda j: (0, j)),
-            pl.BlockSpec((FC, width), lambda j: (j, 0)),
-        ],
-        out_specs=[whole(pack_shape), tw, whole(o.shape), whole(gd.shape)],
+        grid_spec=pltpu.PrefetchScalarGridSpec(
+            num_scalar_prefetch=1,
+            grid=(ff // FC,),
+            in_specs=[
+                tw,
+                tw,
+                tw,
+                tw,
+                whole(o.shape),
+                whole(gd.shape),
+                cols,
+                cols,
+                whole(w_out.shape),
+                pl.BlockSpec((width, FC), lambda j, *_: (0, j)),
+                pl.BlockSpec((width, FC), lambda j, *_: (0, j)),
+                pl.BlockSpec((FC, width), lambda j, *_: (j, 0)),
+            ],
+            out_specs=[whole(pack_shape), whole(pack_shape), tw, whole(o.shape), whole(gd.shape)],
+            scratch_shapes=[
+                pltpu.VMEM((tok, width), B16),
+                pltpu.VMEM((width, tok), B16),
+                pltpu.VMEM((tok, width), F32),
+            ],
+        ),
         out_shape=[
+            sds(pack_shape, B16),
             sds(pack_shape, B16),
             sds((tok, width), F32),
             sds(o.shape, B16),
             sds(gd.shape, F32),
         ],
-        scratch_shapes=[
-            pltpu.VMEM((tok, width), B16),
-            pltpu.VMEM((width, tok), B16),
-            pltpu.VMEM((tok, width), F32),
-        ],
         compiler_params=params(),
         cost_estimate=cost(4 * tok * width * (q_width + 3 * ff), 35e6),
         name="feed_forward_back",
-    )(c, z, h, y, o, gd, g, u, w_out, w_gate, w_up, w_down)
+    )(spot, c, z, h, y, o, gd, g, u, w_out, w_gate, w_up, w_down)
 
 
 def attn_back_kernel(
@@ -448,12 +471,12 @@
         dnear_ref[...] = dkv_scr[WINDOW:, :]
 
 
-def attn_back_call(q, do, qpre, far, near, low_row, gh, cos, sin):
+def attn_back_call(q, do, qpre, far, near, low_row, gh, cos, sin, *deps):
     tok, q_width = q.shape
     block = pl.BlockSpec((QB, q_width), lambda b: (b, 0))
     table = pl.BlockSpec((QB, HD // 2), lambda b: (b, 0))
     return pl.pallas_call(
-        attn_back_kernel,
+        held_back(attn_back_kernel, 9, len(deps)),
         grid=(tok // QB,),
         in_specs=[
             block,
@@ -465,7 +488,8 @@
             whole(gh.shape),
             table,
             table,
-        ],
+        ]
+        + [pl.BlockSpec(memory_space=pl.ANY)] * len(deps),
         out_specs=[block, whole(far.shape), whole(near.shape), whole(gh.shape)],
         out_shape=[
             sds(q.shape, B16),
@@ -480,7 +504,7 @@
         compiler_params=params(),
         cost_estimate=cost(10 * tok * q_width * (WINDOW + QB), 8e6),
         name="attend_back",
-    )(q, do, qpre, far, near, low_row, gh, cos, sin)
+    )(q, do, qpre, far, near, low_row, gh, cos, sin, *deps)
 
 
 def q_back_kernel(a_ref, dq_ref, w_ref, wq_grad_ref, da_ref):
@@ -489,24 +513,29 @@
     da_ref[...] = dot_nt(dq, w_ref[...])
 
 
-def q_back_call(a, dq, w_qkv):
+def q_back_call(layer, a, dq, w_qkv, *deps):
     tok, width = a.shape
     q_width = dq.shape[1]
     return pl.pallas_call(
-        q_back_kernel,
+        held_back(q_back_kernel, 3, len(deps)),
         grid=(1,),
-        in_specs=[whole(a.shape), whole(dq.shape), whole((width, q_width))],
+        in_specs=[
+            whole(a.shape),
+            whole(dq.shape),
+            pl.BlockSpec((None, width, q_width), lambda j: (layer, 0, 0)),
+        ]
+        + [pl.BlockSpec(memory_space=pl.ANY)] * len(deps),
         out_specs=[whole((width, q_width)), whole((tok, width))],
         out_shape=[sds((width, q_width), B16), sds((tok, width), F32)],
         compiler_params=params(),
         cost_estimate=cost(4 * tok * width * q_width, 6e6),
         name="queries_back",
-    )(a, dq, w_qkv)
+    )(a, dq, w_qkv, *deps)
 
 
 def kv_back_kernel(
     a_ref, x_ref, dh_ref, da_ref, dnear_ref, dback_ref, kpre_ref, gd_ref, gh_ref,
-    cos_ref, sin_ref, w_ref, wq_ref, pack_ref, dx_ref, gd_grad_ref, gh_grad_ref,
+    cos_ref, sin_ref, w_ref, wq_ref, gd_part_ref, gh_part_ref, pack_ref, dx_ref,
 ):
     width = x_ref.shape[1]
     part = width // PARTS
@@ -523,10 +552,15 @@
     da = da_ref[...] + dot_nt(both, w_ref[...])
     add, in_grad = rms_back(x_ref[...].astype(F32), gd_ref[0:1, :], da)
     dx_ref[...] = (dh_ref[...] + add).astype(B16)
-    gd_grad_ref[...] = jnp.zeros(gd_grad_ref.shape, F32)
-    gd_grad_ref[0:1, :] = in_grad
-    gh_grad_ref[...] = jnp.zeros(gh_grad_ref.shape, F32)
-    gh_grad_ref[1:2, :] = k_grad
+    gains = [in_grad] + [gd_part_ref[i : i + 1, :] for i in range(1, 4)]
+    gains += [gh_part_ref[0:1, :], k_grad]
+    lines = [g[:, t : t + LANES] for g in gains for t in range(0, g.shape[1], LANES)]
+    n = len(lines) // PARTS
+    blank = jnp.zeros((GAIN_ROWS - n, LANES), F32)
+    for c_part in range(PARTS):
+        block = jnp.concatenate(lines[c_part * n : (c_part + 1) * n] + [blank]).astype(B16)
+        for p in range(PARTS):
+            pack_ref[c_part, p, pack_ref.shape[2] - GAIN_ROWS :, :] = block
     q_tiles = wq_ref.shape[1] // LANES
     tiles = q_tiles + 2 * HD // LANES
     each = tiles // PARTS
@@ -541,11 +575,14 @@
             pack_ref[c_part, p, slot * part : (slot + 1) * part, :] = piece
 
 
-def kv_back_call(a, x, dh, da, dnear, dback, kpre, gd, gh, cos, sin, w_qkv, wq_grad):
+def kv_back_call(
+    layer, a, x, dh, da, dnear, dback, kpre, gd, gh, cos, sin, w_qkv, wq_grad, gd_part, gh_part
+):
     tok, width = a.shape
     q_width = wq_grad.shape[1]
     part = width // PARTS
-    pack_shape = (PARTS, PARTS, part * ((q_width + 2 * HD) // LANES // PARTS), LANES)
+    rows = part * ((q_width + 2 * HD) // LANES // PARTS) + GAIN_ROWS
+    pack_shape = (PARTS, PARTS, rows, LANES)
     tw = whole((tok, width))
     return pl.pallas_call(
         kv_back_kernel,
@@ -562,137 +599,256 @@
             whole(gh.shape),
             whole(cos.shape),
             whole(sin.shape),
-            pl.BlockSpec((width, 2 * HD), lambda j: (0, q_width // (2 * HD))),
+            pl.BlockSpec((None, width, 2 * HD), lambda j: (layer, 0, q_width // (2 * HD))),
             whole(wq_grad.shape),
+            whole(gd.shape),
+            whole(gh.shape),
         ],
-        out_specs=[whole(pack_shape), tw, whole(gd.shape), whole(gh.shape)],
-        out_shape=[
-            sds(pack_shape, B16),
-            sds((tok, width), B16),
-            sds(gd.shape, F32),
-            sds(gh.shape, F32),
-        ],
+        out_specs=[whole(pack_shape), tw],
+        out_shape=[sds(pack_shape, B16), sds((tok, width), B16)],
         compiler_params=params(),
         cost_estimate=cost(8 * tok * width * HD, 10e6),
         name="keys_values_back",
-    )(a, x, dh, da, dnear, dback, kpre, gd, gh, cos, sin, w_qkv, wq_grad)
-
-
-def pack_own(qkv, gains, gate, up, down, out):
-    def by_cols(w):
-        rows, cols = w.shape
-        tiles = cols // (PARTS * LANES)
-        return (
-            w.reshape(rows, PARTS, tiles, LANES)
-            .transpose(1, 2, 0, 3)
-            .reshape(PARTS, tiles * rows, LANES)
+    )(a, x, dh, da, dnear, dback, kpre, gd, gh, cos, sin, w_qkv, wq_grad, gd_part, gh_part)
+
+
+def pack_qkv_kernel(spot, q_ref, k_ref, v_ref, gain_ref, dep_ref, all_ref, own_ref):
+    part = q_ref.shape[0]
+    refs = [(r, t) for r in (q_ref, k_ref, v_ref) for t in range(r.shape[1] // LANES)]
+    each = len(refs) // PARTS
+    for n, (ref, t) in enumerate(refs):
+        rows = slice(n % each * part, (n % each + 1) * part)
+        all_ref[n // each, rows, :] = ref[:, t * LANES : (t + 1) * LANES]
+    for c_part in range(PARTS):
+        all_ref[c_part, each * part :, :] = gain_ref[...]
+    own_ref[0] = all_ref[spot[0]]
+
+
+def pack_qkv(spot, query, key, value, gains, dep):
+    weights = (query, key, value)
+    rows = sum(w.shape[2] for w in weights) // PARTS // LANES * query.shape[1] + GAIN_ROWS
+    return pl.pallas_call(
+        pack_qkv_kernel,
+        grid_spec=pltpu.PrefetchScalarGridSpec(
+            num_scalar_prefetch=1,
+            grid=(1,),
+            in_specs=[
+                pl.BlockSpec((None,) + w.shape[1:], lambda i, spot: (0, 0, 0)) for w in weights
+            ]
+            + [whole(gains.shape), pl.BlockSpec(memory_space=pl.ANY)],
+            out_specs=[whole((PARTS, rows, LANES)), whole((1, rows, LANES))],
+        ),
+        out_shape=[sds((PARTS, rows, LANES), B16), sds((1, rows, LANES), B16)],
+        compiler_params=params(),
+        cost_estimate=cost(0, 2e6),
+        name="pack_qkv",
+    )(spot, *weights, gains, dep)
+
+
+def pack_ffn_kernel(gate_ref, up_ref, down_ref, out_ref, all_ref):
+    at = 0
+    for ref in (gate_ref, up_ref, down_ref, out_ref):
+        rows = ref.shape[0]
+        for t in range(ref.shape[1] // LANES):
+            all_ref[at : at + rows, :] = ref[:, t * LANES : (t + 1) * LANES]
+            at += rows
+
+
+def pack_ffn(gate, up, down, out):
+    by_cols = pl.BlockSpec(
+        (None, gate.shape[1], gate.shape[2] // PARTS), lambda i: (0, 0, i)
+    )
+
+    def by_rows(w):
+        return pl.BlockSpec((None, w.shape[1] // PARTS, w.shape[2]), lambda i: (0, i, 0))
+
+    rows = sum(w.size for w in (gate, up, down, out)) // PARTS // LANES
+    return pl.pallas_call(
+        pack_ffn_kernel,
+        grid=(PARTS,),
+        in_specs=[by_cols, by_cols, by_rows(down), by_rows(out)],
+        out_specs=pl.BlockSpec((None, rows, LANES), lambda i: (i, 0, 0)),
+        out_shape=sds((PARTS, rows, LANES), B16),
+        compiler_params=params(),
+        cost_estimate=cost(0, 5e6),
+        name="pack_ffn",
+    )(gate, up, down, out)
+
+
+def half_quarter_kernel(layer, spot, own_ref, other_ref, *refs):
+    mine = spot[2] == layer
+
+    @pl.when(mine)
+    def _():
+        refs[-1][...] = own_ref[...]
+
+    @pl.when(jnp.logical_not(mine))
+    def _():
+        refs[-1][...] = other_ref[...]
+
+
+def half_quarter(layer, spot, own, other, *deps):
+    shape = (1, own.shape[1] // 2, LANES)
+    block = pl.BlockSpec(shape, lambda i, spot: (spot[0], spot[2], 0))
+    return pl.pallas_call(
+        partial(half_quarter_kernel, layer),
+        grid_spec=pltpu.PrefetchScalarGridSpec(
+            num_scalar_prefetch=1,
+            grid=(1,),
+            in_specs=[block, block] + [pl.BlockSpec(memory_space=pl.ANY)] * len(deps),
+            out_specs=pl.BlockSpec(shape, lambda i, spot: (0, 0, 0)),
+        ),
+        out_shape=sds(shape, B16),
+        compiler_params=params(),
+        cost_estimate=cost(0, 1e6),
+        name="half_quarter",
+    )(spot, own, other, *deps)
+
+
+def joined(parts, *deps):
+    parts = [p if isinstance(p, tuple) else (p, 0, p.shape[1]) for p in parts]
+    counts = [p[0].shape[0] for p in parts]
+
+    def body(*refs):
+        at = 0
+        for (array, low, high), ref in zip(parts, refs):
+            refs[-1][at : at + array.shape[0]] = ref[:, low:high, :]
+            at += array.shape[0]
+
+    shape = (sum(counts), parts[0][2] - parts[0][1], LANES)
+    return pl.pallas_call(
+        body,
+        in_specs=[pl.BlockSpec(memory_space=pltpu.VMEM)] * len(parts)
+        + [pl.BlockSpec(memory_space=pl.ANY)] * len(deps),
+        out_specs=pl.BlockSpec(memory_space=pltpu.VMEM),
+        out_shape=sds(shape, B16),
+        compiler_params=params(),
+        cost_estimate=cost(0, 4 * shape[0] * shape[1] * LANES),
+        name="joined",
+    )(*[p[0] for p in parts], *deps)
+
+
+def place_qkv_kernel(spot, own_ref, other_ref, w_ref, gain_ref):
+    part = w_ref.shape[0] // PARTS
+    each = w_ref.shape[1] // LANES // PARTS
+
+    def take(ref):
+        for c_part in range(PARTS):
+            e = spot[0] ^ c_part
+            for p in range(PARTS):
+                d = spot[1] ^ p
+                at = jnp.where(d == 0, c_part, PARTS + (PARTS - 1) * e + d - 1)
+                for t in range(each):
+                    lane = (c_part * each + t) * LANES
+                    w_ref[p * part : (p + 1) * part, lane : lane + LANES] = ref[
+                        at, t * part : (t + 1) * part, :
+                    ]
+                if c_part == 0:
+                    gain_ref[p] = ref[at, ref.shape[1] - GAIN_ROWS :, :]
+
+    pl.when(pl.program_id(0) == 0)(lambda: take(own_ref))
+    pl.when(pl.program_id(0) == 1)(lambda: take(other_ref))
+
+
+def place_qkv(spot, own, other, width, cols):
+    everything = pl.BlockSpec(own.shape, lambda i, spot: (0, 0, 0))
+    return pl.pallas_call(
+        place_qkv_kernel,
+        grid_spec=pltpu.PrefetchScalarGridSpec(
+            num_scalar_prefetch=1,
+            grid=(2,),
+            in_specs=[everything, everything],
+            out_specs=[
+                pl.BlockSpec((None, width, cols), lambda i, spot: (spot[2] ^ i, 0, 0)),
+                pl.BlockSpec(
+                    (None, PARTS, GAIN_ROWS, LANES), lambda i, spot: (spot[2] ^ i, 0, 0, 0)
+                ),
+            ],
+        ),
+        out_shape=[sds((2, width, cols), B16), sds((2, PARTS, GAIN_ROWS, LANES), B16)],
+        compiler_params=params(),
+        cost_estimate=cost(0, 8e6),
+        name="place_qkv",
+    )(spot, own, other)
+
+
+def place_ffn_kernel(
+    layer, spot, own_ref, other_ref, near_ref, far_ref, got_near_ref, got_far_ref,
+    gate_ref, up_ref, down_ref, out_ref, pieces, sems,
+):
+    step = pl.program_id(0)
+    section = spot[2]
+    last = PARTS * PARTS - PARTS + 1
+    shard = pieces.at[:PARTS]
+    copies = [
+        pltpu.make_async_copy(near_ref, pieces.at[PARTS:last, section], sems.at[1]),
+        pltpu.make_async_copy(got_near_ref, pieces.at[PARTS:last, 1 - section], sems.at[2]),
+        pltpu.make_async_copy(far_ref, pieces.at[last:, section], sems.at[3]),
+        pltpu.make_async_copy(got_far_ref, pieces.at[last:, 1 - section], sems.at[4]),
+    ]
+
+    def shard_copy(do):
+        pl.when(section == layer)(lambda: do(pltpu.make_async_copy(own_ref, shard, sems.at[0])))
+        pl.when(section != layer)(lambda: do(pltpu.make_async_copy(other_ref, shard, sems.at[0])))
+
+    @pl.when(step == 0)
+    def _():
+        shard_copy(lambda copy: copy.start())
+        for copy in copies:
+            copy.start()
+        shard_copy(lambda copy: copy.wait())
+        copies[0].wait()
+        copies[1].wait()
+
+    @pl.when(step == PARTS - 1)
+    def _():
+        copies[2].wait()
+        copies[3].wait()
+
+    width, cols = gate_ref.shape
+    part = width // PARTS
+    half = pieces.shape[2]
+    c_part = spot[0] ^ step
+    for p in range(PARTS):
+        d = spot[1] ^ p
+        index = jnp.where(d == 0, c_part, PARTS + (PARTS - 1) * step + d - 1)
+
+        def piece(at, n):
+            return pieces[index, at // half, at % half : at % half + n, :]
+
+        at = 0
+        for w_ref in (gate_ref, up_ref):
+            for t in range(cols // LANES):
+                w_ref[p * part : (p + 1) * part, t * LANES : (t + 1) * LANES] = piece(at, part)
+                at += part
+        for w_ref in (down_ref, out_ref):
+            rows = w_ref.shape[2]
+            for t in range(width // LANES):
+                w_ref[p, 0, :, t * LANES : (t + 1) * LANES] = piece(at, rows)
+                at += rows
+
+
+def place_ffn(layer, spot, own, other, pieces, width, ff, q_width):
+    cols = pl.BlockSpec((width, ff // PARTS), lambda i, spot: (0, spot[0] ^ i))
+
+    def rows(n):
+        return pl.BlockSpec(
+            (PARTS, 1, n // PARTS**2, width), lambda i, spot: (0, spot[0] ^ i, 0, 0)
         )
 
-    def by_rows(w):
-        rows, cols = w.shape
-        n = rows // PARTS
-        return (
-            w.reshape(PARTS, n, cols // LANES, LANES)
-            .transpose(0, 2, 1, 3)
-            .reshape(PARTS, cols // LANES * n, LANES)
-        )
-
-    gain_rows = jnp.broadcast_to(gains[None], (PARTS,) + gains.shape)
-    return (
-        jnp.concatenate([by_cols(qkv), gain_rows], axis=1),
-        jnp.concatenate([by_cols(gate), by_cols(up), by_rows(down), by_rows(out)], axis=1),
-    )
-
-
-def pick(spot_ref, j):
-    return lax.rem(spot_ref[0] - j + PARTS, PARTS)
-
-
-def piece_specs(rows):
-    def own_map(j, spot):
-        return (jnp.where(spot[2] == 1, pick(spot, j), 0), 0, 0, 0)
-
-    def other_map(j, spot):
-        return (jnp.where(spot[2] == 1, 0, pick(spot, j)), 0, 0, 0)
-
-    shape = (1, PARTS, rows, LANES)
-    return [pl.BlockSpec(shape, own_map), pl.BlockSpec(shape, other_map)]
-
-
-def unpack_qkv_kernel(spot, own_ref, other_ref, w_ref, gain_ref):
-    part = w_ref.shape[0] // PARTS
-
-    def take(ref):
-        for p in range(PARTS):
-            d = lax.rem(spot[1] - p + PARTS, PARTS)
-            for t in range(w_ref.shape[1] // LANES):
-                w_ref[p * part : (p + 1) * part, t * LANES : (t + 1) * LANES] = ref[
-                    0, d, t * part : (t + 1) * part, :
-                ]
-            gain_ref[p] = ref[0, d, ref.shape[2] - GAIN_ROWS :, :]
-
-    pl.when(spot[2] == 1)(lambda: take(own_ref))
-    pl.when(spot[2] == 0)(lambda: take(other_ref))
-
-
-def unpack_qkv(spot, own, other, width, cols):
-    return pl.pallas_call(
-        unpack_qkv_kernel,
+    half = own.shape[1] // 2
+    shard = (PARTS, 2, half, LANES)
+    gate, up, down, out = pl.pallas_call(
+        partial(place_ffn_kernel, layer),
         grid_spec=pltpu.PrefetchScalarGridSpec(
             num_scalar_prefetch=1,
             grid=(PARTS,),
-            in_specs=piece_specs(own.shape[2]),
-            out_specs=[
-                pl.BlockSpec((width, cols // PARTS), lambda j, spot: (0, j)),
-                pl.BlockSpec((PARTS, GAIN_ROWS, LANES), lambda j, spot: (0, 0, 0)),
+            in_specs=[pl.BlockSpec(memory_space=pl.ANY)] * 6,
+            out_specs=[cols, cols, rows(ff), rows(q_width)],
+            scratch_shapes=[
+                pltpu.VMEM((PARTS * PARTS, 2, half, LANES), B16),
+                pltpu.SemaphoreType.DMA((5,)),
             ],
-        ),
-        out_shape=[sds((width, cols), B16), sds((PARTS, GAIN_ROWS, LANES), B16)],
-        compiler_params=params(),
-        cost_estimate=cost(0, 6e6),
-        name="place_qkv",
-    )(spot, own, other)
-
-
-def unpack_ffn_kernel(spot, own_ref, other_ref, gate_ref, up_ref, down_ref, out_ref):
-    width, cols = gate_ref.shape
-    part = width // PARTS
-    tiles = cols // LANES
-    n_gate = tiles * part
-
-    def take(ref):
-        for p in range(PARTS):
-            d = lax.rem(spot[1] - p + PARTS, PARTS)
-            for n, w_ref in enumerate((gate_ref, up_ref)):
-                for t in range(tiles):
-                    at = n * n_gate + t * part
-                    w_ref[p * part : (p + 1) * part, t * LANES : (t + 1) * LANES] = ref[
-                        0, d, at : at + part, :
-                    ]
-            at = 2 * n_gate
-            for w_ref in (down_ref, out_ref):
-                rows = w_ref.shape[2]
-                for t in range(width // LANES):
-                    w_ref[p, 0, :, t * LANES : (t + 1) * LANES] = ref[0, d, at : at + rows, :]
-                    at += rows
-
-    pl.when(spot[2] == 1)(lambda: take(own_ref))
-    pl.when(spot[2] == 0)(lambda: take(other_ref))
-
-
-def unpack_ffn(spot, own, other, width, ff, q_width):
-    cols = pl.BlockSpec((width, ff // PARTS), lambda j, spot: (0, j))
-
-    def rows(n):
-        return pl.BlockSpec((PARTS, 1, n // PARTS**2, width), lambda j, spot: (0, j, 0, 0))
-
-    gate, up, down, out = pl.pallas_call(
-        unpack_ffn_kernel,
-        grid_spec=pltpu.PrefetchScalarGridSpec(
-            num_scalar_prefetch=1,
-            grid=(PARTS,),
-            in_specs=piece_specs(own.shape[2]),
-            out_specs=[cols, cols, rows(ff), rows(q_width)],
         ),
         out_shape=[
             sds((width, ff), B16),
@@ -701,10 +857,196 @@
             sds((PARTS, PARTS, q_width // PARTS**2, width), B16),
         ],
         compiler_params=params(),
-        cost_estimate=cost(0, 22e6),
+        cost_estimate=cost(0, 18e6),
         name="place_ffn",
-    )(spot, own, other)
+    )(spot, own.reshape(shard), other.reshape(shard), *pieces)
     return gate, up, down.reshape(ff, width), out.reshape(q_width, width)
+
+
+def add_split_kernel(spot, first_ref, second_ref, *refs):
+    keep_a, send_a, keep_b, send_b = refs[-PARTS:]
+    half = first_ref.shape[1] // 2
+    a, b = slice(0, half), slice(half, 2 * half)
+    for rows, far, out, n in (
+        (a, 0, keep_a, 0), (a, 2, keep_a, 1), (a, 1, send_a, 0), (a, 3, send_a, 1),
+        (b, 0, keep_b, 0), (b, 1, keep_b, 1), (b, 2, send_b, 0), (b, 3, send_b, 1),
+    ):
+        c_part = spot[0] ^ far
+        total = first_ref[c_part, rows, :].astype(F32) + second_ref[c_part, rows, :].astype(F32)
+        out[n] = total.astype(B16)
+
+
+def add_split(spot, first, second, *deps):
+    n = first.shape[2]
+    block = pl.BlockSpec((PARTS, None, n, LANES), lambda i, spot: (0, i, 0, 0))
+    out = pl.BlockSpec((2, None, n // 2, LANES), lambda i, spot: (0, i, 0, 0))
+    return pl.pallas_call(
+        add_split_kernel,
+        grid_spec=pltpu.PrefetchScalarGridSpec(
+            num_scalar_prefetch=1,
+            grid=(PARTS,),
+            in_specs=[block, block] + [pl.BlockSpec(memory_space=pl.ANY)] * len(deps),
+            out_specs=[out] * PARTS,
+        ),
+        out_shape=[sds((2, PARTS, n // 2, LANES), B16)] * PARTS,
+        compiler_params=params(),
+        cost_estimate=cost(0, 3 * 2 * first.size),
+        name="add_split",
+    )(spot, first, second, *deps)
+
+
+def add_pairs_kernel(a_ref, b_ref, c_ref, d_ref, *refs):
+    refs[-2][...] = (a_ref[...].astype(F32) + b_ref[...].astype(F32)).astype(B16)
+    refs[-1][...] = (c_ref[...].astype(F32) + d_ref[...].astype(F32)).astype(B16)
+
+
+def add_pairs(a, b, c, d, *deps):
+    shape = a.shape[1:]
+    return pl.pallas_call(
+        add_pairs_kernel,
+        grid=(1,),
+        in_specs=[pl.BlockSpec((None,) + shape, lambda i: (1, 0, 0, 0))] * 4
+        + [pl.BlockSpec(memory_space=pl.ANY)] * len(deps),
+        out_specs=[whole(shape)] * 2,
+        out_shape=[sds(shape, B16)] * 2,
+        compiler_params=params(),
+        cost_estimate=cost(0, 6 * a.size),
+        name="add_pairs",
+    )(a, b, c, d, *deps)
+
+
+def sum_parts_kernel(spot, a0, a1, a2, b0, b1, b2, *refs):
+    outs = refs[-PARTS:]
+    half = a0.shape[1]
+    for d in range(PARTS):
+        f = spot[1] ^ d
+        for rows, terms in ((slice(0, half), (a0, a1, a2)), (slice(half, 2 * half), (b0, b1, b2))):
+            total = sum(term[f].astype(F32) for term in terms)
+            outs[d][rows, :] = total.astype(B16)
+
+
+def sum_parts(spot, split, got, last, *deps):
+    keep_a, _, keep_b, _ = split
+    shape = keep_a.shape[1:]
+    first = pl.BlockSpec((None,) + shape, lambda i, spot: (0, 0, 0, 0))
+    one = whole(shape)
+    out = (2 * shape[1], LANES)
+    return pl.pallas_call(
+        sum_parts_kernel,
+        grid_spec=pltpu.PrefetchScalarGridSpec(
+            num_scalar_prefetch=1,
+            grid=(1,),
+            in_specs=[first, first, one] * 2 + [pl.BlockSpec(memory_space=pl.ANY)] * len(deps),
+            out_specs=[whole(out)] * PARTS,
+        ),
+        out_shape=[sds(out, B16)] * PARTS,
+        compiler_params=params(),
+        cost_estimate=cost(0, 10 * keep_a.size),
+        name="sum_parts",
+    )(spot, keep_a, got[0], last[0], keep_b, got[1], last[1], *deps)
+
+
+def choose_ring_kernel(spot, *refs):
+    firsts, seconds, out_ref = refs[:PARTS], refs[PARTS : 2 * PARTS], refs[-1]
+    rows = out_ref.shape[1]
+    for e in range(PARTS):
+
+        @pl.when(spot[2] == 0)
+        def _():
+            out_ref[e] = seconds[e][...]
+
+        @pl.when(spot[2] == 1)
+        def _():
+            out_ref[e] = firsts[e][:rows, :]
+
+
+def choose_ring(spot, firsts, seconds):
+    shape = (PARTS,) + seconds[0].shape
+    return pl.pallas_call(
+        choose_ring_kernel,
+        grid_spec=pltpu.PrefetchScalarGridSpec(
+            num_scalar_prefetch=1,
+            grid=(1,),
+            in_specs=[whole(p.shape) for p in (*firsts, *seconds)],
+            out_specs=whole(shape),
+        ),
+        out_shape=sds(shape, B16),
+        compiler_params=params(),
+        cost_estimate=cost(0, 4e6),
+        name="choose_ring",
+    )(spot, *firsts, *seconds)
+
+
+def finish_kernel(spot, *refs):
+    firsts, seconds, got_ref = refs[:PARTS], refs[PARTS : 2 * PARTS], refs[2 * PARTS]
+    gate_ref, up_ref, down_ref, out_ref, qkv_ref, gain_ref, mine_ref = refs[2 * PARTS + 1 :]
+    half = got_ref.shape[1]
+    part = gate_ref.shape[0]
+    for e in range(PARTS):
+
+        @pl.when(pl.program_id(0) == e)
+        def _():
+            mine_ref[1 - spot[2]] = got_ref[e]
+            n = qkv_ref.shape[1] // LANES
+            for t in range(n):
+                at = half + t * part
+                qkv_ref[:, t * LANES : (t + 1) * LANES] = firsts[e][at : at + part, :].astype(F32)
+            gain_ref[...] = firsts[e][half + n * part :, :].astype(F32)
+
+            @pl.when(spot[2] == 0)
+            def _():
+                mine_ref[0] = firsts[e][:half, :]
+
+            @pl.when(spot[2] == 1)
+            def _():
+                mine_ref[1] = seconds[e][...]
+
+    at = 0
+    for ref in (gate_ref, up_ref, down_ref, out_ref):
+        rows = ref.shape[0]
+        for t in range(ref.shape[1] // LANES):
+            block = mine_ref[at // half, at % half : at % half + rows, :]
+            ref[:, t * LANES : (t + 1) * LANES] = block.astype(F32)
+            at += rows
+
+
+def finish(spot, firsts, seconds, got, width, ff, q_width):
+    part, cols, qkv_cols = width // PARTS, ff // PARTS, (q_width + 2 * HD) // PARTS
+
+    def by_cols(n):
+        return pl.BlockSpec((None, part, n), lambda i, spot: (0, 0, spot[0] ^ i))
+
+    def by_rows(n):
+        return pl.BlockSpec((None, n, width), lambda i, spot: (0, spot[0] ^ i, 0))
+
+    return pl.pallas_call(
+        finish_kernel,
+        grid_spec=pltpu.PrefetchScalarGridSpec(
+            num_scalar_prefetch=1,
+            grid=(PARTS,),
+            in_specs=[whole(p.shape) for p in (*firsts, *seconds, got)],
+            out_specs=[
+                by_cols(cols),
+                by_cols(cols),
+                by_rows(ff // PARTS**2),
+                by_rows(q_width // PARTS**2),
+                by_cols(qkv_cols),
+                pl.BlockSpec((None, GAIN_ROWS, LANES), lambda i, spot: (spot[0] ^ i, 0, 0)),
+            ],
+            scratch_shapes=[pltpu.VMEM((2,) + seconds[0].shape, B16)],
+        ),
+        out_shape=[
+            sds((1, part, ff), F32),
+            sds((1, part, ff), F32),
+            sds((1, ff // PARTS, width), F32),
+            sds((1, q_width // PARTS, width), F32),
+            sds((1, part, q_width + 2 * HD), F32),
+            sds((PARTS, GAIN_ROWS, LANES), F32),
+        ],
+        compiler_params=params(),
+        cost_estimate=cost(0, 12e6),
+        name="finish",
+    )(spot, *firsts, *seconds, got)
 
 
 def split_pack(pack, width, ff, q_width):
@@ -735,21 +1077,22 @@
     )
 
 
-def moved(array, axis, by, layer):
+def moved(array, axis, far, layer=None):
     sizes = [lax.axis_size(name) for name in AXES]
     pairs = []
-    for f in range(sizes[1]):
-        for c in range(sizes[2]):
-            f2 = (f + by) % sizes[1] if axis == "fsdp" else f
-            c2 = (c + by) % sizes[2] if axis == "ctx" else c
-            pairs.append(
-                ((layer * sizes[1] + f) * sizes[2] + c, (layer * sizes[1] + f2) * sizes[2] + c2)
-            )
+    for s in range(sizes[0]) if layer is None else [layer]:
+        for f in range(sizes[1]):
+            for c in range(sizes[2]):
+                f2 = f ^ far if axis == "fsdp" else f
+                c2 = c ^ far if axis == "ctx" else c
+                pairs.append(
+                    ((s * sizes[1] + f) * sizes[2] + c, (s * sizes[1] + f2) * sizes[2] + c2)
+                )
     return lax.ppermute(array, AXES, pairs)
 
 
-def handed(array, to):
-    return lax.ppermute(array, "section", [(1 - to, to)])
+def swapped(array):
+    return lax.ppermute(array, "section", [(0, 1), (1, 0)])
 
 
 def passed_along(array, by):
@@ -758,35 +1101,48 @@
     return lax.ppermute(array, "ctx", pairs)
 
 
-def gathered_pieces(own, layer):
-    shards = [own[0]] + [moved(own[0], "fsdp", d, layer) for d in range(1, PARTS)]
-    travelling = jnp.stack(shards[1:])
-    quarters = [jnp.stack(shards)]
-    for e in range(1, PARTS):
-        quarters.append(jnp.concatenate([own[e][None], moved(travelling, "ctx", e, layer)]))
-    return jnp.stack(quarters)
+FAR = range(1, PARTS)
+
+
+def other_shards(quarter, layer=None):
+    return [moved(quarter, "fsdp", d, layer) for d in FAR]
 
 
 def at(array, index):
-    return lax.dynamic_index_in_dim(array, lax.rem(index, PARTS), 0, keepdims=False)
-
-
-def reduced_pieces(pack, layer, fsdp_index, ctx_index):
-    other = handed(pack, layer)
-
-    def both(index):
-        return at(pack, index).astype(F32) + at(other, index).astype(F32)
-
-    total = both(ctx_index)
-    for e in range(1, PARTS):
-        total += moved(both(ctx_index + e).astype(B16), "ctx", e, layer).astype(F32)
-    rounded = total.astype(B16)
-    piece = at(total, fsdp_index)
-    for d in range(1, PARTS):
-        piece += moved(at(rounded, fsdp_index + d), "fsdp", d, layer).astype(F32)
-    piece = piece.astype(B16)
-    ring = jnp.stack([piece] + [moved(piece, "ctx", e, layer) for e in range(1, PARTS)])
-    return jnp.stack([at(ring, ctx_index - p + PARTS) for p in range(PARTS)])
+    return lax.dynamic_index_in_dim(array, index, 0, keepdims=False)
+
+
+def near_quarters(shards, layer=None):
+    return moved(shards, "ctx", 1, layer), moved(shards, "ctx", 2, layer)
+
+
+def far_quarter(near, deps=(), layer=None):
+    one, two = near
+    rows = one.shape[1]
+    by_one = moved(joined([(one, 0, rows // 2)], *deps), "ctx", 2, layer)
+    by_two = moved(joined([(two, rows // 2, rows)], *deps), "ctx", 1, layer)
+    return jnp.concatenate([by_one, by_two], axis=1)
+
+
+def ctx_near(split):
+    return moved(split[1], "ctx", 1), moved(split[3], "ctx", 2)
+
+
+def ctx_far(split, got, *deps):
+    keep_a, _, keep_b, _ = split
+    send_a, send_b = add_pairs(keep_a, got[0], keep_b, got[1], *deps)
+    return moved(send_a, "ctx", 2), moved(send_b, "ctx", 1)
+
+
+def fsdp_summed(parts, layer=None):
+    total = parts[0].astype(F32)
+    for d in FAR:
+        total += moved(parts[d], "fsdp", d, layer).astype(F32)
+    return total.astype(B16)
+
+
+def ctx_ring(piece):
+    return [piece] + [moved(piece, "ctx", e) for e in FAR]
 
 
 def per_device(
@@ -831,36 +1187,47 @@
         gh = jnp.concatenate(gh + [jnp.zeros((6, HD), raw.dtype)]).astype(F32)
         return gd, gh
 
-    layers = []
+    spot = jnp.stack([ctx_index, fsdp_index, section]).astype(jnp.int32)
     if in_pieces:
         gain_rows = jnp.pad(gain_own, (0, GAIN_ROWS * LANES - gain_own.shape[0]))
-        packs = pack_own(
-            qkv_own,
-            gain_rows.reshape(GAIN_ROWS, LANES),
-            gate_weight[0],
-            up_weight[0],
-            down_weight[0],
-            out_weight[0],
+        gain_rows = gain_rows.reshape(GAIN_ROWS, LANES)
+        ffn_parts = pack_ffn(gate_weight, up_weight, down_weight, out_weight)
+        ffn_other = swapped(ffn_parts)
+        qkv_parts, quarter = pack_qkv(
+            spot, query_weight, key_weight, value_weight, gain_rows, ffn_parts
         )
 
-        def own_first(pack):
-            back = pack[::-1]
-            return lax.dynamic_slice_in_dim(
-                jnp.concatenate([back, back]), PARTS - 1 - ctx_index, PARTS, 0
+        def arriving(layer, *deps):
+            own = half_quarter(layer, spot, ffn_parts, ffn_other, *deps)
+            return own, other_shards(own)
+
+        first_own, first_arriving = arriving(0)
+        shards_in = joined(other_shards(quarter), first_own)
+        near = near_quarters(shards_in)
+        pieces = joined([qkv_parts, shards_in, *near, far_quarter(near)])
+        w_qkv, raw = place_qkv(spot, pieces, swapped(pieces), width, q_width + 2 * HD)
+        raw = raw.reshape(2, PARTS, GAIN_ROWS * LANES)
+        first_shards = joined(first_arriving, w_qkv)
+        first_near = near_quarters(first_shards)
+        _, second_arriving = arriving(1, first_shards)
+
+        def place(layer, shards, near, *deps):
+            far = far_quarter(near, deps)
+            near = joined([shards, *near])
+            pieces = [near, far, swapped(near), swapped(far)]
+            gate, up, down, out = place_ffn(
+                layer, spot, ffn_parts, ffn_other, pieces, width, ff, q_width
             )
-
-        packs = [own_first(pack) for pack in packs]
-        for layer in range(2):
-            spot = jnp.stack([ctx_index, fsdp_index, (section == layer).astype(jnp.int32)])
-            spot = spot.astype(jnp.int32)
-            pieces = gathered_pieces(packs[0], layer)
-            other = handed(pieces, 1 - layer)
-            w_qkv, raw = unpack_qkv(spot, pieces, other, width, qkv_own.shape[1])
-            gains = as_gains(raw.reshape(PARTS, GAIN_ROWS * LANES))
-            pieces = gathered_pieces(packs[1], layer)
-            other = handed(pieces, 1 - layer)
-            gate, up, down, out = unpack_ffn(spot, pieces, other, width, ff, q_width)
-            layers.append((w_qkv, out, gate, up, down) + gains)
+            return out, gate, up, down
+
+        def place_first(q, o):
+            return place(0, first_shards, first_near, q)
+
+        def place_second(q, o):
+            shards = joined(second_arriving, kept[0][7])
+            return place(1, shards, near_quarters(shards), kept[0][13])
+
+        ffn_layers = [place_first, place_second]
     else:
 
         def whole_weight(own):
@@ -871,9 +1238,9 @@
             whole_weight(w)
             for w in (qkv_own, out_weight[0], gate_weight[0], up_weight[0], down_weight[0])
         ]
+        w_qkv = full[0]
         raw = whole_weight(gain_own[None])
-        for layer in range(2):
-            layers.append(tuple(w[layer] for w in full) + as_gains(raw[layer]))
+        ffn_layers = [lambda *deps, n=n: tuple(w[n] for w in full[1:]) for n in range(2)]
 
     def own_row(array):
         return lax.dynamic_index_in_dim(array[:, 0], section, 0, keepdims=False)
@@ -884,85 +1251,98 @@
 
     x = own_row(inputs)
     kept = []
-    for w_qkv, w_out, w_gate, w_up, w_down, gd, gh in layers:
-        a, kpre, near = kv_call(x, gd, gh, cos, sin, w_qkv)
+    for layer in range(2):
+        gd, gh = as_gains(raw[layer])
+        a, kpre, near = kv_call(layer, x, gd, gh, cos, sin, w_qkv)
         far = passed_along(near, 1)
-        qpre, q = q_call(a, gh, cos, sin, w_qkv)
+        qpre, q = q_call(layer, a, gh, cos, sin, w_qkv)
         o = attn_call(q, far, near, low_col)
-        y, h, g, u, z, result = ffn_call(o, x, gd, w_out, w_gate, w_up, w_down)
-        kept.append((x, a, kpre, near, far, qpre, q, o, y, h, g, u, z, result))
+        weights = ffn_layers[layer](q, o)
+        y, h, g, u, z, result = ffn_call(o, x, gd, *weights)
+        kept.append((x, a, kpre, near, far, qpre, q, o, y, h, g, u, z, result, gd, gh, weights))
         x = result
 
-    cot = own_row(grad_out)
-    packs, in_grads, gain_grads = [None] * 2, [None] * 2, [None] * 2
-    for layer in (1, 0):
-        w_qkv, w_out, w_gate, w_up, w_down, gd, gh = layers[layer]
-        x, a, kpre, near, far, qpre, q, o, y, h, g, u, z, result = kept[layer]
-        ffn_pack, dh, do, gd_one = ffn_back_call(
-            cot, z, h, y, o, gd, g, u, w_out, w_gate, w_up, w_down
+    spot_back = spot if in_pieces else jnp.zeros_like(spot)
+
+    def layer_back(layer, cot, attn_deps, q_deps):
+        x, a, kpre, near, far, qpre, q, o, y, h, g, u, z, result, gd, gh, weights = kept[layer]
+        keep, send, dh, do, gd_part = ffn_back_call(spot_back, cot, z, h, y, o, gd, g, u, *weights)
+        dq, dfar, dnear, gh_part = attn_back_call(
+            q, do, qpre, far, near, low_row, gh, cos, sin, *attn_deps(keep, send)
         )
-        dq, dfar, dnear, gh_one = attn_back_call(q, do, qpre, far, near, low_row, gh, cos, sin)
         dback = passed_along(dfar, -1)
         if tok > WINDOW:
             dback = jnp.pad(dback, ((tok - WINDOW, 0), (0, 0)))
-        wq_grad, da = q_back_call(a, dq, w_qkv)
-        qkv_pack, cot, gd_two, gh_two = kv_back_call(
-            a, x, dh, da, dnear, dback, kpre, gd, gh, cos, sin, w_qkv, wq_grad
+        wq_grad, da = q_back_call(layer, a, dq, w_qkv, *q_deps(keep, send, dq))
+        qkv_pack, dx = kv_back_call(
+            layer, a, x, dh, da, dnear, dback, kpre, gd, gh, cos, sin, w_qkv, wq_grad,
+            gd_part, gh_part,
         )
-        in_grads[layer] = cot
-        packs[layer] = (ffn_pack, qkv_pack)
-        gain_grads[layer] = jnp.concatenate(
-            [(gd_one + gd_two)[:4].reshape(-1), (gh_one + gh_two)[:2].reshape(-1)]
+        return (keep, send), qkv_pack, dx
+
+    cot = own_row(grad_out)
+    if in_pieces:
+        state = {}
+
+        def split_second(keep, send, dq):
+            state["split1"] = add_split(spot, keep, swapped(send))
+            state["near1"] = ctx_near(state["split1"])
+            return (state["split1"][0],)
+
+        ffn_pack, qkv_pack, mid = layer_back(1, cot, lambda *_: (), split_second)
+
+        def far_second(keep, send):
+            state["far1"] = ctx_far(state["split1"], state["near1"], keep)
+            return ()
+
+        def split_first(keep, send, dq):
+            parts = sum_parts(spot, state["split1"], state["near1"], state["far1"], dq)
+            state["split0"] = add_split(spot, keep, swapped(send), dq)
+            state["near0"] = ctx_near(state["split0"])
+            state["ffn1"] = fsdp_summed(parts)
+            return (state["split0"][0], parts[0])
+
+        first_ffn_pack, first_qkv_pack, grad_in = layer_back(0, mid, far_second, split_first)
+    else:
+        ffn_pack, qkv_pack, mid = layer_back(1, cot, lambda *_: (), lambda *_: ())
+        first_ffn_pack, first_qkv_pack, grad_in = layer_back(0, mid, lambda *_: (), lambda *_: ())
+    packs = [(first_ffn_pack, first_qkv_pack), (ffn_pack, qkv_pack)]
+    in_grads = [grad_in, mid]
+
+    mine = jnp.stack([kept[0][13], in_grads[0]])
+    others = jnp.stack([kept[1][13], in_grads[1]])
+    got = swapped(jnp.where(first_layer, others, mine))
+    mine = jnp.where(first_layer, mine, others)
+    activations, input_grads = [
+        jnp.stack([jnp.where(first_layer, mine[n], got[n]), jnp.where(first_layer, got[n], mine[n])])
+        for n in range(2)
+    ]
+
+    if in_pieces:
+        keep = jnp.where(first_layer, first_qkv_pack, qkv_pack)
+        qkv_split = add_split(spot, keep, swapped(jnp.where(first_layer, qkv_pack, first_qkv_pack)))
+        seconds = ctx_ring(state["ffn1"])
+        far0 = ctx_far(state["split0"], state["near0"])
+        ffn0 = fsdp_summed(sum_parts(spot, state["split0"], state["near0"], far0))
+        qkv_near = ctx_near(qkv_split)
+        qkv_far = ctx_far(qkv_split, qkv_near)
+        qkv_own = fsdp_summed(sum_parts(spot, qkv_split, qkv_near, qkv_far))
+        firsts = ctx_ring(jnp.concatenate([ffn0, qkv_own]))
+        got = swapped(choose_ring(spot, firsts, seconds))
+        gate_g, up_g, down_g, out_g, qkv_g, gain_sums = finish(
+            spot, firsts, seconds, got, width, ff, q_width
         )
-
-    def by_layer(first, second):
-        own = jnp.where(first_layer, first, second)
-        got = lax.ppermute(jnp.where(first_layer, second, first), "section", [(0, 1), (1, 0)])
-        return jnp.stack([jnp.where(first_layer, own, got), jnp.where(first_layer, got, own)])
-
-    activations = by_layer(kept[0][-1], kept[1][-1])
-    input_grads = by_layer(in_grads[0], in_grads[1])
-
-    gain_sums = lax.psum(jnp.stack(gain_grads), AXES)
-    gain_sums = lax.dynamic_index_in_dim(gain_sums, section, 0, keepdims=False)
-
-    def gain_shard(first, n):
-        return lax.dynamic_slice_in_dim(gain_sums, first + fsdp_index * n, n, 0)[None]
-
-    dn, hn = width // shards, HD // shards
-    d_gains = [gain_shard(i * width, dn) for i in range(4)]
-    h_gains = [gain_shard(4 * width + i * HD, hn) for i in range(2)]
-
-    if in_pieces:
-        done = [None] * 2
-        for layer in (1, 0):
-            done[layer] = tuple(
-                reduced_pieces(p, layer, fsdp_index, ctx_index) for p in packs[layer]
-            )
-        ffn_own, qkv_own = (jnp.where(first_layer, p, r) for p, r in zip(*done))
-        n_gate, n_down, n_out = pack_rows(width, ff, q_width)
-        part = width // PARTS
-
-        def cols(p):
-            tiles = p.shape[1] // part
-            return p.reshape(PARTS, tiles, part, LANES).transpose(2, 0, 1, 3).reshape(part, -1)
-
-        def rows(p):
-            n = p.shape[1] // (width // LANES)
-            return (
-                p.reshape(PARTS, width // LANES, n, LANES).transpose(0, 2, 1, 3).reshape(-1, width)
-            )
-
-        gate_g = cols(ffn_own[:, :n_gate])
-        up_g = cols(ffn_own[:, n_gate : 2 * n_gate])
-        down_g = rows(ffn_own[:, 2 * n_gate : 2 * n_gate + n_down])
-        out_g = rows(ffn_own[:, 2 * n_gate + n_down :])
-        qkv_g = cols(qkv_own)
+        gain_sums = gain_sums[:, : (4 * width + 2 * HD) // LANES // PARTS].reshape(-1)
     else:
         sums = []
-        for ffn_pack, qkv_pack in packs:
+        gain_sums = []
+        for halves, qkv_pack in packs:
+            ffn_pack = jnp.concatenate(halves, axis=2)
             gate, up, down, out = split_pack(ffn_pack, width, ff, q_width)
             part = width // PARTS
+            n = (4 * width + 2 * HD) // LANES // PARTS
+            gain_sums.append(qkv_pack[:, 0, -GAIN_ROWS:][:, :n].reshape(-1))
+            qkv_pack = qkv_pack[:, :, :-GAIN_ROWS]
             tiles = qkv_pack.shape[2] // part
             qkv = (
                 qkv_pack.reshape(PARTS, PARTS, tiles, part, LANES)
@@ -979,11 +1359,18 @@
             )
             for pair in zip(*sums)
         ]
-        gate_g, up_g, down_g, out_g, qkv_g = lax.psum(tuple(shard), "ctx")
-
-    gate_g, up_g, down_g, out_g, qkv_g = (
-        w.astype(F32)[None] for w in (gate_g, up_g, down_g, out_g, qkv_g)
-    )
+        gate_g, up_g, down_g, out_g, qkv_g = (
+            w.astype(F32)[None] for w in lax.psum(tuple(shard), "ctx")
+        )
+        gain_sums = at(lax.psum(jnp.stack(gain_sums), AXES), section).astype(F32)
+
+    def gain_shard(first, n):
+        return lax.dynamic_slice_in_dim(gain_sums, first + fsdp_index * n, n, 0)[None]
+
+    dn, hn = width // shards, HD // shards
+    d_gains = [gain_shard(i * width, dn) for i in range(4)]
+    h_gains = [gain_shard(4 * width + i * HD, hn) for i in range(2)]
+
     return (
         activations[None, :, None],
         input_grads[None, :, None],

time: 814 us -> 552 us (0.68)
  starting transfers between devices: 191 us -> 88.3 us
  blocking collectives: 87.1 us -> 0 us
  waiting for transfers between devices: 222 us -> 138 us
  Pallas kernels: 185 us -> 268 us
  other arithmetic: 76.9 us -> 15.9 us
    psum x1 -> x0, blocking collectives: 87.1 us -> none  [per_device(): gain_sums = lax.psum(jnp.stack(gain_grads), AXES)]
    pallas_call x10 -> x36, Pallas kernels: 116 us -> 199 us  [the longest x2 52.9 us: ffn_back_call(): pl.pallas_call(ffn_back_kernel, grid_spec=pltpu.PrefetchScalarGridSpec(nu...]
    ppermute x60 -> x48, starting transfers between devices: 145 us -> 78.6 us  [moved(): return lax.ppermute(array, AXES, pairs)]
    ppermute x60 -> x48, waiting for transfers between devices: 201 us -> 136 us  [moved(): return lax.ppermute(array, AXES, pairs)]
    convert_element_type x17 -> x3, other arithmetic: 41.2 us -> 0.38 us  [fsdp_summed(): return total.astype(B16)]
    ppermute x10 -> x11, starting transfers between devices: 36.5 us -> 1.55 us  [swapped(): return lax.ppermute(array, 'section', [(0, 1), (1, 0)])]
    ppermute x4, waiting for transfers between devices: 21.3 us -> 1.49 us  [passed_along(): return lax.ppermute(array, 'ctx', pairs)]
    another operation x26 -> x2, other arithmetic: 20.4 us -> 0.76 us  [the longest x1 0.59 us: per_device(): spot = jnp.stack([ctx_index, fsdp_index, section]).astype(jnp.int32)]
  transfers between devices with their start and end apart: 74 -> 63, of which waited for: 22 -> 22; matrix products, arithmetic and copies ran while one was open for 9% -> 3% of each run, Pallas kernels for 17% -> 35%
where the time goes in v2:
time: 552 us; the launch traced here: 546 us
  Pallas kernels  268 us (49%)
  waiting for transfers between devices  138 us (25%)
  starting transfers between devices  88.3 us (16%)
  local copies, waits for them, and re-layouts  34.4 us (6%)
  other arithmetic  15.9 us (3%)
    ppermute x48, waiting for transfers between devices, moved(): return lax.ppermute(array, AXES, pairs)  136 us
    ppermute x48, starting transfers between devices, moved(): return lax.ppermute(array, AXES, pairs)  78.6 us
    pallas_call x2, Pallas kernels, ffn_back_call(): pl.pallas_call(ffn_back_kernel, grid_spec=pltpu.PrefetchScalarGridSpec(nu...  52.9 us
    pallas_call x2, Pallas kernels, attn_back_call(): pl.pallas_call(held_back(attn_back_kernel, 9, len(deps)), grid=(tok // QB...  29.2 us
    pallas_call x2, Pallas kernels, ffn_call(): pl.pallas_call(ffn_kernel, grid=(ff // FC,), in_specs=[whole(o.shape), tw...  27.3 us
    pallas_call x12, Pallas kernels, joined(): pl.pallas_call(body, in_specs=[pl.BlockSpec(memory_space=pltpu.VMEM)] * l...  26.9 us
    unnamed x147, local copies, waits for them, and re-layouts  22.4 us
    pallas_call x3, Pallas kernels, add_split(): pl.pallas_call(add_split_kernel, grid_spec=pltpu.PrefetchScalarGridSpec(n...  19.2 us
  transfers between devices with their start and end apart: 63, of which 22 were waited for; matrix products, arithmetic and copies ran while one was open for 3% of the time, Pallas kernels for 35%

profile of v2, /device:TPU:0, one launch (start us, length us, event | category | flops | bytes accessed | tf_op | source)
XLA Modules:
  0.0 546.1 jit_solution(7454460709209501869)
XLA Ops:
  0.7 4.2 pack_ffn.1.dep_ref.own_ref
  18.6 6.5 %collective-permute-done.1.refs_1_ = bf16[1,512,128]{2,1,0:T(8,128)(2,1)S(1)} collective-permute-done((bf16[1,512,128]{2,1,0:T(8,128)(2,1)}, bf16[1,512,128]{2,1,0:T(8,128)(2,1)S(1)}, u32[]{:S(2)}, u32[]{:S(2)}) %collective-permute-start.1) | collective-permute-done | bytes 131104 | tf_op jit(solution)/shard_map/ppermute | solution.py:1091
  31.2 6.4 %collective-permute-done.4.refs_0_.refs_2_ = bf16[3,512,128]{2,1,0:T(8,128)(2,1)S(1)} collective-permute-done((bf16[3,512,128]{2,1,0:T(8,128)(2,1)}, bf16[3,512,128]{2,1,0:T(8,128)(2,1)S(1)}, u32[]{:S(2)}, u32[]{:S(2)}) %collective-permute-start.4) | collective-permute-done | bytes 393248 | tf_op jit(solution)/shard_map/ppermute | solution.py:1091
  45.9 4.0 collective-permute-done.7
  50.6 3.0 joined.15.own_ref
  56.6 3.3 collective-permute-start.10
  65.5 5.2 place_qkv.1
  73.0 9.7 %collective-permute-done.11.refs_1_ = bf16[1,1120,128]{2,1,0:T(8,128)(2,1)S(1)} collective-permute-done((bf16[1,1120,128]{2,1,0:T(8,128)(2,1)S(1)}, bf16[1,1120,128]{2,1,0:T(8,128)(2,1)S(1)}, u32[]{:S(2)}, u32[]{:S(2)}) %collective-permute-start.11) | collective-permute-done | bytes 286752 | tf_op jit(solution)/shard_map/ppermute | solution.py:1091
  88.2 5.9 %collective-permute-start.20 = (bf16[1,1120,128]{2,1,0:T(8,128)(2,1)}, bf16[1,1120,128]{2,1,0:T(8,128)(2,1)S(1)}, u32[]{:S(2)}, u32[]{:S(2)}) collective-permute-start(bf16[1,1120,128]{2,1,0:T(8,128)(2,1)} %half_quarter.3), channel_id=1, source_target_pairs={{0,4},{1,5},{2,6},{3,7},{4,0},{5,1},{6,2},{7,3},{8,12},{9,13},{10,... | collective-permute-start | bytes 860168 | tf_op jit(solution)/shard_map/ppermute | solution.py:1091
  99.4 3.1 keys_values.2
  102.5 2.9 collective-permute-start.9
  105.4 4.9 queries.2
  110.3 5.1 collective-permute-done.14.refs_2_.refs_0_
  122.3 3.4 joined.17.near_ref
  129.0 6.4 %attend.2.o_ref.refs_3_ = bf16[512,1024]{1,0:T(8,128)(2,1)} custom-call(bf16[512,1024]{1,0:T(8,128)(2,1)} %get-tuple-element.116.q_ref.refs_1_.refs_0_, bf16[512,512]{1,0:T(8,128)(2,1)} %copy-done.65, bf16[512,512]{1,0:T(8,128)(2,1)} %get-tuple-element.117.near_ref.refs_4_, s32[512,1]{1,0:T(8,128)} %subtract_add_fusion.low_ref), custom_call_target="tpu_custom_call" | custom-call | flops 40265318400 | bytes 3000000 | tf_op jit(solution)/shard_map/attend/pallas_call | solution.py:203
  146.2 13.6 %collective-permute-done.24.refs_2_.refs_0_ = bf16[3,1120,128]{2,1,0:T(8,128)(2,1)S(1)} collective-permute-done((bf16[3,1120,128]{2,1,0:T(8,128)(2,1)}, bf16[3,1120,128]{2,1,0:T(8,128)(2,1)S(1)}, u32[]{:S(2)}, u32[]{:S(2)}) %collective-permute-start.24) | collective-permute-done | bytes 860192 | tf_op jit(solution)/shard_map/ppermute | solution.py:1091
  162.2 3.3 joined.21.near_ref
  165.6 8.2 %place_ffn.2 = (bf16[640,2048]{1,0:T(8,128)(2,1)}, bf16[640,2048]{1,0:T(8,128)(2,1)}, bf16[4,4,128,640]{3,2,1,0:T(8,128)(2,1)}, bf16[4,4,64,640]{3,2,1,0:T(8,128)(2,1)}) custom-call(s32[3]{0:T(128)} %pad_add_fusion.spot, bf16[4,2,1120,128]{3,2,1,0:T(8,128)(2,1)} %bitcast.55, bf16[4,2,1120,128]{3,2,1,0:T(8,128)(2,1)} %bitcast.12.other_ref, ...), custom_call_target="tpu_custom_call" | custom-call | bytes 18000000 | tf_op jit(solution)/shard_map/place_ffn/pallas_call | solution.py:841
  173.8 13.7 %feed_forward.2 = (f32[512,640]{1,0:T(8,128)}, f32[512,640]{1,0:T(8,128)}, bf16[512,2048]{1,0:T(8,128)(2,1)}, bf16[512,2048]{1,0:T(8,128)(2,1)}, f32[512,640]{1,0:T(8,128)}, /*index=5*/bf16[512,640]{1,0:T(8,128)(2,1)}) custom-call(bf16[512,1024]{1,0:T(8,128)(2,1)} %attend.2.o_ref.refs_3_, bf16[512,640]{1,0:T(8,128)(2,1)} %dynamic-slice_bitcast_fusion.1.x_ref, ...), custom_call_target="tpu_custom_call" | custom-call | flops 140928614400 | bytes 22000000 | tf_op jit(solution)/shard_map/feed_forward/pallas_call | solution.py:265
  194.1 3.0 keys_values.3
  199.7 4.8 queries.3
  204.6 10.6 %collective-permute-done.25 = bf16[3,560,128]{2,1,0:T(8,128)(2,1)S(1)} collective-permute-done((bf16[3,560,128]{2,1,0:T(8,128)(2,1)}, bf16[3,560,128]{2,1,0:T(8,128)(2,1)S(1)}, u32[]{:S(2)}, u32[]{:S(2)}) %collective-permute-start.25) | collective-permute-done | bytes 430112 | tf_op jit(solution)/shard_map/ppermute | solution.py:1091
  216.3 6.4 %attend.3.o_ref = bf16[512,1024]{1,0:T(8,128)(2,1)} custom-call(bf16[512,1024]{1,0:T(8,128)(2,1)} %get-tuple-element.124.q_ref.refs_0_, bf16[512,512]{1,0:T(8,128)(2,1)} %copy-done.66, bf16[512,512]{1,0:T(8,128)(2,1)} %get-tuple-element.125.near_ref.refs_4_, s32[512,1]{1,0:T(8,128)} %subtract_add_fusion.low_ref), custom_call_target="tpu_custom_call" | custom-call | flops 40265318400 | bytes 3000000 | tf_op jit(solution)/shard_map/attend/pallas_call | solution.py:203
  223.7 8.2 %place_ffn.3 = (bf16[640,2048]{1,0:T(8,128)(2,1)}, bf16[640,2048]{1,0:T(8,128)(2,1)}, bf16[4,4,128,640]{3,2,1,0:T(8,128)(2,1)}, bf16[4,4,64,640]{3,2,1,0:T(8,128)(2,1)}) custom-call(s32[3]{0:T(128)} %pad_add_fusion.spot, bf16[4,2,1120,128]{3,2,1,0:T(8,128)(2,1)} %bitcast.56, bf16[4,2,1120,128]{3,2,1,0:T(8,128)(2,1)} %bitcast.12.other_ref, ...), custom_call_target="tpu_custom_call" | custom-call | bytes 18000000 | tf_op jit(solution)/shard_map/place_ffn/pallas_call | solution.py:841
  231.9 13.6 %feed_forward.3 = (f32[512,640]{1,0:T(8,128)}, f32[512,640]{1,0:T(8,128)}, bf16[512,2048]{1,0:T(8,128)(2,1)}, bf16[512,2048]{1,0:T(8,128)(2,1)}, f32[512,640]{1,0:T(8,128)}, /*index=5*/bf16[512,640]{1,0:T(8,128)(2,1)}) custom-call(bf16[512,1024]{1,0:T(8,128)(2,1)} %attend.3.o_ref, bf16[512,640]{1,0:T(8,128)(2,1)} %get-tuple-element.122.x_ref.refs_1_, ...), custom_call_target="tpu_custom_call" | custom-call | flops 140928614400 | bytes 22000000 | tf_op jit(solution)/shard_map/feed_forward/pallas_call | solution.py:265
  245.5 26.7 %feed_forward_back.2 = (bf16[4,4,1120,128]{3,2,1,0:T(8,128)(2,1)}, bf16[4,4,1120,128]{3,2,1,0:T(8,128)(2,1)}, f32[512,640]{1,0:T(8,128)}, bf16[512,1024]{1,0:T(8,128)(2,1)}, f32[8,640]{1,0:T(8,128)}) custom-call(s32[3]{0:T(128)} %pad_add_fusion.spot, bf16[512,640]{1,0:T(8,128)(2,1)} %dynamic-slice_bitcast_fusion.c_ref, f32[512,640]{1,0:T(8,128)} %get-tuple-element.130.z_ref, ...), custom_call_target="tpu_custom_call" | custom-call | flops 281857228800 | bytes 35000000 | tf_op jit(solution)/shard_map/feed_forward_back/pallas_call | solution.py:385
  272.7 14.5 %attend_back.2 = (bf16[512,1024]{1,0:T(8,128)(2,1)}, bf16[512,512]{1,0:T(8,128)(2,1)}, f32[512,512]{1,0:T(8,128)}, f32[8,256]{1,0:T(8,128)}) custom-call(bf16[512,1024]{1,0:T(8,128)(2,1)} %get-tuple-element.124.q_ref.refs_0_, bf16[512,1024]{1,0:T(8,128)(2,1)} %get-tuple-element.136.refs_1_, bf16[512,1024]{1,0:T(8,128)(2,1)} %get-tuple-element.137.refs_2_, ...), custom_call_target="tpu_custom_call" | custom-call | flops 100663296000 | bytes 8000000 | tf_op jit(solution)/shard_map/attend_back/pallas_call | solution.py:478
  290.7 7.1 %add_split.3 = (bf16[2,4,560,128]{3,2,1,0:T(8,128)(2,1)}, bf16[2,4,560,128]{3,2,1,0:T(8,128)(2,1)}, bf16[2,4,560,128]{3,2,1,0:T(8,128)(2,1)}, bf16[2,4,560,128]{3,2,1,0:T(8,128)(2,1)}) custom-call(s32[3]{0:T(128)} %pad_add_fusion.spot, bf16[4,4,1120,128]{3,2,1,0:T(8,128)(2,1)} %get-tuple-element.139.first_ref, bf16[4,4,1120,128]{3,2,1,0:T(8,128)(2,1)} %copy-done.5), custom_call_target="tpu_custom_call" | custom-call | bytes 13762560 | tf_op jit(solution)/shard_map/add_split/pallas_call | solution.py:883
  302.8 4.6 queries_back.2
  308.2 6.8 %keys_values_back.2 = (bf16[4,4,512,128]{3,2,1,0:T(8,128)(2,1)}, bf16[512,640]{1,0:T(8,128)(2,1)}) custom-call(bf16[512,640]{1,0:T(8,128)(2,1)} %get-tuple-element.123.a_ref.refs_0_, bf16[512,640]{1,0:T(8,128)(2,1)} %get-tuple-element.122.x_ref.refs_1_, f32[512,640]{1,0:T(8,128)} %get-tuple-element.135.dh_ref, f32[512,640]{1,0:T(8,128)} %get-tuple-element.142.da_ref, ...), custom_call_target="tpu_custom_call" | custom-call | flops 20132659200 | bytes 10000000 | tf_op jit(solution)/shard_map/keys_values_back/pallas_call | solution.py:587
  315.0 26.2 %feed_forward_back.3 = (bf16[4,4,1120,128]{3,2,1,0:T(8,128)(2,1)}, bf16[4,4,1120,128]{3,2,1,0:T(8,128)(2,1)}, f32[512,640]{1,0:T(8,128)}, bf16[512,1024]{1,0:T(8,128)(2,1)}, f32[8,640]{1,0:T(8,128)}) custom-call(s32[3]{0:T(128)} %pad_add_fusion.spot, bf16[512,640]{1,0:T(8,128)(2,1)} %get-tuple-element.149.c_ref, f32[512,640]{1,0:T(8,128)} %get-tuple-element.150.z_ref, ...), custom_call_target="tpu_custom_call" | custom-call | flops 281857228800 | bytes 35000000 | tf_op jit(solution)/shard_map/feed_forward_back/pallas_call | solution.py:385
  344.1 14.7 %attend_back.3 = (bf16[512,1024]{1,0:T(8,128)(2,1)}, bf16[512,512]{1,0:T(8,128)(2,1)}, f32[512,512]{1,0:T(8,128)}, f32[8,256]{1,0:T(8,128)}) custom-call(bf16[512,1024]{1,0:T(8,128)(2,1)} %get-tuple-element.116.q_ref.refs_1_.refs_0_, bf16[512,1024]{1,0:T(8,128)(2,1)} %get-tuple-element.156.refs_1_, bf16[512,1024]{1,0:T(8,128)(2,1)} %get-tuple-element.157.refs_2_, ...), custom_call_target="tpu_custom_call" | custom-call | flops 100663296000 | bytes 8000000 | tf_op jit(solution)/shard_map/attend_back/pallas_call | solution.py:478
  361.1 4.0 sum_parts.3
  367.3 7.0 %add_split.4 = (bf16[2,4,560,128]{3,2,1,0:T(8,128)(2,1)}, bf16[2,4,560,128]{3,2,1,0:T(8,128)(2,1)}, bf16[2,4,560,128]{3,2,1,0:T(8,128)(2,1)}, bf16[2,4,560,128]{3,2,1,0:T(8,128)(2,1)}) custom-call(s32[3]{0:T(128)} %pad_add_fusion.spot, bf16[4,4,1120,128]{3,2,1,0:T(8,128)(2,1)} %get-tuple-element.159.first_ref.refs_0_, bf16[4,4,1120,128]{3,2,1,0:T(8,128)(2,1)} %copy-done.4, ...), custom_call_target="tpu_custom_call" | custom-call | bytes 13762560 | tf_op jit(solution)/shard_map/add_split/pallas_call | solution.py:883
  374.3 4.6 queries_back.3
  379.7 6.8 %keys_values_back.3 = (bf16[4,4,512,128]{3,2,1,0:T(8,128)(2,1)}, bf16[512,640]{1,0:T(8,128)(2,1)}) custom-call(bf16[512,640]{1,0:T(8,128)(2,1)} %get-tuple-element.115.a_ref.refs_0_, bf16[512,640]{1,0:T(8,128)(2,1)} %dynamic-slice_bitcast_fusion.1.x_ref, f32[512,640]{1,0:T(8,128)} %get-tuple-element.155.dh_ref, f32[512,640]{1,0:T(8,128)} %get-tuple-element.168.da_ref, ...), custom_call_target="tpu_custom_call" | custom-call | flops 20132659200 | bytes 10000000 | tf_op jit(solution)/shard_map/keys_values_back/pallas_call | solution.py:587
  386.5 3.3 broadcast_select_fusion
  394.5 23.9 %collective-permute-done.38.b_ref.a1 = bf16[2,4,560,128]{3,2,1,0:T(8,128)(2,1)S(1)} collective-permute-done((bf16[2,4,560,128]{3,2,1,0:T(8,128)(2,1)S(1)}, bf16[2,4,560,128]{3,2,1,0:T(8,128)(2,1)S(1)}, u32[]{:S(2)}, u32[]{:S(2)}) %collective-permute-start.38) | collective-permute-done | bytes 1146912 | tf_op jit(solution)/shard_map/ppermute | solution.py:1091
  428.3 5.1 add_split.5
  436.4 3.5 collective-permute-done.40.a2
  444.4 4.0 sum_parts.4
  448.4 3.0 collective-permute-done.46.b_ref.a1
  458.1 16.0 %collective-permute-done.57 = bf16[1120,128]{1,0:T(8,128)(2,1)S(1)} collective-permute-done((bf16[1120,128]{1,0:T(8,128)(2,1)S(1)}, bf16[1120,128]{1,0:T(8,128)(2,1)S(1)}, u32[]{:S(2)}, u32[]{:S(2)}) %collective-permute-start.57) | collective-permute-done | bytes 286752 | tf_op jit(solution)/shard_map/ppermute | solution.py:1091
  486.4 6.3 %collective-permute-start.50 = (bf16[512,128]{1,0:T(8,128)(2,1)}, bf16[512,128]{1,0:T(8,128)(2,1)S(1)}, u32[]{:S(2)}, u32[]{:S(2)}) collective-permute-start(bf16[512,128]{1,0:T(8,128)(2,1)} %get-tuple-element.195), channel_id=1, source_target_pairs={{0,4},{1,5},{2,6},{3,7},{4,0},{5,1},{6,2},{7,3},{8,12},{9,13},{10,... | collective-permute-start | bytes 393224 | tf_op jit(solution)/shard_map/ppermute | solution.py:1091
  495.9 5.6 %collective-permute-done.51 = bf16[512,128]{1,0:T(8,128)(2,1)S(1)} collective-permute-done((bf16[512,128]{1,0:T(8,128)(2,1)}, bf16[512,128]{1,0:T(8,128)(2,1)S(1)}, u32[]{:S(2)}, u32[]{:S(2)}) %collective-permute-start.51) | collective-permute-done | bytes 131104 | tf_op jit(solution)/shard_map/ppermute | solution.py:1091
  506.4 17.7 %collective-permute-done.61.refs_7_ = bf16[1120,128]{1,0:T(8,128)(2,1)S(1)} collective-permute-done((bf16[1120,128]{1,0:T(8,128)(2,1)S(1)}, bf16[1120,128]{1,0:T(8,128)(2,1)S(1)}, u32[]{:S(2)}, u32[]{:S(2)}) %collective-permute-start.61) | collective-permute-done | bytes 286752 | tf_op jit(solution)/shard_map/ppermute | solution.py:1091
  525.9 3.5 choose_ring.1
  534.4 5.8 %finish.1 = (f32[1,160,2048]{2,1,0:T(8,128)}, f32[1,160,2048]{2,1,0:T(8,128)}, f32[1,512,640]{2,1,0:T(8,128)}, f32[1,256,640]{2,1,0:T(8,128)}, f32[1,160,1536]{2,1,0:T(8,128)}, /*index=5*/f32[4,32,128]{2,1,0:T(8,128)}) custom-call(s32[3]{0:T(128)} %pad_add_fusion.spot, bf16[1632,128]{1,0:T(8,128)(2,1)} %copy-done.8, bf16[1632,128]{1,0:T(8,128)(2,1)} %copy-done.21, ...), custom_call_target="tpu_custom_call" | custom-call | bytes 12000000 | tf_op jit(solution)/shard_map/finish/pallas_call | solution.py:1022
  (335 shorter events, 164.5 us)
Async XLA Ops:
  12.0 13.1 %collective-permute-start.1 = (bf16[1,512,128]{2,1,0:T(8,128)(2,1)}, bf16[1,512,128]{2,1,0:T(8,128)(2,1)S(1)}, u32[]{:S(2)}, u32[]{:S(2)}) collective-permute-start(bf16[1,512,128]{2,1,0:T(8,128)(2,1)} %get-tuple-element.112), channel_id=1, source_target_pairs={{0,8},{1,9},{2,10},{3,11},{4,12},{5,13},{6,14},{7,15},{8,0},{9,1},... | collective-permute-start | bytes 393224 | tf_op jit(solution)/shard_map/ppermute | solution.py:1091
  56.6 16.5 %collective-permute-start.10 = (bf16[1,1120,128]{2,1,0:T(8,128)(2,1)S(1)}, bf16[1,1120,128]{2,1,0:T(8,128)(2,1)S(1)}, u32[]{:S(2)}, u32[]{:S(2)}) collective-permute-start(bf16[1,1120,128]{2,1,0:T(8,128)(2,1)S(1)} %copy-done.29), channel_id=1, source_target_pairs={{0,4},{1,5},{2,6},{3,7},{4,0},{5,1},{6,2},{7,3},{8,12},{9,13},{10,... | collective-permute-start | bytes 860168 | tf_op jit(solution)/shard_map/ppermute | solution.py:1091
  59.8 22.9 %collective-permute-start.11 = (bf16[1,1120,128]{2,1,0:T(8,128)(2,1)S(1)}, bf16[1,1120,128]{2,1,0:T(8,128)(2,1)S(1)}, u32[]{:S(2)}, u32[]{:S(2)}) collective-permute-start(bf16[1,1120,128]{2,1,0:T(8,128)(2,1)S(1)} %copy-done.29), channel_id=1, source_target_pairs={{0,8},{1,9},{2,10},{3,11},{4,12},{5,13},{6,14},{7,15},{8,0},{9,1},... | collective-permute-start | bytes 860168 | tf_op jit(solution)/shard_map/ppermute | solution.py:1091
  60.8 21.9 %collective-permute-start.12 = (bf16[1,1120,128]{2,1,0:T(8,128)(2,1)S(1)}, bf16[1,1120,128]{2,1,0:T(8,128)(2,1)S(1)}, u32[]{:S(2)}, u32[]{:S(2)}) collective-permute-start(bf16[1,1120,128]{2,1,0:T(8,128)(2,1)S(1)} %copy-done.29), channel_id=1, source_target_pairs={{0,12},{1,13},{2,14},{3,15},{4,8},{5,9},{6,10},{7,11},{8,4},{9,5},... | collective-permute-start | bytes 860168 | tf_op jit(solution)/shard_map/ppermute | solution.py:1091
  88.2 37.6 %collective-permute-start.20 = (bf16[1,1120,128]{2,1,0:T(8,128)(2,1)}, bf16[1,1120,128]{2,1,0:T(8,128)(2,1)S(1)}, u32[]{:S(2)}, u32[]{:S(2)}) collective-permute-start(bf16[1,1120,128]{2,1,0:T(8,128)(2,1)} %half_quarter.3), channel_id=1, source_target_pairs={{0,4},{1,5},{2,6},{3,7},{4,0},{5,1},{6,2},{7,3},{8,12},{9,13},{10,... | collective-permute-start | bytes 860168 | tf_op jit(solution)/shard_map/ppermute | solution.py:1091
  94.1 41.3 %collective-permute-start.21 = (bf16[1,1120,128]{2,1,0:T(8,128)(2,1)}, bf16[1,1120,128]{2,1,0:T(8,128)(2,1)}, u32[]{:S(2)}, u32[]{:S(2)}) collective-permute-start(bf16[1,1120,128]{2,1,0:T(8,128)(2,1)} %half_quarter.3), channel_id=1, source_target_pairs={{0,8},{1,9},{2,10},{3,11},{4,12},{5,13},{6,14},{7,15},{8,0},{9,1},... | collective-permute-start | bytes 860168 | tf_op jit(solution)/shard_map/ppermute | solution.py:1091
  95.3 20.2 %collective-permute-start.14 = (bf16[3,1120,128]{2,1,0:T(8,128)(2,1)S(1)}, bf16[3,1120,128]{2,1,0:T(8,128)(2,1)S(1)}, u32[]{:S(2)}, u32[]{:S(2)}) collective-permute-start(bf16[3,1120,128]{2,1,0:T(8,128)(2,1)S(1)} %copy-done.2), channel_id=1, source_target_pairs={{0,2},{1,3},{2,0},{3,1},{4,6},{5,7},{6,4},{7,5},{8,10},{9,11},{10,... | collective-permute-start | bytes 2580488 | tf_op jit(solution)/shard_map/ppermute | solution.py:1091
  95.8 23.1 %collective-permute-start.13 = (bf16[3,1120,128]{2,1,0:T(8,128)(2,1)S(1)}, bf16[3,1120,128]{2,1,0:T(8,128)(2,1)S(1)}, u32[]{:S(2)}, u32[]{:S(2)}) collective-permute-start(bf16[3,1120,128]{2,1,0:T(8,128)(2,1)S(1)} %copy-done.2), channel_id=1, source_target_pairs={{0,1},{1,0},{2,3},{3,2},{4,5},{5,4},{6,7},{7,6},{8,9},{9,8},{10,11... | collective-permute-start | bytes 2580488 | tf_op jit(solution)/shard_map/ppermute | solution.py:1091
  102.5 25.7 %collective-permute-start.9 = (bf16[512,512]{1,0:T(8,128)(2,1)}, bf16[512,512]{1,0:T(8,128)(2,1)S(1)}, u32[]{:S(2)}, u32[]{:S(2)}) collective-permute-start(bf16[512,512]{1,0:T(8,128)(2,1)} %get-tuple-element.117.near_ref.refs_4_), channel_id=1, source_target_pairs={{0,1},{1,2},{2,3},{4,5},{5,6},{6,7},{8,9},{9,10},{10,11},{12,13},{... | collective-permute-start | bytes 1572872 | tf_op jit(solution)/shard_map/ppermute | solution.py:1101
  115.5 20.0 %collective-permute-start.22 = (bf16[1,1120,128]{2,1,0:T(8,128)(2,1)S(1)}, bf16[1,1120,128]{2,1,0:T(8,128)(2,1)S(1)}, u32[]{:S(2)}, u32[]{:S(2)}) collective-permute-start(bf16[1,1120,128]{2,1,0:T(8,128)(2,1)S(1)} %copy-done.41), channel_id=1, source_target_pairs={{0,12},{1,13},{2,14},{3,15},{4,8},{5,9},{6,10},{7,11},{8,4},{9,5},... | collective-permute-start | bytes 860168 | tf_op jit(solution)/shard_map/ppermute | solution.py:1091
  118.9 23.3 %collective-permute-start.16 = (bf16[3,560,128]{2,1,0:T(8,128)(2,1)}, bf16[3,560,128]{2,1,0:T(8,128)(2,1)S(1)}, u32[]{:S(2)}, u32[]{:S(2)}) collective-permute-start(bf16[3,560,128]{2,1,0:T(8,128)(2,1)} %joined.19), channel_id=1, source_target_pairs={{0,1},{1,0},{2,3},{3,2},{4,5},{5,4},{6,7},{7,6},{8,9},{9,8},{10,11... | collective-permute-start | bytes 1290248 | tf_op jit(solution)/shard_map/ppermute | solution.py:1091
  125.8 16.4 %collective-permute-start.15 = (bf16[3,560,128]{2,1,0:T(8,128)(2,1)S(1)}, bf16[3,560,128]{2,1,0:T(8,128)(2,1)S(1)}, u32[]{:S(2)}, u32[]{:S(2)}) collective-permute-start(bf16[3,560,128]{2,1,0:T(8,128)(2,1)S(1)} %copy-done.40), channel_id=1, source_target_pairs={{0,2},{1,3},{2,0},{3,1},{4,6},{5,7},{6,4},{7,5},{8,10},{9,11},{10,... | collective-permute-start | bytes 1290248 | tf_op jit(solution)/shard_map/ppermute | solution.py:1091
  128.2 37.4 %collective-permute-start.17 = (bf16[9,1120,128]{2,1,0:T(8,128)(2,1)}, bf16[9,1120,128]{2,1,0:T(8,128)(2,1)}, u32[]{:S(2)}, u32[]{:S(2)}) collective-permute-start(bf16[9,1120,128]{2,1,0:T(8,128)(2,1)} %joined.17.near_ref), channel_id=1, source_target_pairs={{0,16},{16,0},{1,17},{17,1},{2,18},{18,2},{3,19},{19,3},{4,20},{20... | collective-permute-start | bytes 7741448 | tf_op jit(solution)/shard_map/ppermute | solution.py:1095
  138.2 21.6 %collective-permute-start.24 = (bf16[3,1120,128]{2,1,0:T(8,128)(2,1)}, bf16[3,1120,128]{2,1,0:T(8,128)(2,1)S(1)}, u32[]{:S(2)}, u32[]{:S(2)}) collective-permute-start(bf16[3,1120,128]{2,1,0:T(8,128)(2,1)} %joined.20.refs_0_), channel_id=1, source_target_pairs={{0,2},{1,3},{2,0},{3,1},{4,6},{5,7},{6,4},{7,5},{8,10},{9,11},{10,... | collective-permute-start | bytes 2580488 | tf_op jit(solution)/shard_map/ppermute | solution.py:1091
  140.6 20.7 %collective-permute-start.23 = (bf16[3,1120,128]{2,1,0:T(8,128)(2,1)}, bf16[3,1120,128]{2,1,0:T(8,128)(2,1)S(1)}, u32[]{:S(2)}, u32[]{:S(2)}) collective-permute-start(bf16[3,1120,128]{2,1,0:T(8,128)(2,1)} %joined.20.refs_0_), channel_id=1, source_target_pairs={{0,1},{1,0},{2,3},{3,2},{4,5},{5,4},{6,7},{7,6},{8,9},{9,8},{10,11... | collective-permute-start | bytes 2580488 | tf_op jit(solution)/shard_map/ppermute | solution.py:1091
  142.3 23.3 %collective-permute-start.18 = (bf16[3,1120,128]{2,1,0:T(8,128)(2,1)S(1)}, bf16[3,1120,128]{2,1,0:T(8,128)(2,1)}, u32[]{:S(2)}, u32[]{:S(2)}) collective-permute-start(bf16[3,1120,128]{2,1,0:T(8,128)(2,1)S(1)} %constant_dynamic-update-slice_fusion.far_ref), channel_id=1, source_target_pairs={{0,16},{16,0},{1,17},{17,1},{2,18},{18,2},{3,19},{19,3},{4,20},{20... | collective-permute-start | bytes 2580488 | tf_op jit(solution)/shard_map/ppermute | solution.py:1095
  165.6 57.2 %collective-permute-start.27 = (bf16[9,1120,128]{2,1,0:T(8,128)(2,1)}, bf16[9,1120,128]{2,1,0:T(8,128)(2,1)}, u32[]{:S(2)}, u32[]{:S(2)}) collective-permute-start(bf16[9,1120,128]{2,1,0:T(8,128)(2,1)} %joined.21.near_ref), channel_id=1, source_target_pairs={{0,16},{16,0},{1,17},{17,1},{2,18},{18,2},{3,19},{19,3},{4,20},{20... | collective-permute-start | bytes 7741448 | tf_op jit(solution)/shard_map/ppermute | solution.py:1095
  189.4 25.8 %collective-permute-start.26 = (bf16[3,560,128]{2,1,0:T(8,128)(2,1)}, bf16[3,560,128]{2,1,0:T(8,128)(2,1)S(1)}, u32[]{:S(2)}, u32[]{:S(2)}) collective-permute-start(bf16[3,560,128]{2,1,0:T(8,128)(2,1)} %joined.23), channel_id=1, source_target_pairs={{0,1},{1,0},{2,3},{3,2},{4,5},{5,4},{6,7},{7,6},{8,9},{9,8},{10,11... | collective-permute-start | bytes 1290248 | tf_op jit(solution)/shard_map/ppermute | solution.py:1091
  192.9 22.3 %collective-permute-start.25 = (bf16[3,560,128]{2,1,0:T(8,128)(2,1)}, bf16[3,560,128]{2,1,0:T(8,128)(2,1)S(1)}, u32[]{:S(2)}, u32[]{:S(2)}) collective-permute-start(bf16[3,560,128]{2,1,0:T(8,128)(2,1)} %joined.22), channel_id=1, source_target_pairs={{0,2},{1,3},{2,0},{3,1},{4,6},{5,7},{6,4},{7,5},{8,10},{9,11},{10,... | collective-permute-start | bytes 1290248 | tf_op jit(solution)/shard_map/ppermute | solution.py:1091
  197.1 18.3 %collective-permute-start.19 = (bf16[512,512]{1,0:T(8,128)(2,1)}, bf16[512,512]{1,0:T(8,128)(2,1)S(1)}, u32[]{:S(2)}, u32[]{:S(2)}) collective-permute-start(bf16[512,512]{1,0:T(8,128)(2,1)} %get-tuple-element.125.near_ref.refs_4_), channel_id=1, source_target_pairs={{0,1},{1,2},{2,3},{4,5},{5,6},{6,7},{8,9},{9,10},{10,11},{12,13},{... | collective-permute-start | bytes 1572872 | tf_op jit(solution)/shard_map/ppermute | solution.py:1101
  272.3 16.2 %collective-permute-start.29 = (bf16[4,4,1120,128]{3,2,1,0:T(8,128)(2,1)}, bf16[4,4,1120,128]{3,2,1,0:T(8,128)(2,1)S(1)}, u32[]{:S(2)}, u32[]{:S(2)}) collective-permute-start(bf16[4,4,1120,128]{3,2,1,0:T(8,128)(2,1)} %get-tuple-element.140), channel_id=1, source_target_pairs={{0,16},{16,0},{1,17},{17,1},{2,18},{18,2},{3,19},{19,3},{4,20},{20... | collective-permute-start | bytes 13762568 | tf_op jit(solution)/shard_map/ppermute | solution.py:1095
  287.2 20.2 %collective-permute-start.30 = (bf16[512,512]{1,0:T(8,128)(2,1)}, bf16[512,512]{1,0:T(8,128)(2,1)S(1)}, u32[]{:S(2)}, u32[]{:S(2)}) collective-permute-start(bf16[512,512]{1,0:T(8,128)(2,1)} %get-tuple-element.144), channel_id=1, source_target_pairs={{1,0},{2,1},{3,2},{5,4},{6,5},{7,6},{9,8},{10,9},{11,10},{13,12},{... | collective-permute-start | bytes 1572872 | tf_op jit(solution)/shard_map/ppermute | solution.py:1101
  297.8 43.5 %collective-permute-start.32 = (bf16[2,4,560,128]{3,2,1,0:T(8,128)(2,1)}, bf16[2,4,560,128]{3,2,1,0:T(8,128)(2,1)}, u32[]{:S(2)}, u32[]{:S(2)}) collective-permute-start(bf16[2,4,560,128]{3,2,1,0:T(8,128)(2,1)} %get-tuple-element.162), channel_id=1, source_target_pairs={{0,1},{1,0},{2,3},{3,2},{4,5},{5,4},{6,7},{7,6},{8,9},{9,8},{10,11... | collective-permute-start | bytes 3440648 | tf_op jit(solution)/shard_map/ppermute | solution.py:1091
  300.4 40.9 %collective-permute-start.33 = (bf16[2,4,560,128]{3,2,1,0:T(8,128)(2,1)}, bf16[2,4,560,128]{3,2,1,0:T(8,128)(2,1)}, u32[]{:S(2)}, u32[]{:S(2)}) collective-permute-start(bf16[2,4,560,128]{3,2,1,0:T(8,128)(2,1)} %get-tuple-element.164), channel_id=1, source_target_pairs={{0,2},{1,3},{2,0},{3,1},{4,6},{5,7},{6,4},{7,5},{8,10},{9,11},{10,... | collective-permute-start | bytes 3440648 | tf_op jit(solution)/shard_map/ppermute | solution.py:1091
  341.2 23.9 %collective-permute-start.31 = (bf16[4,4,1120,128]{3,2,1,0:T(8,128)(2,1)}, bf16[4,4,1120,128]{3,2,1,0:T(8,128)(2,1)S(1)}, u32[]{:S(2)}, u32[]{:S(2)}) collective-permute-start(bf16[4,4,1120,128]{3,2,1,0:T(8,128)(2,1)} %get-tuple-element.160), channel_id=1, source_target_pairs={{0,16},{16,0},{1,17},{17,1},{2,18},{18,2},{3,19},{19,3},{4,20},{20... | collective-permute-start | bytes 13762568 | tf_op jit(solution)/shard_map/ppermute | solution.py:1095
  344.0 16.1 %collective-permute-start.34 = (bf16[4,560,128]{2,1,0:T(8,128)(2,1)}, bf16[4,560,128]{2,1,0:T(8,128)(2,1)S(1)}, u32[]{:S(2)}, u32[]{:S(2)}) collective-permute-start(bf16[4,560,128]{2,1,0:T(8,128)(2,1)} %get-tuple-element.165), channel_id=1, source_target_pairs={{0,2},{1,3},{2,0},{3,1},{4,6},{5,7},{6,4},{7,5},{8,10},{9,11},{10,... | collective-permute-start | bytes 1720328 | tf_op jit(solution)/shard_map/ppermute | solution.py:1091
  344.0 16.1 %collective-permute-start.35 = (bf16[4,560,128]{2,1,0:T(8,128)(2,1)}, bf16[4,560,128]{2,1,0:T(8,128)(2,1)S(1)}, u32[]{:S(2)}, u32[]{:S(2)}) collective-permute-start(bf16[4,560,128]{2,1,0:T(8,128)(2,1)} %get-tuple-element.166), channel_id=1, source_target_pairs={{0,1},{1,0},{2,3},{3,2},{4,5},{5,4},{6,7},{7,6},{8,9},{9,8},{10,11... | collective-permute-start | bytes 1720328 | tf_op jit(solution)/shard_map/ppermute | solution.py:1091
  358.8 20.1 %collective-permute-start.36 = (bf16[512,512]{1,0:T(8,128)(2,1)}, bf16[512,512]{1,0:T(8,128)(2,1)S(1)}, u32[]{:S(2)}, u32[]{:S(2)}) collective-permute-start(bf16[512,512]{1,0:T(8,128)(2,1)} %get-tuple-element.170), channel_id=1, source_target_pairs={{1,0},{2,1},{3,2},{5,4},{6,5},{7,6},{9,8},{10,9},{11,10},{13,12},{... | collective-permute-start | bytes 1572872 | tf_op jit(solution)/shard_map/ppermute | solution.py:1101
  389.8 37.2 %collective-permute-start.45 = (bf16[4,4,512,128]{3,2,1,0:T(8,128)(2,1)S(1)}, bf16[4,4,512,128]{3,2,1,0:T(8,128)(2,1)S(1)}, u32[]{:S(2)}, u32[]{:S(2)}) collective-permute-start(bf16[4,4,512,128]{3,2,1,0:T(8,128)(2,1)S(1)} %get-tuple-element.267), channel_id=1, source_target_pairs={{0,16},{16,0},{1,17},{17,1},{2,18},{18,2},{3,19},{19,3},{4,20},{20... | collective-permute-start | bytes 6291464 | tf_op jit(solution)/shard_map/ppermute | solution.py:1095
  390.3 28.1 %collective-permute-start.38 = (bf16[2,4,560,128]{3,2,1,0:T(8,128)(2,1)S(1)}, bf16[2,4,560,128]{3,2,1,0:T(8,128)(2,1)S(1)}, u32[]{:S(2)}, u32[]{:S(2)}) collective-permute-start(bf16[2,4,560,128]{3,2,1,0:T(8,128)(2,1)S(1)} %copy-done.64), channel_id=1, source_target_pairs={{0,1},{1,0},{2,3},{3,2},{4,5},{5,4},{6,7},{7,6},{8,9},{9,8},{10,11... | collective-permute-start | bytes 3440648 | tf_op jit(solution)/shard_map/ppermute | solution.py:1091
  392.6 27.5 %collective-permute-start.39 = (bf16[2,4,560,128]{3,2,1,0:T(8,128)(2,1)S(1)}, bf16[2,4,560,128]{3,2,1,0:T(8,128)(2,1)S(1)}, u32[]{:S(2)}, u32[]{:S(2)}) collective-permute-start(bf16[2,4,560,128]{3,2,1,0:T(8,128)(2,1)S(1)} %copy-done.63), channel_id=1, source_target_pairs={{0,2},{1,3},{2,0},{3,1},{4,6},{5,7},{6,4},{7,5},{8,10},{9,11},{10,... | collective-permute-start | bytes 3440648 | tf_op jit(solution)/shard_map/ppermute | solution.py:1091
  423.9 16.1 %collective-permute-start.40 = (bf16[4,560,128]{2,1,0:T(8,128)(2,1)}, bf16[4,560,128]{2,1,0:T(8,128)(2,1)S(1)}, u32[]{:S(2)}, u32[]{:S(2)}) collective-permute-start(bf16[4,560,128]{2,1,0:T(8,128)(2,1)} %get-tuple-element.180), channel_id=1, source_target_pairs={{0,2},{1,3},{2,0},{3,1},{4,6},{5,7},{6,4},{7,5},{8,10},{9,11},{10,... | collective-permute-start | bytes 1720328 | tf_op jit(solution)/shard_map/ppermute | solution.py:1091
  425.6 16.3 %collective-permute-start.41 = (bf16[4,560,128]{2,1,0:T(8,128)(2,1)}, bf16[4,560,128]{2,1,0:T(8,128)(2,1)S(1)}, u32[]{:S(2)}, u32[]{:S(2)}) collective-permute-start(bf16[4,560,128]{2,1,0:T(8,128)(2,1)} %get-tuple-element.181), channel_id=1, source_target_pairs={{0,1},{1,0},{2,3},{3,2},{4,5},{5,4},{6,7},{7,6},{8,9},{9,8},{10,11... | collective-permute-start | bytes 1720328 | tf_op jit(solution)/shard_map/ppermute | solution.py:1091
  433.5 17.9 %collective-permute-start.46 = (bf16[2,4,256,128]{3,2,1,0:T(8,128)(2,1)}, bf16[2,4,256,128]{3,2,1,0:T(8,128)(2,1)S(1)}, u32[]{:S(2)}, u32[]{:S(2)}) collective-permute-start(bf16[2,4,256,128]{3,2,1,0:T(8,128)(2,1)} %get-tuple-element.189), channel_id=1, source_target_pairs={{0,1},{1,0},{2,3},{3,2},{4,5},{5,4},{6,7},{7,6},{8,9},{9,8},{10,11... | collective-permute-start | bytes 1572872 | tf_op jit(solution)/shard_map/ppermute | solution.py:1091
  434.1 19.3 %collective-permute-start.47 = (bf16[2,4,256,128]{3,2,1,0:T(8,128)(2,1)}, bf16[2,4,256,128]{3,2,1,0:T(8,128)(2,1)S(1)}, u32[]{:S(2)}, u32[]{:S(2)}) collective-permute-start(bf16[2,4,256,128]{3,2,1,0:T(8,128)(2,1)} %get-tuple-element.191), channel_id=1, source_target_pairs={{0,2},{1,3},{2,0},{3,1},{4,6},{5,7},{6,4},{7,5},{8,10},{9,11},{10,... | collective-permute-start | bytes 1572872 | tf_op jit(solution)/shard_map/ppermute | solution.py:1091
  434.4 22.0 %collective-permute-start.56 = (bf16[1120,128]{1,0:T(8,128)(2,1)S(1)}, bf16[1120,128]{1,0:T(8,128)(2,1)S(1)}, u32[]{:S(2)}, u32[]{:S(2)}) collective-permute-start(bf16[1120,128]{1,0:T(8,128)(2,1)S(1)} %copy-done.71), channel_id=1, source_target_pairs={{0,4},{1,5},{2,6},{3,7},{4,0},{5,1},{6,2},{7,3},{8,12},{9,13},{10,... | collective-permute-start | bytes 860168 | tf_op jit(solution)/shard_map/ppermute | solution.py:1091
  440.0 34.1 %collective-permute-start.57 = (bf16[1120,128]{1,0:T(8,128)(2,1)S(1)}, bf16[1120,128]{1,0:T(8,128)(2,1)S(1)}, u32[]{:S(2)}, u32[]{:S(2)}) collective-permute-start(bf16[1120,128]{1,0:T(8,128)(2,1)S(1)} %copy-done.70), channel_id=1, source_target_pairs={{0,8},{1,9},{2,10},{3,11},{4,12},{5,13},{6,14},{7,15},{8,0},{9,1},... | collective-permute-start | bytes 860168 | tf_op jit(solution)/shard_map/ppermute | solution.py:1091
  441.9 33.9 %collective-permute-start.58 = (bf16[1120,128]{1,0:T(8,128)(2,1)S(1)}, bf16[1120,128]{1,0:T(8,128)(2,1)S(1)}, u32[]{:S(2)}, u32[]{:S(2)}) collective-permute-start(bf16[1120,128]{1,0:T(8,128)(2,1)S(1)} %copy-done.69), channel_id=1, source_target_pairs={{0,12},{1,13},{2,14},{3,15},{4,8},{5,9},{6,10},{7,11},{8,4},{9,5},... | collective-permute-start | bytes 860168 | tf_op jit(solution)/shard_map/ppermute | solution.py:1091
  451.4 35.0 %collective-permute-start.42 = (bf16[1120,128]{1,0:T(8,128)(2,1)}, bf16[1120,128]{1,0:T(8,128)(2,1)S(1)}, u32[]{:S(2)}, u32[]{:S(2)}) collective-permute-start(bf16[1120,128]{1,0:T(8,128)(2,1)} %get-tuple-element.183), channel_id=1, source_target_pairs={{0,4},{1,5},{2,6},{3,7},{4,0},{5,1},{6,2},{7,3},{8,12},{9,13},{10,... | collective-permute-start | bytes 860168 | tf_op jit(solution)/shard_map/ppermute | solution.py:1091
  453.4 39.2 %collective-permute-start.43 = (bf16[1120,128]{1,0:T(8,128)(2,1)}, bf16[1120,128]{1,0:T(8,128)(2,1)S(1)}, u32[]{:S(2)}, u32[]{:S(2)}) collective-permute-start(bf16[1120,128]{1,0:T(8,128)(2,1)} %get-tuple-element.184), channel_id=1, source_target_pairs={{0,8},{1,9},{2,10},{3,11},{4,12},{5,13},{6,14},{7,15},{8,0},{9,1},... | collective-permute-start | bytes 860168 | tf_op jit(solution)/shard_map/ppermute | solution.py:1091
  456.4 36.6 %collective-permute-start.44 = (bf16[1120,128]{1,0:T(8,128)(2,1)}, bf16[1120,128]{1,0:T(8,128)(2,1)S(1)}, u32[]{:S(2)}, u32[]{:S(2)}) collective-permute-start(bf16[1120,128]{1,0:T(8,128)(2,1)} %get-tuple-element.185), channel_id=1, source_target_pairs={{0,12},{1,13},{2,14},{3,15},{4,8},{5,9},{6,10},{7,11},{8,4},{9,5},... | collective-permute-start | bytes 860168 | tf_op jit(solution)/shard_map/ppermute | solution.py:1091
  480.7 22.7 %collective-permute-start.59 = (bf16[1120,128]{1,0:T(8,128)(2,1)S(1)}, bf16[1120,128]{1,0:T(8,128)(2,1)S(1)}, u32[]{:S(2)}, u32[]{:S(2)}) collective-permute-start(bf16[1120,128]{1,0:T(8,128)(2,1)S(1)} %add_convert_fusion.refs_4_), channel_id=1, source_target_pairs={{0,1},{1,0},{2,3},{3,2},{4,5},{5,4},{6,7},{7,6},{8,9},{9,8},{10,11... | collective-permute-start | bytes 860168 | tf_op jit(solution)/shard_map/ppermute | solution.py:1091
  482.4 22.8 %collective-permute-start.60 = (bf16[1120,128]{1,0:T(8,128)(2,1)S(1)}, bf16[1120,128]{1,0:T(8,128)(2,1)S(1)}, u32[]{:S(2)}, u32[]{:S(2)}) collective-permute-start(bf16[1120,128]{1,0:T(8,128)(2,1)S(1)} %add_convert_fusion.refs_4_), channel_id=1, source_target_pairs={{0,2},{1,3},{2,0},{3,1},{4,6},{5,7},{6,4},{7,5},{8,10},{9,11},{10,... | collective-permute-start | bytes 860168 | tf_op jit(solution)/shard_map/ppermute | solution.py:1091
  495.9 33.5 %collective-permute-start.37 = (bf16[2,512,640]{2,1,0:T(8,128)(2,1)}, bf16[2,512,640]{2,1,0:T(8,128)(2,1)}, u32[]{:S(2)}, u32[]{:S(2)}) collective-permute-start(bf16[2,512,640]{2,1,0:T(8,128)(2,1)} %get-tuple-element.274), channel_id=1, source_target_pairs={{0,16},{16,0},{1,17},{17,1},{2,18},{18,2},{3,19},{19,3},{4,20},{20... | collective-permute-start | bytes 3932168 | tf_op jit(solution)/shard_map/ppermute | solution.py:1095
  501.7 22.4 %collective-permute-start.53 = (bf16[1632,128]{1,0:T(8,128)(2,1)S(1)}, bf16[1632,128]{1,0:T(8,128)(2,1)S(1)}, u32[]{:S(2)}, u32[]{:S(2)}) collective-permute-start(bf16[1632,128]{1,0:T(8,128)(2,1)S(1)} %pad_maximum_fusion.2.refs_0_), channel_id=1, source_target_pairs={{0,1},{1,0},{2,3},{3,2},{4,5},{5,4},{6,7},{7,6},{8,9},{9,8},{10,11... | collective-permute-start | bytes 1253384 | tf_op jit(solution)/shard_map/ppermute | solution.py:1091
  502.2 21.9 %collective-permute-start.54 = (bf16[1632,128]{1,0:T(8,128)(2,1)S(1)}, bf16[1632,128]{1,0:T(8,128)(2,1)S(1)}, u32[]{:S(2)}, u32[]{:S(2)}) collective-permute-start(bf16[1632,128]{1,0:T(8,128)(2,1)S(1)} %pad_maximum_fusion.2.refs_0_), channel_id=1, source_target_pairs={{0,2},{1,3},{2,0},{3,1},{4,6},{5,7},{6,4},{7,5},{8,10},{9,11},{10,... | collective-permute-start | bytes 1253384 | tf_op jit(solution)/shard_map/ppermute | solution.py:1091
  503.4 20.7 %collective-permute-start.55 = (bf16[1632,128]{1,0:T(8,128)(2,1)S(1)}, bf16[1632,128]{1,0:T(8,128)(2,1)S(1)}, u32[]{:S(2)}, u32[]{:S(2)}) collective-permute-start(bf16[1632,128]{1,0:T(8,128)(2,1)S(1)} %pad_maximum_fusion.2.refs_0_), channel_id=1, source_target_pairs={{0,3},{1,2},{2,1},{3,0},{4,7},{5,6},{6,5},{7,4},{8,11},{9,10},{10,... | collective-permute-start | bytes 1253384 | tf_op jit(solution)/shard_map/ppermute | solution.py:1091
  505.2 18.8 %collective-permute-start.61 = (bf16[1120,128]{1,0:T(8,128)(2,1)S(1)}, bf16[1120,128]{1,0:T(8,128)(2,1)S(1)}, u32[]{:S(2)}, u32[]{:S(2)}) collective-permute-start(bf16[1120,128]{1,0:T(8,128)(2,1)S(1)} %add_convert_fusion.refs_4_), channel_id=1, source_target_pairs={{0,3},{1,2},{2,1},{3,0},{4,7},{5,6},{6,5},{7,4},{8,11},{9,10},{10,... | collective-permute-start | bytes 860168 | tf_op jit(solution)/shard_map/ppermute | solution.py:1091
  (87 other events, 647.7 us)

commit v3 on v2

--- a/solution.py
+++ b/solution.py
@@ -198,24 +198,25 @@
         o_ref[:, h * HD : (h + 1) * HD] = (dot(e.astype(B16), vals) / total).astype(B16)
 
 
-def attn_call(q, far, near, low):
+def attn_call(q, far, near, low, *deps):
     tok, q_width = q.shape
     return pl.pallas_call(
-        attn_kernel,
+        held_back(attn_kernel, 4, len(deps)),
         grid=(tok // QB,),
         in_specs=[
             pl.BlockSpec((QB, q_width), lambda b: (b, 0)),
             whole(far.shape),
             whole(near.shape),
             pl.BlockSpec((QB, 1), lambda b: (b, 0)),
-        ],
+        ]
+        + [pl.BlockSpec(memory_space=pl.ANY)] * len(deps),
         out_specs=pl.BlockSpec((QB, q_width), lambda b: (b, 0)),
         out_shape=sds((tok, q_width), B16),
         scratch_shapes=[pltpu.VMEM((WINDOW + tok, 2 * HD), B16)],
         compiler_params=params(),
         cost_estimate=cost(4 * tok * q_width * (WINDOW + QB), 3e6),
         name="attend",
-    )(q, far, near, low)
+    )(q, far, near, low, *deps)
 
 
 FC = 512
@@ -257,13 +258,13 @@
         out_ref[...] = (h_ref[...] + zz * inv_rms(zz) * gd_ref[3:4, :]).astype(B16)
 
 
-def ffn_call(o, x, gd, w_out, w_gate, w_up, w_down):
+def ffn_call(o, x, gd, w_out, w_gate, w_up, w_down, *deps):
     tok, width = x.shape
     ff = w_gate.shape[1]
     cols = pl.BlockSpec((tok, FC), lambda j: (0, j))
     tw = whole((tok, width))
     return pl.pallas_call(
-        ffn_kernel,
+        held_back(ffn_kernel, 7, len(deps)),
         grid=(ff // FC,),
         in_specs=[
             whole(o.shape),
@@ -273,7 +274,8 @@
             pl.BlockSpec((width, FC), lambda j: (0, j)),
             pl.BlockSpec((width, FC), lambda j: (0, j)),
             pl.BlockSpec((FC, width), lambda j: (j, 0)),
-        ],
+        ]
+        + [pl.BlockSpec(memory_space=pl.ANY)] * len(deps),
         out_specs=[tw, tw, cols, cols, tw, tw],
         out_shape=[
             sds((tok, width), F32),
@@ -287,7 +289,7 @@
         compiler_params=params(),
         cost_estimate=cost(2 * tok * width * (o.shape[1] + 3 * ff), 22e6),
         name="feed_forward",
-    )(o, x, gd, w_out, w_gate, w_up, w_down)
+    )(o, x, gd, w_out, w_gate, w_up, w_down, *deps)
 
 
 def ffn_back_kernel(
@@ -576,7 +578,8 @@
 
 
 def kv_back_call(
-    layer, a, x, dh, da, dnear, dback, kpre, gd, gh, cos, sin, w_qkv, wq_grad, gd_part, gh_part
+    layer, a, x, dh, da, dnear, dback, kpre, gd, gh, cos, sin, w_qkv, wq_grad, gd_part, gh_part,
+    *deps,
 ):
     tok, width = a.shape
     q_width = wq_grad.shape[1]
@@ -585,7 +588,7 @@
     pack_shape = (PARTS, PARTS, rows, LANES)
     tw = whole((tok, width))
     return pl.pallas_call(
-        kv_back_kernel,
+        held_back(kv_back_kernel, 15, len(deps)),
         grid=(1,),
         in_specs=[
             tw,
@@ -603,13 +606,14 @@
             whole(wq_grad.shape),
             whole(gd.shape),
             whole(gh.shape),
-        ],
+        ]
+        + [pl.BlockSpec(memory_space=pl.ANY)] * len(deps),
         out_specs=[whole(pack_shape), tw],
         out_shape=[sds(pack_shape, B16), sds((tok, width), B16)],
         compiler_params=params(),
         cost_estimate=cost(8 * tok * width * HD, 10e6),
         name="keys_values_back",
-    )(a, x, dh, da, dnear, dback, kpre, gd, gh, cos, sin, w_qkv, wq_grad, gd_part, gh_part)
+    )(a, x, dh, da, dnear, dback, kpre, gd, gh, cos, sin, w_qkv, wq_grad, gd_part, gh_part, *deps)
 
 
 def pack_qkv_kernel(spot, q_ref, k_ref, v_ref, gain_ref, dep_ref, all_ref, own_ref):
@@ -915,6 +919,13 @@
     )(a, b, c, d, *deps)
 
 
+def sum_pairs_kernel(spot, a0, a1, a2, b0, b1, b2, *refs):
+    sum_parts_kernel(
+        spot, a0, a1, a2, b0, b1, b2,
+        refs[-2].at[0], refs[-1].at[0], refs[-2].at[1], refs[-1].at[1],
+    )
+
+
 def sum_parts_kernel(spot, a0, a1, a2, b0, b1, b2, *refs):
     outs = refs[-PARTS:]
     half = a0.shape[1]
@@ -925,21 +936,22 @@
             outs[d][rows, :] = total.astype(B16)
 
 
-def sum_parts(spot, split, got, last, *deps):
+def sum_parts(spot, split, got, last, *deps, pairs=False):
     keep_a, _, keep_b, _ = split
     shape = keep_a.shape[1:]
     first = pl.BlockSpec((None,) + shape, lambda i, spot: (0, 0, 0, 0))
     one = whole(shape)
-    out = (2 * shape[1], LANES)
-    return pl.pallas_call(
-        sum_parts_kernel,
+    out = ((2,) if pairs else ()) + (2 * shape[1], LANES)
+    count = 2 if pairs else PARTS
+    return pl.pallas_call(
+        sum_pairs_kernel if pairs else sum_parts_kernel,
         grid_spec=pltpu.PrefetchScalarGridSpec(
             num_scalar_prefetch=1,
             grid=(1,),
             in_specs=[first, first, one] * 2 + [pl.BlockSpec(memory_space=pl.ANY)] * len(deps),
-            out_specs=[whole(out)] * PARTS,
+            out_specs=[whole(out)] * count,
         ),
-        out_shape=[sds(out, B16)] * PARTS,
+        out_shape=[sds(out, B16)] * count,
         compiler_params=params(),
         cost_estimate=cost(0, 10 * keep_a.size),
         name="sum_parts",
@@ -979,7 +991,11 @@
 
 def finish_kernel(spot, *refs):
     firsts, seconds, got_ref = refs[:PARTS], refs[PARTS : 2 * PARTS], refs[2 * PARTS]
-    gate_ref, up_ref, down_ref, out_ref, qkv_ref, gain_ref, mine_ref = refs[2 * PARTS + 1 :]
+    gate_ref, up_ref, down_ref, out_ref, q_ref, k_ref, v_ref, gain_ref, mine_ref = refs[
+        2 * PARTS + 1 :
+    ]
+    places = [(ref, t) for ref in (q_ref, k_ref, v_ref) for t in range(ref.shape[1] // LANES)]
+    n = len(places) // PARTS
     half = got_ref.shape[1]
     part = gate_ref.shape[0]
     for e in range(PARTS):
@@ -987,10 +1003,15 @@
         @pl.when(pl.program_id(0) == e)
         def _():
             mine_ref[1 - spot[2]] = got_ref[e]
-            n = qkv_ref.shape[1] // LANES
-            for t in range(n):
-                at = half + t * part
-                qkv_ref[:, t * LANES : (t + 1) * LANES] = firsts[e][at : at + part, :].astype(F32)
+            for c_part in range(PARTS):
+
+                @pl.when(spot[0] ^ e == c_part)
+                def _():
+                    for t in range(n):
+                        ref, tile = places[c_part * n + t]
+                        block = firsts[e][half + t * part : half + (t + 1) * part, :]
+                        ref[:, tile * LANES : (tile + 1) * LANES] = block.astype(F32)
+
             gain_ref[...] = firsts[e][half + n * part :, :].astype(F32)
 
             @pl.when(spot[2] == 0)
@@ -1011,7 +1032,7 @@
 
 
 def finish(spot, firsts, seconds, got, width, ff, q_width):
-    part, cols, qkv_cols = width // PARTS, ff // PARTS, (q_width + 2 * HD) // PARTS
+    part, cols = width // PARTS, ff // PARTS
 
     def by_cols(n):
         return pl.BlockSpec((None, part, n), lambda i, spot: (0, 0, spot[0] ^ i))
@@ -1030,7 +1051,10 @@
                 by_cols(cols),
                 by_rows(ff // PARTS**2),
                 by_rows(q_width // PARTS**2),
-                by_cols(qkv_cols),
+                *[
+                    pl.BlockSpec((None, part, n), lambda i, spot: (0, 0, 0))
+                    for n in (q_width, HD, HD)
+                ],
                 pl.BlockSpec((None, GAIN_ROWS, LANES), lambda i, spot: (spot[0] ^ i, 0, 0)),
             ],
             scratch_shapes=[pltpu.VMEM((2,) + seconds[0].shape, B16)],
@@ -1040,7 +1064,7 @@
             sds((1, part, ff), F32),
             sds((1, ff // PARTS, width), F32),
             sds((1, q_width // PARTS, width), F32),
-            sds((1, part, q_width + 2 * HD), F32),
+            *[sds((1, part, n), F32) for n in (q_width, HD, HD)],
             sds((PARTS, GAIN_ROWS, LANES), F32),
         ],
         compiler_params=params(),
@@ -1116,11 +1140,15 @@
     return moved(shards, "ctx", 1, layer), moved(shards, "ctx", 2, layer)
 
 
-def far_quarter(near, deps=(), layer=None):
+def near_halves(near, *deps):
     one, two = near
     rows = one.shape[1]
-    by_one = moved(joined([(one, 0, rows // 2)], *deps), "ctx", 2, layer)
-    by_two = moved(joined([(two, rows // 2, rows)], *deps), "ctx", 1, layer)
+    return joined([(one, 0, rows // 2)], *deps), joined([(two, rows // 2, rows)], *deps)
+
+
+def far_quarter(halves):
+    by_one = moved(halves[0], "ctx", 2)
+    by_two = moved(halves[1], "ctx", 1)
     return jnp.concatenate([by_one, by_two], axis=1)
 
 
@@ -1128,9 +1156,13 @@
     return moved(split[1], "ctx", 1), moved(split[3], "ctx", 2)
 
 
-def ctx_far(split, got, *deps):
+def far_sends(split, got, *deps):
     keep_a, _, keep_b, _ = split
-    send_a, send_b = add_pairs(keep_a, got[0], keep_b, got[1], *deps)
+    return add_pairs(keep_a, got[0], keep_b, got[1], *deps)
+
+
+def ctx_far(sends):
+    send_a, send_b = sends
     return moved(send_a, "ctx", 2), moved(send_b, "ctx", 1)
 
 
@@ -1139,6 +1171,16 @@
     for d in FAR:
         total += moved(parts[d], "fsdp", d, layer).astype(F32)
     return total.astype(B16)
+
+
+def fsdp_summed_in_two(keep, send):
+    got = moved(send, "fsdp", 1)
+
+    def both(n):
+        return keep[n].astype(F32) + got[n].astype(F32)
+
+    last = moved(both(1).astype(B16), "fsdp", 2)
+    return (both(0) + last.astype(F32)).astype(B16)
 
 
 def ctx_ring(piece):
@@ -1187,6 +1229,13 @@
         gh = jnp.concatenate(gh + [jnp.zeros((6, HD), raw.dtype)]).astype(F32)
         return gd, gh
 
+    def own_row(array):
+        return lax.dynamic_index_in_dim(array[:, 0], section, 0, keepdims=False)
+
+    offset, low = layout_for(own_row(lengths), ctx_index * tok, tok)
+    cos, sin = rope_tables(offset)
+    low_col, low_row = low[:, None], low[None, :]
+
     spot = jnp.stack([ctx_index, fsdp_index, section]).astype(jnp.int32)
     if in_pieces:
         gain_rows = jnp.pad(gain_own, (0, GAIN_ROWS * LANES - gain_own.shape[0]))
@@ -1202,32 +1251,48 @@
             return own, other_shards(own)
 
         first_own, first_arriving = arriving(0)
-        shards_in = joined(other_shards(quarter), first_own)
+        shards_in = joined(other_shards(quarter), first_own, *first_arriving[:2])
         near = near_quarters(shards_in)
-        pieces = joined([qkv_parts, shards_in, *near, far_quarter(near)])
+        far = far_quarter(near_halves(near, first_arriving[2]))
+        pieces = joined(
+            [qkv_parts, shards_in, *near, far], *first_arriving, cos, sin, low_col
+        )
         w_qkv, raw = place_qkv(spot, pieces, swapped(pieces), width, q_width + 2 * HD)
         raw = raw.reshape(2, PARTS, GAIN_ROWS * LANES)
-        first_shards = joined(first_arriving, w_qkv)
+        first_shards = joined(first_arriving, pieces)
         first_near = near_quarters(first_shards)
         _, second_arriving = arriving(1, first_shards)
 
-        def place(layer, shards, near, *deps):
-            far = far_quarter(near, deps)
+        def other_half(shards, near, far):
             near = joined([shards, *near])
-            pieces = [near, far, swapped(near), swapped(far)]
+            return near, far, swapped(near), swapped(far)
+
+        state = {}
+
+        def before_attend(layer, q):
+            if layer == 0:
+                far = far_quarter(near_halves(first_near, q, *second_arriving))
+                state["pieces"] = other_half(first_shards, first_near, far)
+                return second_arriving
+            far = far_quarter(state["halves"])
+            state["pieces"] = other_half(*state["shards"], far)
+            return (far,)
+
+        def before_ffn(layer, o, gate):
+            if layer == 1:
+                return ()
+            shards = joined(second_arriving, o)
+            near = near_quarters(shards)
+            state["shards"] = (shards, near)
+            state["halves"] = near_halves(near, gate)
+            return ()
+
+        def place(layer):
             gate, up, down, out = place_ffn(
-                layer, spot, ffn_parts, ffn_other, pieces, width, ff, q_width
+                layer, spot, ffn_parts, ffn_other, state["pieces"], width, ff, q_width
             )
             return out, gate, up, down
 
-        def place_first(q, o):
-            return place(0, first_shards, first_near, q)
-
-        def place_second(q, o):
-            shards = joined(second_arriving, kept[0][7])
-            return place(1, shards, near_quarters(shards), kept[0][13])
-
-        ffn_layers = [place_first, place_second]
     else:
 
         def whole_weight(own):
@@ -1240,14 +1305,16 @@
         ]
         w_qkv = full[0]
         raw = whole_weight(gain_own[None])
-        ffn_layers = [lambda *deps, n=n: tuple(w[n] for w in full[1:]) for n in range(2)]
-
-    def own_row(array):
-        return lax.dynamic_index_in_dim(array[:, 0], section, 0, keepdims=False)
-
-    offset, low = layout_for(own_row(lengths), ctx_index * tok, tok)
-    cos, sin = rope_tables(offset)
-    low_col, low_row = low[:, None], low[None, :]
+
+        def place(layer):
+            return tuple(w[layer] for w in full[1:])
+
+        def before_attend(layer, q):
+            return ()
+
+        def before_ffn(layer, o, gate):
+            return ()
+
 
     x = own_row(inputs)
     kept = []
@@ -1256,15 +1323,15 @@
         a, kpre, near = kv_call(layer, x, gd, gh, cos, sin, w_qkv)
         far = passed_along(near, 1)
         qpre, q = q_call(layer, a, gh, cos, sin, w_qkv)
-        o = attn_call(q, far, near, low_col)
-        weights = ffn_layers[layer](q, o)
-        y, h, g, u, z, result = ffn_call(o, x, gd, *weights)
+        o = attn_call(q, far, near, low_col, *before_attend(layer, q))
+        weights = place(layer)
+        y, h, g, u, z, result = ffn_call(o, x, gd, *weights, *before_ffn(layer, o, weights[1]))
         kept.append((x, a, kpre, near, far, qpre, q, o, y, h, g, u, z, result, gd, gh, weights))
         x = result
 
     spot_back = spot if in_pieces else jnp.zeros_like(spot)
 
-    def layer_back(layer, cot, attn_deps, q_deps):
+    def layer_back(layer, cot, attn_deps, q_deps, kv_deps):
         x, a, kpre, near, far, qpre, q, o, y, h, g, u, z, result, gd, gh, weights = kept[layer]
         keep, send, dh, do, gd_part = ffn_back_call(spot_back, cot, z, h, y, o, gd, g, u, *weights)
         dq, dfar, dnear, gh_part = attn_back_call(
@@ -1276,36 +1343,43 @@
         wq_grad, da = q_back_call(layer, a, dq, w_qkv, *q_deps(keep, send, dq))
         qkv_pack, dx = kv_back_call(
             layer, a, x, dh, da, dnear, dback, kpre, gd, gh, cos, sin, w_qkv, wq_grad,
-            gd_part, gh_part,
+            gd_part, gh_part, *kv_deps(),
         )
         return (keep, send), qkv_pack, dx
 
     cot = own_row(grad_out)
     if in_pieces:
-        state = {}
-
         def split_second(keep, send, dq):
             state["split1"] = add_split(spot, keep, swapped(send))
             state["near1"] = ctx_near(state["split1"])
             return (state["split1"][0],)
 
-        ffn_pack, qkv_pack, mid = layer_back(1, cot, lambda *_: (), split_second)
+        ffn_pack, qkv_pack, mid = layer_back(1, cot, lambda *_: (), split_second, lambda: ())
 
         def far_second(keep, send):
-            state["far1"] = ctx_far(state["split1"], state["near1"], keep)
-            return ()
+            sends = far_sends(state["split1"], state["near1"], keep)
+            state["far1"] = ctx_far(sends)
+            return (sends[0],)
 
         def split_first(keep, send, dq):
-            parts = sum_parts(spot, state["split1"], state["near1"], state["far1"], dq)
             state["split0"] = add_split(spot, keep, swapped(send), dq)
             state["near0"] = ctx_near(state["split0"])
-            state["ffn1"] = fsdp_summed(parts)
-            return (state["split0"][0], parts[0])
-
-        first_ffn_pack, first_qkv_pack, grad_in = layer_back(0, mid, far_second, split_first)
+            parts = sum_parts(
+                spot, state["split1"], state["near1"], state["far1"], state["split0"][0], pairs=True
+            )
+            state["ffn1"] = fsdp_summed_in_two(*parts)
+            return (parts[0],)
+
+        def far_first():
+            state["sends0"] = far_sends(state["split0"], state["near0"])
+            return (state["sends0"][0],)
+
+        first_ffn_pack, first_qkv_pack, grad_in = layer_back(
+            0, mid, far_second, split_first, far_first
+        )
     else:
-        ffn_pack, qkv_pack, mid = layer_back(1, cot, lambda *_: (), lambda *_: ())
-        first_ffn_pack, first_qkv_pack, grad_in = layer_back(0, mid, lambda *_: (), lambda *_: ())
+        ffn_pack, qkv_pack, mid = layer_back(1, cot, *[lambda *_: ()] * 3)
+        first_ffn_pack, first_qkv_pack, grad_in = layer_back(0, mid, *[lambda *_: ()] * 3)
     packs = [(first_ffn_pack, first_qkv_pack), (ffn_pack, qkv_pack)]
     in_grads = [grad_in, mid]
 
@@ -1322,14 +1396,14 @@
         keep = jnp.where(first_layer, first_qkv_pack, qkv_pack)
         qkv_split = add_split(spot, keep, swapped(jnp.where(first_layer, qkv_pack, first_qkv_pack)))
         seconds = ctx_ring(state["ffn1"])
-        far0 = ctx_far(state["split0"], state["near0"])
+        far0 = ctx_far(state["sends0"])
         ffn0 = fsdp_summed(sum_parts(spot, state["split0"], state["near0"], far0))
         qkv_near = ctx_near(qkv_split)
-        qkv_far = ctx_far(qkv_split, qkv_near)
+        qkv_far = ctx_far(far_sends(qkv_split, qkv_near))
         qkv_own = fsdp_summed(sum_parts(spot, qkv_split, qkv_near, qkv_far))
         firsts = ctx_ring(jnp.concatenate([ffn0, qkv_own]))
         got = swapped(choose_ring(spot, firsts, seconds))
-        gate_g, up_g, down_g, out_g, qkv_g, gain_sums = finish(
+        gate_g, up_g, down_g, out_g, q_g, k_g, v_g, gain_sums = finish(
             spot, firsts, seconds, got, width, ff, q_width
         )
         gain_sums = gain_sums[:, : (4 * width + 2 * HD) // LANES // PARTS].reshape(-1)
@@ -1362,6 +1436,7 @@
         gate_g, up_g, down_g, out_g, qkv_g = (
             w.astype(F32)[None] for w in lax.psum(tuple(shard), "ctx")
         )
+        q_g, k_g, v_g = jnp.split(qkv_g, [q_width, q_width + HD], axis=2)
         gain_sums = at(lax.psum(jnp.stack(gain_sums), AXES), section).astype(F32)
 
     def gain_shard(first, n):
@@ -1375,9 +1450,9 @@
         activations[None, :, None],
         input_grads[None, :, None],
         d_gains[0],
-        qkv_g[:, :, :q_width],
-        qkv_g[:, :, q_width : q_width + HD],
-        qkv_g[:, :, q_width + HD :],
+        q_g,
+        k_g,
+        v_g,
         h_gains[0],
         h_gains[1],
         out_g,

time: 552 us -> 517 us (0.937)
  waiting for transfers between devices: 138 us -> 114 us
  starting transfers between devices: 88.3 us -> 77.7 us
    ppermute x48 -> x47, waiting for transfers between devices: 136 us -> 114 us  [moved(): return lax.ppermute(array, AXES, pairs)]
    ppermute x48 -> x47, starting transfers between devices: 78.6 us -> 68.1 us  [moved(): return lax.ppermute(array, AXES, pairs)]
    unnamed x147 -> x139, local copies, waits for them, and re-layouts: 22.4 us -> 25.6 us
  transfers between devices with their start and end apart: 63 -> 62, of which waited for: 22 -> 22; matrix products, arithmetic and copies ran while one was open for 3% -> 4% of each run, Pallas kernels for 35% -> 39%
where the time goes in v3:
time: 517 us; the launch traced here: 510 us
  Pallas kernels  268 us (52%)
  waiting for transfers between devices  114 us (22%)
  starting transfers between devices  77.7 us (15%)
  local copies, waits for them, and re-layouts  31.8 us (6%)
  other arithmetic  16.9 us (3%)
    ppermute x47, waiting for transfers between devices, moved(): return lax.ppermute(array, AXES, pairs)  114 us
    ppermute x47, starting transfers between devices, moved(): return lax.ppermute(array, AXES, pairs)  68.1 us
    pallas_call x2, Pallas kernels, ffn_back_call(): pl.pallas_call(ffn_back_kernel, grid_spec=pltpu.PrefetchScalarGridSpec(nu...  52.8 us
    pallas_call x2, Pallas kernels, attn_back_call(): pl.pallas_call(held_back(attn_back_kernel, 9, len(deps)), grid=(tok // QB...  29.3 us
    pallas_call x2, Pallas kernels, ffn_call(): pl.pallas_call(held_back(ffn_kernel, 7, len(deps)), grid=(ff // FC,), in_...  27.4 us
    pallas_call x12, Pallas kernels, joined(): pl.pallas_call(body, in_specs=[pl.BlockSpec(memory_space=pltpu.VMEM)] * l...  26.7 us
    unnamed x139, local copies, waits for them, and re-layouts  25.6 us
    pallas_call x3, Pallas kernels, add_split(): pl.pallas_call(add_split_kernel, grid_spec=pltpu.PrefetchScalarGridSpec(n...  19.5 us
  transfers between devices with their start and end apart: 62, of which 22 were waited for; matrix products, arithmetic and copies ran while one was open for 4% of the time, Pallas kernels for 39%

profile of v3, /device:TPU:0, one launch (start us, length us, event | category | flops | bytes accessed | tf_op | source)
XLA Modules:
  0.0 510.5 jit_solution(8593219681925346598)
XLA Ops:
  0.7 4.1 pack_ffn.1.dep_ref.own_ref
  18.2 3.5 collective-permute-start.5
  21.9 3.3 collective-permute-done.1.refs_1_
  25.2 7.4 %collective-permute-done.4.refs_4_.refs_5_.refs_0_ = bf16[1,1120,128]{2,1,0:T(8,128)(2,1)S(1)} collective-permute-done((bf16[1,1120,128]{2,1,0:T(8,128)(2,1)}, bf16[1,1120,128]{2,1,0:T(8,128)(2,1)S(1)}, u32[]{:S(2)}, u32[]{:S(2)}) %collective-permute-start.4) | collective-permute-done | bytes 286752 | tf_op jit(solution)/shard_map/ppermute | solution.py:1115
  32.6 7.0 %collective-permute-done.5.refs_5_.refs_6_.refs_1_ = bf16[1,1120,128]{2,1,0:T(8,128)(2,1)S(1)} collective-permute-done((bf16[1,1120,128]{2,1,0:T(8,128)(2,1)}, bf16[1,1120,128]{2,1,0:T(8,128)(2,1)S(1)}, u32[]{:S(2)}, u32[]{:S(2)}) %collective-permute-start.5) | collective-permute-done | bytes 286752 | tf_op jit(solution)/shard_map/ppermute | solution.py:1115
  49.6 5.1 collective-permute-done.8.refs_1_.refs_7_.refs_2_
  63.8 2.9 collective-permute-done.10
  67.5 2.9 joined.15.own_ref.refs_3_
  76.1 3.9 collective-permute-start.13
  85.2 5.2 %place_qkv.1 = (bf16[2,640,1536]{2,1,0:T(8,128)(2,1)}, bf16[2,4,32,128]{3,2,1,0:T(8,128)(2,1)}) custom-call(s32[3]{0:T(128)} %pad_add_fusion.spot, bf16[16,512,128]{2,1,0:T(8,128)(2,1)} %joined.15.own_ref.refs_3_, bf16[16,512,128]{2,1,0:T(8,128)(2,1)} %copy-done.17), custom_call_target="tpu_custom_call" | custom-call | bytes 8000000 | tf_op jit(solution)/shard_map/place_qkv/pallas_call | solution.py:759
  93.5 3.1 keys_values.2
  96.6 4.8 queries.2
  108.5 3.1 collective-permute-start.12
  117.8 3.3 joined.17.near_ref
  122.2 5.4 %collective-permute-done.18 = bf16[3,560,128]{2,1,0:T(8,128)(2,1)S(1)} collective-permute-done((bf16[3,560,128]{2,1,0:T(8,128)(2,1)}, bf16[3,560,128]{2,1,0:T(8,128)(2,1)S(1)}, u32[]{:S(2)}, u32[]{:S(2)}) %collective-permute-start.18) | collective-permute-done | bytes 430112 | tf_op jit(solution)/shard_map/ppermute | solution.py:1115
  127.6 5.7 %collective-permute-done.19 = bf16[3,560,128]{2,1,0:T(8,128)(2,1)S(1)} collective-permute-done((bf16[3,560,128]{2,1,0:T(8,128)(2,1)}, bf16[3,560,128]{2,1,0:T(8,128)(2,1)S(1)}, u32[]{:S(2)}, u32[]{:S(2)}) %collective-permute-start.19) | collective-permute-done | bytes 430112 | tf_op jit(solution)/shard_map/ppermute | solution.py:1115
  134.3 6.4 %attend.2.refs_0_.refs_3_.o_ref = bf16[512,1024]{1,0:T(8,128)(2,1)} custom-call(bf16[512,1024]{1,0:T(8,128)(2,1)} %get-tuple-element.116.refs_0_.refs_1_, bf16[512,512]{1,0:T(8,128)(2,1)} %copy-done.64, bf16[512,512]{1,0:T(8,128)(2,1)} %get-tuple-element.117.refs_2_.refs_4_, s32[512,1]{1,0:T(8,128)} %subtract_add_fusion.refs_10_.refs_3_, ...), custom_call_target="tpu_custom_call" | custom-call | flops 40265318400 | bytes 3000000 | tf_op jit(solution)/shard_map/attend/pallas_call | solution.py:203
  144.8 8.2 %place_ffn.2 = (bf16[640,2048]{1,0:T(8,128)(2,1)}, bf16[640,2048]{1,0:T(8,128)(2,1)}, bf16[4,4,128,640]{3,2,1,0:T(8,128)(2,1)}, bf16[4,4,64,640]{3,2,1,0:T(8,128)(2,1)}) custom-call(s32[3]{0:T(128)} %pad_add_fusion.spot, bf16[4,2,1120,128]{3,2,1,0:T(8,128)(2,1)} %bitcast.61, bf16[4,2,1120,128]{3,2,1,0:T(8,128)(2,1)} %bitcast.12.other_ref, ...), custom_call_target="tpu_custom_call" | custom-call | bytes 18000000 | tf_op jit(solution)/shard_map/place_ffn/pallas_call | solution.py:845
  153.0 13.7 %feed_forward.2 = (f32[512,640]{1,0:T(8,128)}, f32[512,640]{1,0:T(8,128)}, bf16[512,2048]{1,0:T(8,128)(2,1)}, bf16[512,2048]{1,0:T(8,128)(2,1)}, f32[512,640]{1,0:T(8,128)}, /*index=5*/bf16[512,640]{1,0:T(8,128)(2,1)}) custom-call(bf16[512,1024]{1,0:T(8,128)(2,1)} %attend.2.refs_0_.refs_3_.o_ref, bf16[512,640]{1,0:T(8,128)(2,1)} %dynamic-slice_bitcast_fusion.1.x_ref.refs_1_, ...), custom_call_target="tpu_custom_call" | custom-call | flops 140928614400 | bytes 22000000 | tf_op jit(solution)/shard_map/feed_forward/pallas_call | solution.py:266
  166.7 3.1 keys_values.3
  178.5 4.8 queries.3
  183.3 3.3 joined.23.near_ref
  186.7 7.8 %collective-permute-done.24 = bf16[3,560,128]{2,1,0:T(8,128)(2,1)S(1)} collective-permute-done((bf16[3,560,128]{2,1,0:T(8,128)(2,1)}, bf16[3,560,128]{2,1,0:T(8,128)(2,1)S(1)}, u32[]{:S(2)}, u32[]{:S(2)}) %collective-permute-start.24) | collective-permute-done | bytes 430112 | tf_op jit(solution)/shard_map/ppermute | solution.py:1115
  196.6 6.4 %attend.3.refs_0_.o_ref = bf16[512,1024]{1,0:T(8,128)(2,1)} custom-call(bf16[512,1024]{1,0:T(8,128)(2,1)} %get-tuple-element.124.refs_0_, bf16[512,512]{1,0:T(8,128)(2,1)} %copy-done.65, bf16[512,512]{1,0:T(8,128)(2,1)} %get-tuple-element.125.refs_2_.refs_4_, s32[512,1]{1,0:T(8,128)} %subtract_add_fusion.refs_10_.refs_3_, bf16[3,1120,128]{2,1,0:T(8,128)(2,1)} %copy-done.23), custom_call_target="tpu_custom_call" | custom-call | flops 40265318400 | bytes 3000000 | tf_op jit(solution)/shard_map/attend/pallas_call | solution.py:203
  205.4 8.2 %place_ffn.3 = (bf16[640,2048]{1,0:T(8,128)(2,1)}, bf16[640,2048]{1,0:T(8,128)(2,1)}, bf16[4,4,128,640]{3,2,1,0:T(8,128)(2,1)}, bf16[4,4,64,640]{3,2,1,0:T(8,128)(2,1)}) custom-call(s32[3]{0:T(128)} %pad_add_fusion.spot, bf16[4,2,1120,128]{3,2,1,0:T(8,128)(2,1)} %bitcast.62, bf16[4,2,1120,128]{3,2,1,0:T(8,128)(2,1)} %bitcast.12.other_ref, ...), custom_call_target="tpu_custom_call" | custom-call | bytes 18000000 | tf_op jit(solution)/shard_map/place_ffn/pallas_call | solution.py:845
  213.6 13.7 %feed_forward.3 = (f32[512,640]{1,0:T(8,128)}, f32[512,640]{1,0:T(8,128)}, bf16[512,2048]{1,0:T(8,128)(2,1)}, bf16[512,2048]{1,0:T(8,128)(2,1)}, f32[512,640]{1,0:T(8,128)}, /*index=5*/bf16[512,640]{1,0:T(8,128)(2,1)}) custom-call(bf16[512,1024]{1,0:T(8,128)(2,1)} %attend.3.refs_0_.o_ref, bf16[512,640]{1,0:T(8,128)(2,1)} %get-tuple-element.122.x_ref.refs_1_, ...), custom_call_target="tpu_custom_call" | custom-call | flops 140928614400 | bytes 22000000 | tf_op jit(solution)/shard_map/feed_forward/pallas_call | solution.py:266
  227.3 26.6 %feed_forward_back.2 = (bf16[4,4,1120,128]{3,2,1,0:T(8,128)(2,1)}, bf16[4,4,1120,128]{3,2,1,0:T(8,128)(2,1)}, f32[512,640]{1,0:T(8,128)}, bf16[512,1024]{1,0:T(8,128)(2,1)}, f32[8,640]{1,0:T(8,128)}) custom-call(s32[3]{0:T(128)} %pad_add_fusion.spot, bf16[512,640]{1,0:T(8,128)(2,1)} %dynamic-slice_bitcast_fusion.c_ref, f32[512,640]{1,0:T(8,128)} %get-tuple-element.130.z_ref, ...), custom_call_target="tpu_custom_call" | custom-call | flops 281857228800 | bytes 35000000 | tf_op jit(solution)/shard_map/feed_forward_back/pallas_call | solution.py:387
  254.3 14.6 %attend_back.2 = (bf16[512,1024]{1,0:T(8,128)(2,1)}, bf16[512,512]{1,0:T(8,128)(2,1)}, f32[512,512]{1,0:T(8,128)}, f32[8,256]{1,0:T(8,128)}) custom-call(bf16[512,1024]{1,0:T(8,128)(2,1)} %get-tuple-element.124.refs_0_, bf16[512,1024]{1,0:T(8,128)(2,1)} %get-tuple-element.136.refs_1_, bf16[512,1024]{1,0:T(8,128)(2,1)} %get-tuple-element.137.refs_2_, ...), custom_call_target="tpu_custom_call" | custom-call | flops 100663296000 | bytes 8000000 | tf_op jit(solution)/shard_map/attend_back/pallas_call | solution.py:480
  272.4 7.4 %add_split.3 = (bf16[2,4,560,128]{3,2,1,0:T(8,128)(2,1)}, bf16[2,4,560,128]{3,2,1,0:T(8,128)(2,1)}, bf16[2,4,560,128]{3,2,1,0:T(8,128)(2,1)}, bf16[2,4,560,128]{3,2,1,0:T(8,128)(2,1)}) custom-call(s32[3]{0:T(128)} %pad_add_fusion.spot, bf16[4,4,1120,128]{3,2,1,0:T(8,128)(2,1)} %get-tuple-element.139.first_ref, bf16[4,4,1120,128]{3,2,1,0:T(8,128)(2,1)} %copy-done.4), custom_call_target="tpu_custom_call" | custom-call | bytes 13762560 | tf_op jit(solution)/shard_map/add_split/pallas_call | solution.py:887
  283.9 4.6 queries_back.2
  289.3 6.8 %keys_values_back.2 = (bf16[4,4,512,128]{3,2,1,0:T(8,128)(2,1)}, bf16[512,640]{1,0:T(8,128)(2,1)}) custom-call(bf16[512,640]{1,0:T(8,128)(2,1)} %get-tuple-element.123.a_ref.refs_0_, bf16[512,640]{1,0:T(8,128)(2,1)} %get-tuple-element.122.x_ref.refs_1_, f32[512,640]{1,0:T(8,128)} %get-tuple-element.135.refs_2_, f32[512,640]{1,0:T(8,128)} %get-tuple-element.142.refs_3_, ...), custom_call_target="tpu_custom_call" | custom-call | flops 20132659200 | bytes 10000000 | tf_op jit(solution)/shard_map/keys_values_back/pallas_call | solution.py:590
  296.1 26.2 %feed_forward_back.3 = (bf16[4,4,1120,128]{3,2,1,0:T(8,128)(2,1)}, bf16[4,4,1120,128]{3,2,1,0:T(8,128)(2,1)}, f32[512,640]{1,0:T(8,128)}, bf16[512,1024]{1,0:T(8,128)(2,1)}, f32[8,640]{1,0:T(8,128)}) custom-call(s32[3]{0:T(128)} %pad_add_fusion.spot, bf16[512,640]{1,0:T(8,128)(2,1)} %get-tuple-element.149.c_ref, f32[512,640]{1,0:T(8,128)} %get-tuple-element.150.z_ref, ...), custom_call_target="tpu_custom_call" | custom-call | flops 281857228800 | bytes 35000000 | tf_op jit(solution)/shard_map/feed_forward_back/pallas_call | solution.py:387
  325.7 14.7 %attend_back.3 = (bf16[512,1024]{1,0:T(8,128)(2,1)}, bf16[512,512]{1,0:T(8,128)(2,1)}, f32[512,512]{1,0:T(8,128)}, f32[8,256]{1,0:T(8,128)}) custom-call(bf16[512,1024]{1,0:T(8,128)(2,1)} %get-tuple-element.116.refs_0_.refs_1_, bf16[512,1024]{1,0:T(8,128)(2,1)} %get-tuple-element.156.refs_1_, bf16[512,1024]{1,0:T(8,128)(2,1)} %get-tuple-element.157.refs_2_, ...), custom_call_target="tpu_custom_call" | custom-call | flops 100663296000 | bytes 8000000 | tf_op jit(solution)/shard_map/attend_back/pallas_call | solution.py:480
  344.0 7.0 %add_split.4 = (bf16[2,4,560,128]{3,2,1,0:T(8,128)(2,1)}, bf16[2,4,560,128]{3,2,1,0:T(8,128)(2,1)}, bf16[2,4,560,128]{3,2,1,0:T(8,128)(2,1)}, bf16[2,4,560,128]{3,2,1,0:T(8,128)(2,1)}) custom-call(s32[3]{0:T(128)} %pad_add_fusion.spot, bf16[4,4,1120,128]{3,2,1,0:T(8,128)(2,1)} %get-tuple-element.161.refs_0_.first_ref, bf16[4,4,1120,128]{3,2,1,0:T(8,128)(2,1)} %copy-done.3, ...), custom_call_target="tpu_custom_call" | custom-call | bytes 13762560 | tf_op jit(solution)/shard_map/add_split/pallas_call | solution.py:887
  356.6 4.0 sum_parts.3
  360.6 4.6 queries_back.3
  365.2 16.0 %collective-permute-done.37.b_ref.a1 = bf16[2,4,560,128]{3,2,1,0:T(8,128)(2,1)S(1)} collective-permute-done((bf16[2,4,560,128]{3,2,1,0:T(8,128)(2,1)}, bf16[2,4,560,128]{3,2,1,0:T(8,128)(2,1)S(1)}, u32[]{:S(2)}, u32[]{:S(2)}) %collective-permute-start.37) | collective-permute-done | bytes 1146912 | tf_op jit(solution)/shard_map/ppermute | solution.py:1115
  386.1 6.8 %keys_values_back.3 = (bf16[4,4,512,128]{3,2,1,0:T(8,128)(2,1)}, bf16[512,640]{1,0:T(8,128)(2,1)}) custom-call(bf16[512,640]{1,0:T(8,128)(2,1)} %get-tuple-element.115.a_ref.refs_0_, bf16[512,640]{1,0:T(8,128)(2,1)} %dynamic-slice_bitcast_fusion.1.x_ref.refs_1_, f32[512,640]{1,0:T(8,128)} %get-tuple-element.155.refs_2_, ...), custom_call_target="tpu_custom_call" | custom-call | flops 20132659200 | bytes 10000000 | tf_op jit(solution)/shard_map/keys_values_back/pallas_call | solution.py:590
  392.9 3.3 broadcast_select_fusion
  396.2 5.6 %collective-permute-start.56 = (bf16[2,1120,128]{2,1,0:T(8,128)(2,1)S(1)}, bf16[2,1120,128]{2,1,0:T(8,128)(2,1)S(1)}, u32[]{:S(2)}, u32[]{:S(2)}) collective-permute-start(bf16[2,1120,128]{2,1,0:T(8,128)(2,1)S(1)} %copy-done.61), channel_id=1, source_target_pairs={{0,4},{1,5},{2,6},{3,7},{4,0},{5,1},{6,2},{7,3},{8,12},{9,13},{10,... | collective-permute-start | bytes 1720328 | tf_op jit(solution)/shard_map/ppermute | solution.py:1115
  406.3 5.1 add_split.5
  419.9 3.9 sum_parts.4
  425.8 3.5 collective-permute-done.46.b_ref.a1
  446.7 4.1 collective-permute-done.43
  453.5 11.7 %collective-permute-done.51 = bf16[512,128]{1,0:T(8,128)(2,1)S(1)} collective-permute-done((bf16[512,128]{1,0:T(8,128)(2,1)}, bf16[512,128]{1,0:T(8,128)(2,1)S(1)}, u32[]{:S(2)}, u32[]{:S(2)}) %collective-permute-start.51) | collective-permute-done | bytes 131104 | tf_op jit(solution)/shard_map/ppermute | solution.py:1115
  471.6 19.7 %collective-permute-done.60.refs_7_ = bf16[1120,128]{1,0:T(8,128)(2,1)S(1)} collective-permute-done((bf16[1120,128]{1,0:T(8,128)(2,1)S(1)}, bf16[1120,128]{1,0:T(8,128)(2,1)S(1)}, u32[]{:S(2)}, u32[]{:S(2)}) %collective-permute-start.60) | collective-permute-done | bytes 286752 | tf_op jit(solution)/shard_map/ppermute | solution.py:1115
  493.8 3.5 choose_ring.1
  502.2 5.8 %finish.1 = (f32[1,160,2048]{2,1,0:T(8,128)}, f32[1,160,2048]{2,1,0:T(8,128)}, f32[1,512,640]{2,1,0:T(8,128)}, f32[1,256,640]{2,1,0:T(8,128)}, f32[1,160,1024]{2...) custom-call(s32[3]{0:T(128)} %pad_add_fusion.spot, ...), custom_call_target="tpu_custom_call" | custom-call | bytes 12000000 | tf_op jit(solution)/shard_map/finish/pallas_call | solution.py:1043
  (324 shorter events, 156.9 us)
Async XLA Ops:
  12.1 13.1 %collective-permute-start.1 = (bf16[1,512,128]{2,1,0:T(8,128)(2,1)}, bf16[1,512,128]{2,1,0:T(8,128)(2,1)S(1)}, u32[]{:S(2)}, u32[]{:S(2)}) collective-permute-start(bf16[1,512,128]{2,1,0:T(8,128)(2,1)} %get-tuple-element.112), channel_id=1, source_target_pairs={{0,8},{1,9},{2,10},{3,11},{4,12},{5,13},{6,14},{7,15},{8,0},{9,1},... | collective-permute-start | bytes 393224 | tf_op jit(solution)/shard_map/ppermute | solution.py:1115
  17.3 15.3 %collective-permute-start.4 = (bf16[1,1120,128]{2,1,0:T(8,128)(2,1)}, bf16[1,1120,128]{2,1,0:T(8,128)(2,1)S(1)}, u32[]{:S(2)}, u32[]{:S(2)}) collective-permute-start(bf16[1,1120,128]{2,1,0:T(8,128)(2,1)} %half_quarter.2.refs_3_), channel_id=1, source_target_pairs={{0,4},{1,5},{2,6},{3,7},{4,0},{5,1},{6,2},{7,3},{8,12},{9,13},{10,... | collective-permute-start | bytes 860168 | tf_op jit(solution)/shard_map/ppermute | solution.py:1115
  18.2 21.5 %collective-permute-start.5 = (bf16[1,1120,128]{2,1,0:T(8,128)(2,1)}, bf16[1,1120,128]{2,1,0:T(8,128)(2,1)S(1)}, u32[]{:S(2)}, u32[]{:S(2)}) collective-permute-start(bf16[1,1120,128]{2,1,0:T(8,128)(2,1)} %half_quarter.2.refs_3_), channel_id=1, source_target_pairs={{0,8},{1,9},{2,10},{3,11},{4,12},{5,13},{6,14},{7,15},{8,0},{9,1},... | collective-permute-start | bytes 860168 | tf_op jit(solution)/shard_map/ppermute | solution.py:1115
  43.7 14.7 %collective-permute-start.7 = (bf16[3,512,128]{2,1,0:T(8,128)(2,1)}, bf16[3,512,128]{2,1,0:T(8,128)(2,1)S(1)}, u32[]{:S(2)}, u32[]{:S(2)}) collective-permute-start(bf16[3,512,128]{2,1,0:T(8,128)(2,1)} %joined.12.refs_1_), channel_id=1, source_target_pairs={{0,2},{1,3},{2,0},{3,1},{4,6},{5,7},{6,4},{7,5},{8,10},{9,11},{10,... | collective-permute-start | bytes 1179656 | tf_op jit(solution)/shard_map/ppermute | solution.py:1115
  70.4 13.5 %collective-permute-start.11 = (bf16[16,512,128]{2,1,0:T(8,128)(2,1)}, bf16[16,512,128]{2,1,0:T(8,128)(2,1)S(1)}, u32[]{:S(2)}, u32[]{:S(2)}) collective-permute-start(bf16[16,512,128]{2,1,0:T(8,128)(2,1)} %joined.15.own_ref.refs_3_), channel_id=1, source_target_pairs={{0,16},{16,0},{1,17},{17,1},{2,18},{18,2},{3,19},{19,3},{4,20},{20... | collective-permute-start | bytes 6291464 | tf_op jit(solution)/shard_map/ppermute | solution.py:1119
  76.1 25.3 %collective-permute-start.13 = (bf16[1,1120,128]{2,1,0:T(8,128)(2,1)}, bf16[1,1120,128]{2,1,0:T(8,128)(2,1)S(1)}, u32[]{:S(2)}, u32[]{:S(2)}) collective-permute-start(bf16[1,1120,128]{2,1,0:T(8,128)(2,1)} %half_quarter.3), channel_id=1, source_target_pairs={{0,4},{1,5},{2,6},{3,7},{4,0},{5,1},{6,2},{7,3},{8,12},{9,13},{10,... | collective-permute-start | bytes 860168 | tf_op jit(solution)/shard_map/ppermute | solution.py:1115
  80.0 23.1 %collective-permute-start.14 = (bf16[1,1120,128]{2,1,0:T(8,128)(2,1)}, bf16[1,1120,128]{2,1,0:T(8,128)(2,1)S(1)}, u32[]{:S(2)}, u32[]{:S(2)}) collective-permute-start(bf16[1,1120,128]{2,1,0:T(8,128)(2,1)} %half_quarter.3), channel_id=1, source_target_pairs={{0,8},{1,9},{2,10},{3,11},{4,12},{5,13},{6,14},{7,15},{8,0},{9,1},... | collective-permute-start | bytes 860168 | tf_op jit(solution)/shard_map/ppermute | solution.py:1115
  80.0 23.1 %collective-permute-start.15 = (bf16[1,1120,128]{2,1,0:T(8,128)(2,1)}, bf16[1,1120,128]{2,1,0:T(8,128)(2,1)}, u32[]{:S(2)}, u32[]{:S(2)}) collective-permute-start(bf16[1,1120,128]{2,1,0:T(8,128)(2,1)} %half_quarter.3), channel_id=1, source_target_pairs={{0,12},{1,13},{2,14},{3,15},{4,8},{5,9},{6,10},{7,11},{8,4},{9,5},... | collective-permute-start | bytes 860168 | tf_op jit(solution)/shard_map/ppermute | solution.py:1115
  82.4 29.2 %collective-permute-start.17 = (bf16[3,1120,128]{2,1,0:T(8,128)(2,1)S(1)}, bf16[3,1120,128]{2,1,0:T(8,128)(2,1)S(1)}, u32[]{:S(2)}, u32[]{:S(2)}) collective-permute-start(bf16[3,1120,128]{2,1,0:T(8,128)(2,1)S(1)} %copy-done.2), channel_id=1, source_target_pairs={{0,2},{1,3},{2,0},{3,1},{4,6},{5,7},{6,4},{7,5},{8,10},{9,11},{10,... | collective-permute-start | bytes 2580488 | tf_op jit(solution)/shard_map/ppermute | solution.py:1115
  83.9 20.7 %collective-permute-start.16 = (bf16[3,1120,128]{2,1,0:T(8,128)(2,1)S(1)}, bf16[3,1120,128]{2,1,0:T(8,128)(2,1)S(1)}, u32[]{:S(2)}, u32[]{:S(2)}) collective-permute-start(bf16[3,1120,128]{2,1,0:T(8,128)(2,1)S(1)} %copy-done.2), channel_id=1, source_target_pairs={{0,1},{1,0},{2,3},{3,2},{4,5},{5,4},{6,7},{7,6},{8,9},{9,8},{10,11... | collective-permute-start | bytes 2580488 | tf_op jit(solution)/shard_map/ppermute | solution.py:1115
  107.4 20.2 %collective-permute-start.18 = (bf16[3,560,128]{2,1,0:T(8,128)(2,1)}, bf16[3,560,128]{2,1,0:T(8,128)(2,1)S(1)}, u32[]{:S(2)}, u32[]{:S(2)}) collective-permute-start(bf16[3,560,128]{2,1,0:T(8,128)(2,1)} %joined.18), channel_id=1, source_target_pairs={{0,2},{1,3},{2,0},{3,1},{4,6},{5,7},{6,4},{7,5},{8,10},{9,11},{10,... | collective-permute-start | bytes 1290248 | tf_op jit(solution)/shard_map/ppermute | solution.py:1115
  108.5 24.9 %collective-permute-start.12 = (bf16[512,512]{1,0:T(8,128)(2,1)}, bf16[512,512]{1,0:T(8,128)(2,1)S(1)}, u32[]{:S(2)}, u32[]{:S(2)}) collective-permute-start(bf16[512,512]{1,0:T(8,128)(2,1)} %get-tuple-element.117.refs_2_.refs_4_), channel_id=1, source_target_pairs={{0,1},{1,2},{2,3},{4,5},{5,6},{6,7},{8,9},{9,10},{10,11},{12,13},{... | collective-permute-start | bytes 1572872 | tf_op jit(solution)/shard_map/ppermute | solution.py:1125
  114.5 18.8 %collective-permute-start.19 = (bf16[3,560,128]{2,1,0:T(8,128)(2,1)}, bf16[3,560,128]{2,1,0:T(8,128)(2,1)S(1)}, u32[]{:S(2)}, u32[]{:S(2)}) collective-permute-start(bf16[3,560,128]{2,1,0:T(8,128)(2,1)} %joined.19), channel_id=1, source_target_pairs={{0,1},{1,0},{2,3},{3,2},{4,5},{5,4},{6,7},{7,6},{8,9},{9,8},{10,11... | collective-permute-start | bytes 1290248 | tf_op jit(solution)/shard_map/ppermute | solution.py:1115
  121.1 22.8 %collective-permute-start.20 = (bf16[9,1120,128]{2,1,0:T(8,128)(2,1)}, bf16[9,1120,128]{2,1,0:T(8,128)(2,1)}, u32[]{:S(2)}, u32[]{:S(2)}) collective-permute-start(bf16[9,1120,128]{2,1,0:T(8,128)(2,1)} %joined.17.near_ref), channel_id=1, source_target_pairs={{0,16},{16,0},{1,17},{17,1},{2,18},{18,2},{3,19},{19,3},{4,20},{20... | collective-permute-start | bytes 7741448 | tf_op jit(solution)/shard_map/ppermute | solution.py:1119
  142.9 33.2 %collective-permute-start.23 = (bf16[3,1120,128]{2,1,0:T(8,128)(2,1)}, bf16[3,1120,128]{2,1,0:T(8,128)(2,1)}, u32[]{:S(2)}, u32[]{:S(2)}) collective-permute-start(bf16[3,1120,128]{2,1,0:T(8,128)(2,1)} %joined.20.refs_0_), channel_id=1, source_target_pairs={{0,1},{1,0},{2,3},{3,2},{4,5},{5,4},{6,7},{7,6},{8,9},{9,8},{10,11... | collective-permute-start | bytes 2580488 | tf_op jit(solution)/shard_map/ppermute | solution.py:1115
  142.9 29.8 %collective-permute-start.25 = (bf16[3,1120,128]{2,1,0:T(8,128)(2,1)}, bf16[3,1120,128]{2,1,0:T(8,128)(2,1)}, u32[]{:S(2)}, u32[]{:S(2)}) collective-permute-start(bf16[3,1120,128]{2,1,0:T(8,128)(2,1)} %joined.20.refs_0_), channel_id=1, source_target_pairs={{0,2},{1,3},{2,0},{3,1},{4,6},{5,7},{6,4},{7,5},{8,10},{9,11},{10,... | collective-permute-start | bytes 2580488 | tf_op jit(solution)/shard_map/ppermute | solution.py:1115
  169.7 25.8 %collective-permute-start.22 = (bf16[512,512]{1,0:T(8,128)(2,1)}, bf16[512,512]{1,0:T(8,128)(2,1)S(1)}, u32[]{:S(2)}, u32[]{:S(2)}) collective-permute-start(bf16[512,512]{1,0:T(8,128)(2,1)} %get-tuple-element.125.refs_2_.refs_4_), channel_id=1, source_target_pairs={{0,1},{1,2},{2,3},{4,5},{5,6},{6,7},{8,9},{9,10},{10,11},{12,13},{... | collective-permute-start | bytes 1572872 | tf_op jit(solution)/shard_map/ppermute | solution.py:1125
  174.6 20.8 %collective-permute-start.26 = (bf16[3,560,128]{2,1,0:T(8,128)(2,1)}, bf16[3,560,128]{2,1,0:T(8,128)(2,1)S(1)}, u32[]{:S(2)}, u32[]{:S(2)}) collective-permute-start(bf16[3,560,128]{2,1,0:T(8,128)(2,1)} %joined.22), channel_id=1, source_target_pairs={{0,1},{1,0},{2,3},{3,2},{4,5},{5,4},{6,7},{7,6},{8,9},{9,8},{10,11... | collective-permute-start | bytes 1290248 | tf_op jit(solution)/shard_map/ppermute | solution.py:1115
  178.0 16.5 %collective-permute-start.24 = (bf16[3,560,128]{2,1,0:T(8,128)(2,1)}, bf16[3,560,128]{2,1,0:T(8,128)(2,1)S(1)}, u32[]{:S(2)}, u32[]{:S(2)}) collective-permute-start(bf16[3,560,128]{2,1,0:T(8,128)(2,1)} %joined.21), channel_id=1, source_target_pairs={{0,2},{1,3},{2,0},{3,1},{4,6},{5,7},{6,4},{7,5},{8,10},{9,11},{10,... | collective-permute-start | bytes 1290248 | tf_op jit(solution)/shard_map/ppermute | solution.py:1115
  186.7 16.3 %collective-permute-start.27 = (bf16[9,1120,128]{2,1,0:T(8,128)(2,1)}, bf16[9,1120,128]{2,1,0:T(8,128)(2,1)S(1)}, u32[]{:S(2)}, u32[]{:S(2)}) collective-permute-start(bf16[9,1120,128]{2,1,0:T(8,128)(2,1)} %joined.23.near_ref), channel_id=1, source_target_pairs={{0,16},{16,0},{1,17},{17,1},{2,18},{18,2},{3,19},{19,3},{4,20},{20... | collective-permute-start | bytes 7741448 | tf_op jit(solution)/shard_map/ppermute | solution.py:1119
  254.0 16.2 %collective-permute-start.29 = (bf16[4,4,1120,128]{3,2,1,0:T(8,128)(2,1)}, bf16[4,4,1120,128]{3,2,1,0:T(8,128)(2,1)S(1)}, u32[]{:S(2)}, u32[]{:S(2)}) collective-permute-start(bf16[4,4,1120,128]{3,2,1,0:T(8,128)(2,1)} %get-tuple-element.140), channel_id=1, source_target_pairs={{0,16},{16,0},{1,17},{17,1},{2,18},{18,2},{3,19},{19,3},{4,20},{20... | collective-permute-start | bytes 13762568 | tf_op jit(solution)/shard_map/ppermute | solution.py:1119
  268.9 19.6 %collective-permute-start.30 = (bf16[512,512]{1,0:T(8,128)(2,1)}, bf16[512,512]{1,0:T(8,128)(2,1)S(1)}, u32[]{:S(2)}, u32[]{:S(2)}) collective-permute-start(bf16[512,512]{1,0:T(8,128)(2,1)} %get-tuple-element.144), channel_id=1, source_target_pairs={{1,0},{2,1},{3,2},{5,4},{6,5},{7,6},{9,8},{10,9},{11,10},{13,12},{... | collective-permute-start | bytes 1572872 | tf_op jit(solution)/shard_map/ppermute | solution.py:1125
  279.8 42.6 %collective-permute-start.31 = (bf16[2,4,560,128]{3,2,1,0:T(8,128)(2,1)}, bf16[2,4,560,128]{3,2,1,0:T(8,128)(2,1)}, u32[]{:S(2)}, u32[]{:S(2)}) collective-permute-start(bf16[2,4,560,128]{3,2,1,0:T(8,128)(2,1)} %get-tuple-element.158), channel_id=1, source_target_pairs={{0,1},{1,0},{2,3},{3,2},{4,5},{5,4},{6,7},{7,6},{8,9},{9,8},{10,11... | collective-permute-start | bytes 3440648 | tf_op jit(solution)/shard_map/ppermute | solution.py:1115
  282.4 40.0 %collective-permute-start.32 = (bf16[2,4,560,128]{3,2,1,0:T(8,128)(2,1)}, bf16[2,4,560,128]{3,2,1,0:T(8,128)(2,1)}, u32[]{:S(2)}, u32[]{:S(2)}) collective-permute-start(bf16[2,4,560,128]{3,2,1,0:T(8,128)(2,1)} %get-tuple-element.160), channel_id=1, source_target_pairs={{0,2},{1,3},{2,0},{3,1},{4,6},{5,7},{6,4},{7,5},{8,10},{9,11},{10,... | collective-permute-start | bytes 3440648 | tf_op jit(solution)/shard_map/ppermute | solution.py:1115
  322.3 19.5 %collective-permute-start.35 = (bf16[4,4,1120,128]{3,2,1,0:T(8,128)(2,1)}, bf16[4,4,1120,128]{3,2,1,0:T(8,128)(2,1)S(1)}, u32[]{:S(2)}, u32[]{:S(2)}) collective-permute-start(bf16[4,4,1120,128]{3,2,1,0:T(8,128)(2,1)} %get-tuple-element.165), channel_id=1, source_target_pairs={{0,16},{16,0},{1,17},{17,1},{2,18},{18,2},{3,19},{19,3},{4,20},{20... | collective-permute-start | bytes 13762568 | tf_op jit(solution)/shard_map/ppermute | solution.py:1119
  325.1 30.5 %collective-permute-start.33 = (bf16[4,560,128]{2,1,0:T(8,128)(2,1)}, bf16[4,560,128]{2,1,0:T(8,128)(2,1)S(1)}, u32[]{:S(2)}, u32[]{:S(2)}) collective-permute-start(bf16[4,560,128]{2,1,0:T(8,128)(2,1)} %get-tuple-element.162.refs_9_), channel_id=1, source_target_pairs={{0,2},{1,3},{2,0},{3,1},{4,6},{5,7},{6,4},{7,5},{8,10},{9,11},{10,... | collective-permute-start | bytes 1720328 | tf_op jit(solution)/shard_map/ppermute | solution.py:1115
  325.6 30.0 %collective-permute-start.34 = (bf16[4,560,128]{2,1,0:T(8,128)(2,1)}, bf16[4,560,128]{2,1,0:T(8,128)(2,1)S(1)}, u32[]{:S(2)}, u32[]{:S(2)}) collective-permute-start(bf16[4,560,128]{2,1,0:T(8,128)(2,1)} %get-tuple-element.164), channel_id=1, source_target_pairs={{0,1},{1,0},{2,3},{3,2},{4,5},{5,4},{6,7},{7,6},{8,9},{9,8},{10,11... | collective-permute-start | bytes 1720328 | tf_op jit(solution)/shard_map/ppermute | solution.py:1115
  340.5 44.8 %collective-permute-start.36 = (bf16[512,512]{1,0:T(8,128)(2,1)}, bf16[512,512]{1,0:T(8,128)(2,1)S(1)}, u32[]{:S(2)}, u32[]{:S(2)}) collective-permute-start(bf16[512,512]{1,0:T(8,128)(2,1)} %get-tuple-element.170), channel_id=1, source_target_pairs={{1,0},{2,1},{3,2},{5,4},{6,5},{7,6},{9,8},{10,9},{11,10},{13,12},{... | collective-permute-start | bytes 1572872 | tf_op jit(solution)/shard_map/ppermute | solution.py:1125
  351.0 30.1 %collective-permute-start.37 = (bf16[2,4,560,128]{3,2,1,0:T(8,128)(2,1)}, bf16[2,4,560,128]{3,2,1,0:T(8,128)(2,1)S(1)}, u32[]{:S(2)}, u32[]{:S(2)}) collective-permute-start(bf16[2,4,560,128]{3,2,1,0:T(8,128)(2,1)} %get-tuple-element.175), channel_id=1, source_target_pairs={{0,1},{1,0},{2,3},{3,2},{4,5},{5,4},{6,7},{7,6},{8,9},{9,8},{10,11... | collective-permute-start | bytes 3440648 | tf_op jit(solution)/shard_map/ppermute | solution.py:1115
  353.7 27.5 %collective-permute-start.38 = (bf16[2,4,560,128]{3,2,1,0:T(8,128)(2,1)}, bf16[2,4,560,128]{3,2,1,0:T(8,128)(2,1)S(1)}, u32[]{:S(2)}, u32[]{:S(2)}) collective-permute-start(bf16[2,4,560,128]{3,2,1,0:T(8,128)(2,1)} %get-tuple-element.177), channel_id=1, source_target_pairs={{0,2},{1,3},{2,0},{3,1},{4,6},{5,7},{6,4},{7,5},{8,10},{9,11},{10,... | collective-permute-start | bytes 3440648 | tf_op jit(solution)/shard_map/ppermute | solution.py:1115
  396.2 19.2 %collective-permute-start.56 = (bf16[2,1120,128]{2,1,0:T(8,128)(2,1)S(1)}, bf16[2,1120,128]{2,1,0:T(8,128)(2,1)S(1)}, u32[]{:S(2)}, u32[]{:S(2)}) collective-permute-start(bf16[2,1120,128]{2,1,0:T(8,128)(2,1)S(1)} %copy-done.61), channel_id=1, source_target_pairs={{0,4},{1,5},{2,6},{3,7},{4,0},{5,1},{6,2},{7,3},{8,12},{9,13},{10,... | collective-permute-start | bytes 1720328 | tf_op jit(solution)/shard_map/ppermute | solution.py:1115
  401.8 15.8 %collective-permute-start.40 = (bf16[4,560,128]{2,1,0:T(8,128)(2,1)S(1)}, bf16[4,560,128]{2,1,0:T(8,128)(2,1)S(1)}, u32[]{:S(2)}, u32[]{:S(2)}) collective-permute-start(bf16[4,560,128]{2,1,0:T(8,128)(2,1)S(1)} %copy-done.63), channel_id=1, source_target_pairs={{0,2},{1,3},{2,0},{3,1},{4,6},{5,7},{6,4},{7,5},{8,10},{9,11},{10,... | collective-permute-start | bytes 1720328 | tf_op jit(solution)/shard_map/ppermute | solution.py:1115
  403.3 15.8 %collective-permute-start.41 = (bf16[4,560,128]{2,1,0:T(8,128)(2,1)S(1)}, bf16[4,560,128]{2,1,0:T(8,128)(2,1)S(1)}, u32[]{:S(2)}, u32[]{:S(2)}) collective-permute-start(bf16[4,560,128]{2,1,0:T(8,128)(2,1)S(1)} %copy-done.62), channel_id=1, source_target_pairs={{0,1},{1,0},{2,3},{3,2},{4,5},{5,4},{6,7},{7,6},{8,9},{9,8},{10,11... | collective-permute-start | bytes 1720328 | tf_op jit(solution)/shard_map/ppermute | solution.py:1115
  411.4 17.9 %collective-permute-start.46 = (bf16[2,4,256,128]{3,2,1,0:T(8,128)(2,1)}, bf16[2,4,256,128]{3,2,1,0:T(8,128)(2,1)S(1)}, u32[]{:S(2)}, u32[]{:S(2)}) collective-permute-start(bf16[2,4,256,128]{3,2,1,0:T(8,128)(2,1)} %get-tuple-element.189), channel_id=1, source_target_pairs={{0,1},{1,0},{2,3},{3,2},{4,5},{5,4},{6,7},{7,6},{8,9},{9,8},{10,11... | collective-permute-start | bytes 1572872 | tf_op jit(solution)/shard_map/ppermute | solution.py:1115
  411.7 19.0 %collective-permute-start.47 = (bf16[2,4,256,128]{3,2,1,0:T(8,128)(2,1)}, bf16[2,4,256,128]{3,2,1,0:T(8,128)(2,1)S(1)}, u32[]{:S(2)}, u32[]{:S(2)}) collective-permute-start(bf16[2,4,256,128]{3,2,1,0:T(8,128)(2,1)} %get-tuple-element.191), channel_id=1, source_target_pairs={{0,2},{1,3},{2,0},{3,1},{4,6},{5,7},{6,4},{7,5},{8,10},{9,11},{10,... | collective-permute-start | bytes 1572872 | tf_op jit(solution)/shard_map/ppermute | solution.py:1115
  415.5 19.3 %collective-permute-start.57 = (bf16[1120,128]{1,0:T(8,128)(2,1)S(1)}, bf16[1120,128]{1,0:T(8,128)(2,1)S(1)}, u32[]{:S(2)}, u32[]{:S(2)}) collective-permute-start(bf16[1120,128]{1,0:T(8,128)(2,1)S(1)} %fusion.1), channel_id=1, source_target_pairs={{0,8},{1,9},{2,10},{3,11},{4,12},{5,13},{6,14},{7,15},{8,0},{9,1},... | collective-permute-start | bytes 860168 | tf_op jit(solution)/shard_map/ppermute | solution.py:1115
  423.9 22.8 %collective-permute-start.42 = (bf16[1120,128]{1,0:T(8,128)(2,1)}, bf16[1120,128]{1,0:T(8,128)(2,1)S(1)}, u32[]{:S(2)}, u32[]{:S(2)}) collective-permute-start(bf16[1120,128]{1,0:T(8,128)(2,1)} %get-tuple-element.183), channel_id=1, source_target_pairs={{0,4},{1,5},{2,6},{3,7},{4,0},{5,1},{6,2},{7,3},{8,12},{9,13},{10,... | collective-permute-start | bytes 860168 | tf_op jit(solution)/shard_map/ppermute | solution.py:1115
  423.9 26.9 %collective-permute-start.43 = (bf16[1120,128]{1,0:T(8,128)(2,1)}, bf16[1120,128]{1,0:T(8,128)(2,1)S(1)}, u32[]{:S(2)}, u32[]{:S(2)}) collective-permute-start(bf16[1120,128]{1,0:T(8,128)(2,1)} %get-tuple-element.184), channel_id=1, source_target_pairs={{0,8},{1,9},{2,10},{3,11},{4,12},{5,13},{6,14},{7,15},{8,0},{9,1},... | collective-permute-start | bytes 860168 | tf_op jit(solution)/shard_map/ppermute | solution.py:1115
  429.3 21.5 %collective-permute-start.44 = (bf16[1120,128]{1,0:T(8,128)(2,1)}, bf16[1120,128]{1,0:T(8,128)(2,1)S(1)}, u32[]{:S(2)}, u32[]{:S(2)}) collective-permute-start(bf16[1120,128]{1,0:T(8,128)(2,1)} %get-tuple-element.185), channel_id=1, source_target_pairs={{0,12},{1,13},{2,14},{3,15},{4,8},{5,9},{6,10},{7,11},{8,4},{9,5},... | collective-permute-start | bytes 860168 | tf_op jit(solution)/shard_map/ppermute | solution.py:1115
  441.0 27.6 %collective-permute-start.58 = (bf16[1120,128]{1,0:T(8,128)(2,1)S(1)}, bf16[1120,128]{1,0:T(8,128)(2,1)S(1)}, u32[]{:S(2)}, u32[]{:S(2)}) collective-permute-start(bf16[1120,128]{1,0:T(8,128)(2,1)S(1)} %fusion.refs_4_), channel_id=1, source_target_pairs={{0,1},{1,0},{2,3},{3,2},{4,5},{5,4},{6,7},{7,6},{8,9},{9,8},{10,11... | collective-permute-start | bytes 860168 | tf_op jit(solution)/shard_map/ppermute | solution.py:1115
  442.7 26.5 %collective-permute-start.59 = (bf16[1120,128]{1,0:T(8,128)(2,1)S(1)}, bf16[1120,128]{1,0:T(8,128)(2,1)S(1)}, u32[]{:S(2)}, u32[]{:S(2)}) collective-permute-start(bf16[1120,128]{1,0:T(8,128)(2,1)S(1)} %fusion.refs_4_), channel_id=1, source_target_pairs={{0,2},{1,3},{2,0},{3,1},{4,6},{5,7},{6,4},{7,5},{8,10},{9,11},{10,... | collective-permute-start | bytes 860168 | tf_op jit(solution)/shard_map/ppermute | solution.py:1115
  450.8 14.4 %collective-permute-start.51 = (bf16[512,128]{1,0:T(8,128)(2,1)}, bf16[512,128]{1,0:T(8,128)(2,1)S(1)}, u32[]{:S(2)}, u32[]{:S(2)}) collective-permute-start(bf16[512,128]{1,0:T(8,128)(2,1)} %get-tuple-element.196), channel_id=1, source_target_pairs={{0,8},{1,9},{2,10},{3,11},{4,12},{5,13},{6,14},{7,15},{8,0},{9,1},... | collective-permute-start | bytes 393224 | tf_op jit(solution)/shard_map/ppermute | solution.py:1115
  450.8 14.4 %collective-permute-start.52 = (bf16[512,128]{1,0:T(8,128)(2,1)}, bf16[512,128]{1,0:T(8,128)(2,1)S(1)}, u32[]{:S(2)}, u32[]{:S(2)}) collective-permute-start(bf16[512,128]{1,0:T(8,128)(2,1)} %get-tuple-element.197), channel_id=1, source_target_pairs={{0,12},{1,13},{2,14},{3,15},{4,8},{5,9},{6,10},{7,11},{8,4},{9,5},... | collective-permute-start | bytes 393224 | tf_op jit(solution)/shard_map/ppermute | solution.py:1115
  453.4 43.9 %collective-permute-start.39 = (bf16[2,512,640]{2,1,0:T(8,128)(2,1)}, bf16[2,512,640]{2,1,0:T(8,128)(2,1)}, u32[]{:S(2)}, u32[]{:S(2)}) collective-permute-start(bf16[2,512,640]{2,1,0:T(8,128)(2,1)} %get-tuple-element.274), channel_id=1, source_target_pairs={{0,16},{16,0},{1,17},{17,1},{2,18},{18,2},{3,19},{19,3},{4,20},{20... | collective-permute-start | bytes 3932168 | tf_op jit(solution)/shard_map/ppermute | solution.py:1119
  465.3 26.0 %collective-permute-start.53 = (bf16[1632,128]{1,0:T(8,128)(2,1)S(1)}, bf16[1632,128]{1,0:T(8,128)(2,1)S(1)}, u32[]{:S(2)}, u32[]{:S(2)}) collective-permute-start(bf16[1632,128]{1,0:T(8,128)(2,1)S(1)} %pad_maximum_fusion.2.refs_0_), channel_id=1, source_target_pairs={{0,1},{1,0},{2,3},{3,2},{4,5},{5,4},{6,7},{7,6},{8,9},{9,8},{10,11... | collective-permute-start | bytes 1253384 | tf_op jit(solution)/shard_map/ppermute | solution.py:1115
  467.6 24.6 %collective-permute-start.54 = (bf16[1632,128]{1,0:T(8,128)(2,1)S(1)}, bf16[1632,128]{1,0:T(8,128)(2,1)S(1)}, u32[]{:S(2)}, u32[]{:S(2)}) collective-permute-start(bf16[1632,128]{1,0:T(8,128)(2,1)S(1)} %pad_maximum_fusion.2.refs_0_), channel_id=1, source_target_pairs={{0,2},{1,3},{2,0},{3,1},{4,6},{5,7},{6,4},{7,5},{8,10},{9,11},{10,... | collective-permute-start | bytes 1253384 | tf_op jit(solution)/shard_map/ppermute | solution.py:1115
  468.6 23.6 %collective-permute-start.55 = (bf16[1632,128]{1,0:T(8,128)(2,1)S(1)}, bf16[1632,128]{1,0:T(8,128)(2,1)S(1)}, u32[]{:S(2)}, u32[]{:S(2)}) collective-permute-start(bf16[1632,128]{1,0:T(8,128)(2,1)S(1)} %pad_maximum_fusion.2.refs_0_), channel_id=1, source_target_pairs={{0,3},{1,2},{2,1},{3,0},{4,7},{5,6},{6,5},{7,4},{8,11},{9,10},{10,... | collective-permute-start | bytes 1253384 | tf_op jit(solution)/shard_map/ppermute | solution.py:1115
  469.2 22.1 %collective-permute-start.60 = (bf16[1120,128]{1,0:T(8,128)(2,1)S(1)}, bf16[1120,128]{1,0:T(8,128)(2,1)S(1)}, u32[]{:S(2)}, u32[]{:S(2)}) collective-permute-start(bf16[1120,128]{1,0:T(8,128)(2,1)S(1)} %fusion.refs_4_), channel_id=1, source_target_pairs={{0,3},{1,2},{2,1},{3,0},{4,7},{5,6},{6,5},{7,4},{8,11},{9,10},{10,... | collective-permute-start | bytes 860168 | tf_op jit(solution)/shard_map/ppermute | solution.py:1115
  (82 other events, 582.4 us)

commit v4 on v3

--- a/solution.py
+++ b/solution.py
@@ -92,7 +92,7 @@
 
 
 def cost(flops, nbytes):
-    return pl.CostEstimate(flops=int(flops) * 30, bytes_accessed=int(nbytes), transcendentals=0)
+    return pl.CostEstimate(flops=int(flops) * 400, bytes_accessed=int(nbytes), transcendentals=0)
 
 
 def whole(shape):

time: 517 us -> 513 us (level)
  local copies, waits for them, and re-layouts: 31.8 us -> 23.2 us
    unnamed x139 -> x111, local copies, waits for them, and re-layouts: 25.6 us -> 13.6 us
  transfers between devices with their start and end apart: 62 -> 62, of which waited for: 22 -> 22; matrix products, arithmetic and copies ran while one was open for 4% -> 5% of each run, Pallas kernels for 39% -> 39%
where the time goes in v4:
time: 513 us; the launch traced here: 504 us
  Pallas kernels  268 us (52%)
  waiting for transfers between devices  112 us (22%)
  starting transfers between devices  82 us (16%)
  local copies, waits for them, and re-layouts  23.2 us (5%)
  other arithmetic  17.6 us (3%)
    ppermute x47, waiting for transfers between devices, moved(): return lax.ppermute(array, AXES, pairs)  112 us
    ppermute x47, starting transfers between devices, moved(): return lax.ppermute(array, AXES, pairs)  71.6 us
    pallas_call x2, Pallas kernels, ffn_back_call(): pl.pallas_call(ffn_back_kernel, grid_spec=pltpu.PrefetchScalarGridSpec(nu...  52.7 us
    pallas_call x2, Pallas kernels, attn_back_call(): pl.pallas_call(held_back(attn_back_kernel, 9, len(deps)), grid=(tok // QB...  29.3 us
    pallas_call x2, Pallas kernels, ffn_call(): pl.pallas_call(held_back(ffn_kernel, 7, len(deps)), grid=(ff // FC,), in_...  27.3 us
    pallas_call x12, Pallas kernels, joined(): pl.pallas_call(body, in_specs=[pl.BlockSpec(memory_space=pltpu.VMEM)] * l...  26.8 us
    pallas_call x3, Pallas kernels, add_split(): pl.pallas_call(add_split_kernel, grid_spec=pltpu.PrefetchScalarGridSpec(n...  19.3 us
    pallas_call x2, Pallas kernels, place_ffn(): pl.pallas_call(partial(place_ffn_kernel, layer), grid_spec=pltpu.Prefetch...  16.3 us
  transfers between devices with their start and end apart: 62, of which 22 were waited for; matrix products, arithmetic and copies ran while one was open for 5% of the time, Pallas kernels for 39%

profile of v4, /device:TPU:0, one launch (start us, length us, event | category | flops | bytes accessed | tf_op | source)
XLA Modules:
  0.0 504.3 jit_solution(6469921831701278383)
XLA Ops:
  0.7 4.1 pack_ffn.1.dep_ref.own_ref
  18.2 3.5 collective-permute-start.5
  21.9 3.3 collective-permute-done.1.refs_1_
  25.2 7.4 %collective-permute-done.4.refs_4_.refs_5_.refs_0_ = bf16[1,1120,128]{2,1,0:T(8,128)(2,1)S(1)} collective-permute-done((bf16[1,1120,128]{2,1,0:T(8,128)(2,1)}, bf16[1,1120,128]{2,1,0:T(8,128)(2,1)S(1)}, u32[]{:S(2)}, u32[]{:S(2)}) %collective-permute-start.4) | collective-permute-done | bytes 286752 | tf_op jit(solution)/shard_map/ppermute | solution.py:1115
  32.6 7.0 %collective-permute-done.5.refs_5_.refs_6_.refs_1_ = bf16[1,1120,128]{2,1,0:T(8,128)(2,1)S(1)} collective-permute-done((bf16[1,1120,128]{2,1,0:T(8,128)(2,1)}, bf16[1,1120,128]{2,1,0:T(8,128)(2,1)S(1)}, u32[]{:S(2)}, u32[]{:S(2)}) %collective-permute-start.5) | collective-permute-done | bytes 286752 | tf_op jit(solution)/shard_map/ppermute | solution.py:1115
  49.6 5.1 %collective-permute-done.8.refs_1_.refs_7_.refs_2_ = bf16[1,1120,128]{2,1,0:T(8,128)(2,1)S(1)} collective-permute-done((bf16[1,1120,128]{2,1,0:T(8,128)(2,1)S(1)}, bf16[1,1120,128]{2,1,0:T(8,128)(2,1)S(1)}, u32[]{:S(2)}, u32[]{:S(2)}) %collective-permute-start.8) | collective-permute-done | bytes 286752 | tf_op jit(solution)/shard_map/ppermute | solution.py:1115
  75.9 3.9 collective-permute-start.13
  85.0 5.3 %place_qkv.1 = (bf16[2,640,1536]{2,1,0:T(8,128)(2,1)}, bf16[2,4,32,128]{3,2,1,0:T(8,128)(2,1)}) custom-call(s32[3]{0:T(128)} %pad_add_fusion.spot, bf16[16,512,128]{2,1,0:T(8,128)(2,1)} %joined.15.own_ref.refs_3_, bf16[16,512,128]{2,1,0:T(8,128)(2,1)} %copy-done.7), custom_call_target="tpu_custom_call" | custom-call | bytes 8000000 | tf_op jit(solution)/shard_map/place_qkv/pallas_call | solution.py:759
  93.4 3.0 keys_values.2
  96.4 4.8 queries.2
  107.8 3.1 collective-permute-start.12
  116.2 3.3 joined.17.near_ref
  121.4 5.5 %collective-permute-done.18 = bf16[3,560,128]{2,1,0:T(8,128)(2,1)S(1)} collective-permute-done((bf16[3,560,128]{2,1,0:T(8,128)(2,1)}, bf16[3,560,128]{2,1,0:T(8,128)(2,1)S(1)}, u32[]{:S(2)}, u32[]{:S(2)}) %collective-permute-start.18) | collective-permute-done | bytes 430112 | tf_op jit(solution)/shard_map/ppermute | solution.py:1115
  127.7 4.6 collective-permute-done.19
  134.0 6.4 %attend.2.refs_0_.refs_3_.o_ref = bf16[512,1024]{1,0:T(8,128)(2,1)} custom-call(bf16[512,1024]{1,0:T(8,128)(2,1)} %get-tuple-element.116.refs_0_.refs_1_, bf16[512,512]{1,0:T(8,128)(2,1)} %copy-done.53, bf16[512,512]{1,0:T(8,128)(2,1)} %get-tuple-element.117.refs_2_.refs_4_, s32[512,1]{1,0:T(8,128)} %subtract_add_fusion.refs_10_.refs_3_, ...), custom_call_target="tpu_custom_call" | custom-call | flops 536870912000 | bytes 3000000 | tf_op jit(solution)/shard_map/attend/pallas_call | solution.py:203
  143.6 8.2 %place_ffn.2 = (bf16[640,2048]{1,0:T(8,128)(2,1)}, bf16[640,2048]{1,0:T(8,128)(2,1)}, bf16[4,4,128,640]{3,2,1,0:T(8,128)(2,1)}, bf16[4,4,64,640]{3,2,1,0:T(8,128)(2,1)}) custom-call(s32[3]{0:T(128)} %pad_add_fusion.spot, bf16[4,2,1120,128]{3,2,1,0:T(8,128)(2,1)} %bitcast.61, bf16[4,2,1120,128]{3,2,1,0:T(8,128)(2,1)} %bitcast.12.other_ref, ...), custom_call_target="tpu_custom_call" | custom-call | bytes 18000000 | tf_op jit(solution)/shard_map/place_ffn/pallas_call | solution.py:845
  151.8 13.7 %feed_forward.2 = (f32[512,640]{1,0:T(8,128)}, f32[512,640]{1,0:T(8,128)}, bf16[512,2048]{1,0:T(8,128)(2,1)}, bf16[512,2048]{1,0:T(8,128)(2,1)}, f32[512,640]{1,0:T(8,128)}, /*index=5*/bf16[512,640]{1,0:T(8,128)(2,1)}) custom-call(bf16[512,1024]{1,0:T(8,128)(2,1)} %attend.2.refs_0_.refs_3_.o_ref, bf16[512,640]{1,0:T(8,128)(2,1)} %dynamic-slice_bitcast_fusion.1.x_ref.refs_1_, ...), custom_call_target="tpu_custom_call" | custom-call | flops 1879048192000 | bytes 22000000 | tf_op jit(solution)/shard_map/feed_forward/pallas_call | solution.py:266
  165.4 3.0 keys_values.3
  168.5 3.7 collective-permute-start.22
  177.3 4.8 queries.3
  182.1 3.3 joined.23.near_ref
  185.5 7.9 %collective-permute-done.24 = bf16[3,560,128]{2,1,0:T(8,128)(2,1)} collective-permute-done((bf16[3,560,128]{2,1,0:T(8,128)(2,1)}, bf16[3,560,128]{2,1,0:T(8,128)(2,1)}, u32[]{:S(2)}, u32[]{:S(2)}) %collective-permute-start.24) | collective-permute-done | bytes 430112 | tf_op jit(solution)/shard_map/ppermute | solution.py:1115
  197.1 6.4 %attend.3.refs_0_.o_ref = bf16[512,1024]{1,0:T(8,128)(2,1)} custom-call(bf16[512,1024]{1,0:T(8,128)(2,1)} %get-tuple-element.124.refs_0_, bf16[512,512]{1,0:T(8,128)(2,1)} %collective-permute-done.22.refs_1_.refs_3_, bf16[512,512]{1,0:T(8,128)(2,1)} %get-tuple-element.125.refs_2_.refs_4_, s32[512,1]{1,0:T(8,128)} %subtract_add_fusion.refs_10_.refs_3_, ...), custom_call_target="tpu_custom_call" | custom-call | flops 536870912000 | bytes 3000000 | tf_op jit(solution)/shard_map/attend/pallas_call | solution.py:203
  203.5 8.2 %place_ffn.3 = (bf16[640,2048]{1,0:T(8,128)(2,1)}, bf16[640,2048]{1,0:T(8,128)(2,1)}, bf16[4,4,128,640]{3,2,1,0:T(8,128)(2,1)}, bf16[4,4,64,640]{3,2,1,0:T(8,128)(2,1)}) custom-call(s32[3]{0:T(128)} %pad_add_fusion.spot, bf16[4,2,1120,128]{3,2,1,0:T(8,128)(2,1)} %bitcast.62, bf16[4,2,1120,128]{3,2,1,0:T(8,128)(2,1)} %bitcast.12.other_ref, ...), custom_call_target="tpu_custom_call" | custom-call | bytes 18000000 | tf_op jit(solution)/shard_map/place_ffn/pallas_call | solution.py:845
  211.7 13.7 %feed_forward.3 = (f32[512,640]{1,0:T(8,128)}, f32[512,640]{1,0:T(8,128)}, bf16[512,2048]{1,0:T(8,128)(2,1)}, bf16[512,2048]{1,0:T(8,128)(2,1)}, f32[512,640]{1,0:T(8,128)}, /*index=5*/bf16[512,640]{1,0:T(8,128)(2,1)}) custom-call(bf16[512,1024]{1,0:T(8,128)(2,1)} %attend.3.refs_0_.o_ref, bf16[512,640]{1,0:T(8,128)(2,1)} %get-tuple-element.122.x_ref.refs_1_, ...), custom_call_target="tpu_custom_call" | custom-call | flops 1879048192000 | bytes 22000000 | tf_op jit(solution)/shard_map/feed_forward/pallas_call | solution.py:266
  225.3 26.5 %feed_forward_back.2 = (bf16[4,4,1120,128]{3,2,1,0:T(8,128)(2,1)}, bf16[4,4,1120,128]{3,2,1,0:T(8,128)(2,1)}, f32[512,640]{1,0:T(8,128)}, bf16[512,1024]{1,0:T(8,128)(2,1)}, f32[8,640]{1,0:T(8,128)}) custom-call(s32[3]{0:T(128)} %pad_add_fusion.spot, bf16[512,640]{1,0:T(8,128)(2,1)} %dynamic-slice_bitcast_fusion.c_ref, f32[512,640]{1,0:T(8,128)} %get-tuple-element.130.z_ref, ...), custom_call_target="tpu_custom_call" | custom-call | flops 3758096384000 | bytes 35000000 | tf_op jit(solution)/shard_map/feed_forward_back/pallas_call | solution.py:387
  252.4 14.5 %attend_back.2 = (bf16[512,1024]{1,0:T(8,128)(2,1)}, bf16[512,512]{1,0:T(8,128)(2,1)}, f32[512,512]{1,0:T(8,128)}, f32[8,256]{1,0:T(8,128)}) custom-call(bf16[512,1024]{1,0:T(8,128)(2,1)} %get-tuple-element.124.refs_0_, bf16[512,1024]{1,0:T(8,128)(2,1)} %get-tuple-element.136.refs_1_, bf16[512,1024]{1,0:T(8,128)(2,1)} %get-tuple-element.137.refs_2_, ...), custom_call_target="tpu_custom_call" | custom-call | flops 1342177280000 | bytes 8000000 | tf_op jit(solution)/shard_map/attend_back/pallas_call | solution.py:480
  268.2 7.3 %add_split.3 = (bf16[2,4,560,128]{3,2,1,0:T(8,128)(2,1)}, bf16[2,4,560,128]{3,2,1,0:T(8,128)(2,1)}, bf16[2,4,560,128]{3,2,1,0:T(8,128)(2,1)}, bf16[2,4,560,128]{3,2,1,0:T(8,128)(2,1)}) custom-call(s32[3]{0:T(128)} %pad_add_fusion.spot, bf16[4,4,1120,128]{3,2,1,0:T(8,128)(2,1)} %get-tuple-element.139.first_ref, ...), custom_call_target="tpu_custom_call" | custom-call | bytes 13762560 | tf_op jit(solution)/shard_map/add_split/pallas_call | solution.py:887
  278.2 3.3 collective-permute-start.32
  281.5 4.6 queries_back.2
  286.1 6.7 %keys_values_back.2 = (bf16[4,4,512,128]{3,2,1,0:T(8,128)(2,1)}, bf16[512,640]{1,0:T(8,128)(2,1)}) custom-call(bf16[512,640]{1,0:T(8,128)(2,1)} %get-tuple-element.123.a_ref.refs_0_, bf16[512,640]{1,0:T(8,128)(2,1)} %get-tuple-element.122.x_ref.refs_1_, f32[512,640]{1,0:T(8,128)} %get-tuple-element.135.refs_2_, f32[512,640]{1,0:T(8,128)} %get-tuple-element.142.refs_3_, ...), custom_call_target="tpu_custom_call" | custom-call | flops 268435456000 | bytes 10000000 | tf_op jit(solution)/shard_map/keys_values_back/pallas_call | solution.py:590
  292.8 26.2 %feed_forward_back.3 = (bf16[4,4,1120,128]{3,2,1,0:T(8,128)(2,1)}, bf16[4,4,1120,128]{3,2,1,0:T(8,128)(2,1)}, f32[512,640]{1,0:T(8,128)}, bf16[512,1024]{1,0:T(8,128)(2,1)}, f32[8,640]{1,0:T(8,128)}) custom-call(s32[3]{0:T(128)} %pad_add_fusion.spot, bf16[512,640]{1,0:T(8,128)(2,1)} %get-tuple-element.149.c_ref, f32[512,640]{1,0:T(8,128)} %get-tuple-element.150.z_ref, ...), custom_call_target="tpu_custom_call" | custom-call | flops 3758096384000 | bytes 35000000 | tf_op jit(solution)/shard_map/feed_forward_back/pallas_call | solution.py:387
  322.1 14.8 %attend_back.3 = (bf16[512,1024]{1,0:T(8,128)(2,1)}, bf16[512,512]{1,0:T(8,128)(2,1)}, f32[512,512]{1,0:T(8,128)}, f32[8,256]{1,0:T(8,128)}) custom-call(bf16[512,1024]{1,0:T(8,128)(2,1)} %get-tuple-element.116.refs_0_.refs_1_, bf16[512,1024]{1,0:T(8,128)(2,1)} %get-tuple-element.156.refs_1_, bf16[512,1024]{1,0:T(8,128)(2,1)} %get-tuple-element.157.refs_2_, ...), custom_call_target="tpu_custom_call" | custom-call | flops 1342177280000 | bytes 8000000 | tf_op jit(solution)/shard_map/attend_back/pallas_call | solution.py:480
  338.2 7.0 %add_split.4 = (bf16[2,4,560,128]{3,2,1,0:T(8,128)(2,1)}, bf16[2,4,560,128]{3,2,1,0:T(8,128)(2,1)}, bf16[2,4,560,128]{3,2,1,0:T(8,128)(2,1)}, bf16[2,4,560,128]{3,2,1,0:T(8,128)(2,1)}) custom-call(s32[3]{0:T(128)} %pad_add_fusion.spot, bf16[4,4,1120,128]{3,2,1,0:T(8,128)(2,1)} %get-tuple-element.161.refs_0_.first_ref, ...), custom_call_target="tpu_custom_call" | custom-call | bytes 13762560 | tf_op jit(solution)/shard_map/add_split/pallas_call | solution.py:887
  350.5 3.9 sum_parts.3
  354.4 4.6 queries_back.3
  359.0 18.7 %collective-permute-done.37.b_ref.a1 = bf16[2,4,560,128]{3,2,1,0:T(8,128)(2,1)} collective-permute-done((bf16[2,4,560,128]{3,2,1,0:T(8,128)(2,1)}, bf16[2,4,560,128]{3,2,1,0:T(8,128)(2,1)}, u32[]{:S(2)}, u32[]{:S(2)}) %collective-permute-start.37) | collective-permute-done | bytes 1146912 | tf_op jit(solution)/shard_map/ppermute | solution.py:1115
  380.5 6.7 %keys_values_back.3 = (bf16[4,4,512,128]{3,2,1,0:T(8,128)(2,1)}, bf16[512,640]{1,0:T(8,128)(2,1)}) custom-call(bf16[512,640]{1,0:T(8,128)(2,1)} %get-tuple-element.115.a_ref.refs_0_, bf16[512,640]{1,0:T(8,128)(2,1)} %dynamic-slice_bitcast_fusion.1.x_ref.refs_1_, f32[512,640]{1,0:T(8,128)} %get-tuple-element.155.refs_2_, ...), custom_call_target="tpu_custom_call" | custom-call | flops 268435456000 | bytes 10000000 | tf_op jit(solution)/shard_map/keys_values_back/pallas_call | solution.py:590
  387.2 4.0 broadcast_select_fusion
  391.2 5.3 %collective-permute-start.56 = (bf16[2,1120,128]{2,1,0:T(8,128)(2,1)S(1)}, bf16[2,1120,128]{2,1,0:T(8,128)(2,1)S(1)}, u32[]{:S(2)}, u32[]{:S(2)}) collective-permute-start(bf16[2,1120,128]{2,1,0:T(8,128)(2,1)S(1)} %copy-done.49), channel_id=1, source_target_pairs={{0,4},{1,5},{2,6},{3,7},{4,0},{5,1},{6,2},{7,3},{8,12},{9,13},{10,... | collective-permute-start | bytes 1720328 | tf_op jit(solution)/shard_map/ppermute | solution.py:1115
  401.0 4.9 add_split.5
  414.9 4.0 sum_parts.4
  420.9 3.3 collective-permute-done.46.b_ref.a1
  429.7 9.6 %collective-permute-done.57 = bf16[1120,128]{1,0:T(8,128)(2,1)S(1)} collective-permute-done((bf16[1120,128]{1,0:T(8,128)(2,1)S(1)}, bf16[1120,128]{1,0:T(8,128)(2,1)S(1)}, u32[]{:S(2)}, u32[]{:S(2)}) %collective-permute-start.57) | collective-permute-done | bytes 286752 | tf_op jit(solution)/shard_map/ppermute | solution.py:1115
  456.8 3.9 collective-permute-done.51
  466.9 18.3 %collective-permute-done.60.refs_7_ = bf16[1120,128]{1,0:T(8,128)(2,1)S(1)} collective-permute-done((bf16[1120,128]{1,0:T(8,128)(2,1)S(1)}, bf16[1120,128]{1,0:T(8,128)(2,1)S(1)}, u32[]{:S(2)}, u32[]{:S(2)}) %collective-permute-start.60) | collective-permute-done | bytes 286752 | tf_op jit(solution)/shard_map/ppermute | solution.py:1115
  487.6 3.5 choose_ring.1
  496.1 5.8 %finish.1 = (f32[1,160,2048]{2,1,0:T(8,128)}, f32[1,160,2048]{2,1,0:T(8,128)}, f32[1,512,640]{2,1,0:T(8,128)}, f32[1,256,640]{2,1,0:T(8,128)}, f32[1,160,1024]{2...) custom-call(s32[3]{0:T(128)} %pad_add_fusion.spot, ...), custom_call_target="tpu_custom_call" | custom-call | bytes 12000000 | tf_op jit(solution)/shard_map/finish/pallas_call | solution.py:1043
  (296 shorter events, 151.8 us)
Async XLA Ops:
  12.1 13.1 %collective-permute-start.1 = (bf16[1,512,128]{2,1,0:T(8,128)(2,1)}, bf16[1,512,128]{2,1,0:T(8,128)(2,1)S(1)}, u32[]{:S(2)}, u32[]{:S(2)}) collective-permute-start(bf16[1,512,128]{2,1,0:T(8,128)(2,1)} %get-tuple-element.112), channel_id=1, source_target_pairs={{0,8},{1,9},{2,10},{3,11},{4,12},{5,13},{6,14},{7,15},{8,0},{9,1},... | collective-permute-start | bytes 393224 | tf_op jit(solution)/shard_map/ppermute | solution.py:1115
  17.3 15.3 %collective-permute-start.4 = (bf16[1,1120,128]{2,1,0:T(8,128)(2,1)}, bf16[1,1120,128]{2,1,0:T(8,128)(2,1)S(1)}, u32[]{:S(2)}, u32[]{:S(2)}) collective-permute-start(bf16[1,1120,128]{2,1,0:T(8,128)(2,1)} %half_quarter.2.refs_3_), channel_id=1, source_target_pairs={{0,4},{1,5},{2,6},{3,7},{4,0},{5,1},{6,2},{7,3},{8,12},{9,13},{10,... | collective-permute-start | bytes 860168 | tf_op jit(solution)/shard_map/ppermute | solution.py:1115
  18.2 21.5 %collective-permute-start.5 = (bf16[1,1120,128]{2,1,0:T(8,128)(2,1)}, bf16[1,1120,128]{2,1,0:T(8,128)(2,1)S(1)}, u32[]{:S(2)}, u32[]{:S(2)}) collective-permute-start(bf16[1,1120,128]{2,1,0:T(8,128)(2,1)} %half_quarter.2.refs_3_), channel_id=1, source_target_pairs={{0,8},{1,9},{2,10},{3,11},{4,12},{5,13},{6,14},{7,15},{8,0},{9,1},... | collective-permute-start | bytes 860168 | tf_op jit(solution)/shard_map/ppermute | solution.py:1115
  42.2 12.5 %collective-permute-start.6 = (bf16[3,512,128]{2,1,0:T(8,128)(2,1)}, bf16[3,512,128]{2,1,0:T(8,128)(2,1)S(1)}, u32[]{:S(2)}, u32[]{:S(2)}) collective-permute-start(bf16[3,512,128]{2,1,0:T(8,128)(2,1)} %joined.12.refs_1_), channel_id=1, source_target_pairs={{0,1},{1,0},{2,3},{3,2},{4,5},{5,4},{6,7},{7,6},{8,9},{9,8},{10,11... | collective-permute-start | bytes 1179656 | tf_op jit(solution)/shard_map/ppermute | solution.py:1115
  43.7 14.7 %collective-permute-start.7 = (bf16[3,512,128]{2,1,0:T(8,128)(2,1)}, bf16[3,512,128]{2,1,0:T(8,128)(2,1)S(1)}, u32[]{:S(2)}, u32[]{:S(2)}) collective-permute-start(bf16[3,512,128]{2,1,0:T(8,128)(2,1)} %joined.12.refs_1_), channel_id=1, source_target_pairs={{0,2},{1,3},{2,0},{3,1},{4,6},{5,7},{6,4},{7,5},{8,10},{9,11},{10,... | collective-permute-start | bytes 1179656 | tf_op jit(solution)/shard_map/ppermute | solution.py:1115
  70.4 13.3 %collective-permute-start.11 = (bf16[16,512,128]{2,1,0:T(8,128)(2,1)}, bf16[16,512,128]{2,1,0:T(8,128)(2,1)S(1)}, u32[]{:S(2)}, u32[]{:S(2)}) collective-permute-start(bf16[16,512,128]{2,1,0:T(8,128)(2,1)} %joined.15.own_ref.refs_3_), channel_id=1, source_target_pairs={{0,16},{16,0},{1,17},{17,1},{2,18},{18,2},{3,19},{19,3},{4,20},{20... | collective-permute-start | bytes 6291464 | tf_op jit(solution)/shard_map/ppermute | solution.py:1119
  75.9 25.4 %collective-permute-start.13 = (bf16[1,1120,128]{2,1,0:T(8,128)(2,1)}, bf16[1,1120,128]{2,1,0:T(8,128)(2,1)}, u32[]{:S(2)}, u32[]{:S(2)}) collective-permute-start(bf16[1,1120,128]{2,1,0:T(8,128)(2,1)} %half_quarter.3), channel_id=1, source_target_pairs={{0,4},{1,5},{2,6},{3,7},{4,0},{5,1},{6,2},{7,3},{8,12},{9,13},{10,... | collective-permute-start | bytes 860168 | tf_op jit(solution)/shard_map/ppermute | solution.py:1115
  79.8 23.2 %collective-permute-start.14 = (bf16[1,1120,128]{2,1,0:T(8,128)(2,1)}, bf16[1,1120,128]{2,1,0:T(8,128)(2,1)}, u32[]{:S(2)}, u32[]{:S(2)}) collective-permute-start(bf16[1,1120,128]{2,1,0:T(8,128)(2,1)} %half_quarter.3), channel_id=1, source_target_pairs={{0,8},{1,9},{2,10},{3,11},{4,12},{5,13},{6,14},{7,15},{8,0},{9,1},... | collective-permute-start | bytes 860168 | tf_op jit(solution)/shard_map/ppermute | solution.py:1115
  79.8 23.2 %collective-permute-start.15 = (bf16[1,1120,128]{2,1,0:T(8,128)(2,1)}, bf16[1,1120,128]{2,1,0:T(8,128)(2,1)}, u32[]{:S(2)}, u32[]{:S(2)}) collective-permute-start(bf16[1,1120,128]{2,1,0:T(8,128)(2,1)} %half_quarter.3), channel_id=1, source_target_pairs={{0,12},{1,13},{2,14},{3,15},{4,8},{5,9},{6,10},{7,11},{8,4},{9,5},... | collective-permute-start | bytes 860168 | tf_op jit(solution)/shard_map/ppermute | solution.py:1115
  82.2 28.7 %collective-permute-start.17 = (bf16[3,1120,128]{2,1,0:T(8,128)(2,1)}, bf16[3,1120,128]{2,1,0:T(8,128)(2,1)}, u32[]{:S(2)}, u32[]{:S(2)}) collective-permute-start(bf16[3,1120,128]{2,1,0:T(8,128)(2,1)} %joined.16.refs_0_), channel_id=1, source_target_pairs={{0,2},{1,3},{2,0},{3,1},{4,6},{5,7},{6,4},{7,5},{8,10},{9,11},{10,... | collective-permute-start | bytes 2580488 | tf_op jit(solution)/shard_map/ppermute | solution.py:1115
  83.7 21.0 %collective-permute-start.16 = (bf16[3,1120,128]{2,1,0:T(8,128)(2,1)}, bf16[3,1120,128]{2,1,0:T(8,128)(2,1)}, u32[]{:S(2)}, u32[]{:S(2)}) collective-permute-start(bf16[3,1120,128]{2,1,0:T(8,128)(2,1)} %joined.16.refs_0_), channel_id=1, source_target_pairs={{0,1},{1,0},{2,3},{3,2},{4,5},{5,4},{6,7},{7,6},{8,9},{9,8},{10,11... | collective-permute-start | bytes 2580488 | tf_op jit(solution)/shard_map/ppermute | solution.py:1115
  106.7 20.2 %collective-permute-start.18 = (bf16[3,560,128]{2,1,0:T(8,128)(2,1)}, bf16[3,560,128]{2,1,0:T(8,128)(2,1)S(1)}, u32[]{:S(2)}, u32[]{:S(2)}) collective-permute-start(bf16[3,560,128]{2,1,0:T(8,128)(2,1)} %joined.18), channel_id=1, source_target_pairs={{0,2},{1,3},{2,0},{3,1},{4,6},{5,7},{6,4},{7,5},{8,10},{9,11},{10,... | collective-permute-start | bytes 1290248 | tf_op jit(solution)/shard_map/ppermute | solution.py:1115
  107.8 25.4 %collective-permute-start.12 = (bf16[512,512]{1,0:T(8,128)(2,1)S(1)}, bf16[512,512]{1,0:T(8,128)(2,1)S(1)}, u32[]{:S(2)}, u32[]{:S(2)}) collective-permute-start(bf16[512,512]{1,0:T(8,128)(2,1)S(1)} %copy-done.52), channel_id=1, source_target_pairs={{0,1},{1,2},{2,3},{4,5},{5,6},{6,7},{8,9},{9,10},{10,11},{12,13},{... | collective-permute-start | bytes 1572872 | tf_op jit(solution)/shard_map/ppermute | solution.py:1125
  112.8 19.5 %collective-permute-start.19 = (bf16[3,560,128]{2,1,0:T(8,128)(2,1)}, bf16[3,560,128]{2,1,0:T(8,128)(2,1)S(1)}, u32[]{:S(2)}, u32[]{:S(2)}) collective-permute-start(bf16[3,560,128]{2,1,0:T(8,128)(2,1)} %joined.19), channel_id=1, source_target_pairs={{0,1},{1,0},{2,3},{3,2},{4,5},{5,4},{6,7},{7,6},{8,9},{9,8},{10,11... | collective-permute-start | bytes 1290248 | tf_op jit(solution)/shard_map/ppermute | solution.py:1115
  119.5 24.1 %collective-permute-start.20 = (bf16[9,1120,128]{2,1,0:T(8,128)(2,1)}, bf16[9,1120,128]{2,1,0:T(8,128)(2,1)}, u32[]{:S(2)}, u32[]{:S(2)}) collective-permute-start(bf16[9,1120,128]{2,1,0:T(8,128)(2,1)} %joined.17.near_ref), channel_id=1, source_target_pairs={{0,16},{16,0},{1,17},{17,1},{2,18},{18,2},{3,19},{19,3},{4,20},{20... | collective-permute-start | bytes 7741448 | tf_op jit(solution)/shard_map/ppermute | solution.py:1119
  142.5 32.2 %collective-permute-start.23 = (bf16[3,1120,128]{2,1,0:T(8,128)(2,1)}, bf16[3,1120,128]{2,1,0:T(8,128)(2,1)}, u32[]{:S(2)}, u32[]{:S(2)}) collective-permute-start(bf16[3,1120,128]{2,1,0:T(8,128)(2,1)} %joined.20.refs_0_), channel_id=1, source_target_pairs={{0,1},{1,0},{2,3},{3,2},{4,5},{5,4},{6,7},{7,6},{8,9},{9,8},{10,11... | collective-permute-start | bytes 2580488 | tf_op jit(solution)/shard_map/ppermute | solution.py:1115
  142.5 29.6 %collective-permute-start.25 = (bf16[3,1120,128]{2,1,0:T(8,128)(2,1)}, bf16[3,1120,128]{2,1,0:T(8,128)(2,1)}, u32[]{:S(2)}, u32[]{:S(2)}) collective-permute-start(bf16[3,1120,128]{2,1,0:T(8,128)(2,1)} %joined.20.refs_0_), channel_id=1, source_target_pairs={{0,2},{1,3},{2,0},{3,1},{4,6},{5,7},{6,4},{7,5},{8,10},{9,11},{10,... | collective-permute-start | bytes 2580488 | tf_op jit(solution)/shard_map/ppermute | solution.py:1115
  168.5 28.6 %collective-permute-start.22 = (bf16[512,512]{1,0:T(8,128)(2,1)}, bf16[512,512]{1,0:T(8,128)(2,1)}, u32[]{:S(2)}, u32[]{:S(2)}) collective-permute-start(bf16[512,512]{1,0:T(8,128)(2,1)} %get-tuple-element.125.refs_2_.refs_4_), channel_id=1, source_target_pairs={{0,1},{1,2},{2,3},{4,5},{5,6},{6,7},{8,9},{9,10},{10,11},{12,13},{... | collective-permute-start | bytes 1572872 | tf_op jit(solution)/shard_map/ppermute | solution.py:1125
  174.1 21.1 %collective-permute-start.26 = (bf16[3,560,128]{2,1,0:T(8,128)(2,1)}, bf16[3,560,128]{2,1,0:T(8,128)(2,1)}, u32[]{:S(2)}, u32[]{:S(2)}) collective-permute-start(bf16[3,560,128]{2,1,0:T(8,128)(2,1)} %joined.22), channel_id=1, source_target_pairs={{0,1},{1,0},{2,3},{3,2},{4,5},{5,4},{6,7},{7,6},{8,9},{9,8},{10,11... | collective-permute-start | bytes 1290248 | tf_op jit(solution)/shard_map/ppermute | solution.py:1115
  176.7 16.6 %collective-permute-start.24 = (bf16[3,560,128]{2,1,0:T(8,128)(2,1)}, bf16[3,560,128]{2,1,0:T(8,128)(2,1)}, u32[]{:S(2)}, u32[]{:S(2)}) collective-permute-start(bf16[3,560,128]{2,1,0:T(8,128)(2,1)} %joined.21), channel_id=1, source_target_pairs={{0,2},{1,3},{2,0},{3,1},{4,6},{5,7},{6,4},{7,5},{8,10},{9,11},{10,... | collective-permute-start | bytes 1290248 | tf_op jit(solution)/shard_map/ppermute | solution.py:1115
  185.4 18.1 %collective-permute-start.27 = (bf16[9,1120,128]{2,1,0:T(8,128)(2,1)}, bf16[9,1120,128]{2,1,0:T(8,128)(2,1)}, u32[]{:S(2)}, u32[]{:S(2)}) collective-permute-start(bf16[9,1120,128]{2,1,0:T(8,128)(2,1)} %joined.23.near_ref), channel_id=1, source_target_pairs={{0,16},{16,0},{1,17},{17,1},{2,18},{18,2},{3,19},{19,3},{4,20},{20... | collective-permute-start | bytes 7741448 | tf_op jit(solution)/shard_map/ppermute | solution.py:1119
  251.8 16.4 %collective-permute-start.29 = (bf16[4,4,1120,128]{3,2,1,0:T(8,128)(2,1)}, bf16[4,4,1120,128]{3,2,1,0:T(8,128)(2,1)}, u32[]{:S(2)}, u32[]{:S(2)}) collective-permute-start(bf16[4,4,1120,128]{3,2,1,0:T(8,128)(2,1)} %get-tuple-element.140), channel_id=1, source_target_pairs={{0,16},{16,0},{1,17},{17,1},{2,18},{18,2},{3,19},{19,3},{4,20},{20... | collective-permute-start | bytes 13762568 | tf_op jit(solution)/shard_map/ppermute | solution.py:1119
  266.9 19.2 %collective-permute-start.30 = (bf16[512,512]{1,0:T(8,128)(2,1)}, bf16[512,512]{1,0:T(8,128)(2,1)}, u32[]{:S(2)}, u32[]{:S(2)}) collective-permute-start(bf16[512,512]{1,0:T(8,128)(2,1)} %get-tuple-element.144), channel_id=1, source_target_pairs={{1,0},{2,1},{3,2},{5,4},{6,5},{7,6},{9,8},{10,9},{11,10},{13,12},{... | collective-permute-start | bytes 1572872 | tf_op jit(solution)/shard_map/ppermute | solution.py:1125
  275.5 43.6 %collective-permute-start.31 = (bf16[2,4,560,128]{3,2,1,0:T(8,128)(2,1)}, bf16[2,4,560,128]{3,2,1,0:T(8,128)(2,1)}, u32[]{:S(2)}, u32[]{:S(2)}) collective-permute-start(bf16[2,4,560,128]{3,2,1,0:T(8,128)(2,1)} %get-tuple-element.158), channel_id=1, source_target_pairs={{0,1},{1,0},{2,3},{3,2},{4,5},{5,4},{6,7},{7,6},{8,9},{9,8},{10,11... | collective-permute-start | bytes 3440648 | tf_op jit(solution)/shard_map/ppermute | solution.py:1115
  278.2 41.0 %collective-permute-start.32 = (bf16[2,4,560,128]{3,2,1,0:T(8,128)(2,1)}, bf16[2,4,560,128]{3,2,1,0:T(8,128)(2,1)}, u32[]{:S(2)}, u32[]{:S(2)}) collective-permute-start(bf16[2,4,560,128]{3,2,1,0:T(8,128)(2,1)} %get-tuple-element.160), channel_id=1, source_target_pairs={{0,2},{1,3},{2,0},{3,1},{4,6},{5,7},{6,4},{7,5},{8,10},{9,11},{10,... | collective-permute-start | bytes 3440648 | tf_op jit(solution)/shard_map/ppermute | solution.py:1115
  319.0 19.2 %collective-permute-start.35 = (bf16[4,4,1120,128]{3,2,1,0:T(8,128)(2,1)}, bf16[4,4,1120,128]{3,2,1,0:T(8,128)(2,1)}, u32[]{:S(2)}, u32[]{:S(2)}) collective-permute-start(bf16[4,4,1120,128]{3,2,1,0:T(8,128)(2,1)} %get-tuple-element.165), channel_id=1, source_target_pairs={{0,16},{16,0},{1,17},{17,1},{2,18},{18,2},{3,19},{19,3},{4,20},{20... | collective-permute-start | bytes 13762568 | tf_op jit(solution)/shard_map/ppermute | solution.py:1119
  321.8 28.6 %collective-permute-start.33 = (bf16[4,560,128]{2,1,0:T(8,128)(2,1)}, bf16[4,560,128]{2,1,0:T(8,128)(2,1)}, u32[]{:S(2)}, u32[]{:S(2)}) collective-permute-start(bf16[4,560,128]{2,1,0:T(8,128)(2,1)} %get-tuple-element.162.refs_9_), channel_id=1, source_target_pairs={{0,2},{1,3},{2,0},{3,1},{4,6},{5,7},{6,4},{7,5},{8,10},{9,11},{10,... | collective-permute-start | bytes 1720328 | tf_op jit(solution)/shard_map/ppermute | solution.py:1115
  322.1 28.3 %collective-permute-start.34 = (bf16[4,560,128]{2,1,0:T(8,128)(2,1)}, bf16[4,560,128]{2,1,0:T(8,128)(2,1)}, u32[]{:S(2)}, u32[]{:S(2)}) collective-permute-start(bf16[4,560,128]{2,1,0:T(8,128)(2,1)} %get-tuple-element.164), channel_id=1, source_target_pairs={{0,1},{1,0},{2,3},{3,2},{4,5},{5,4},{6,7},{7,6},{8,9},{9,8},{10,11... | collective-permute-start | bytes 1720328 | tf_op jit(solution)/shard_map/ppermute | solution.py:1115
  336.9 43.5 %collective-permute-start.36 = (bf16[512,512]{1,0:T(8,128)(2,1)}, bf16[512,512]{1,0:T(8,128)(2,1)}, u32[]{:S(2)}, u32[]{:S(2)}) collective-permute-start(bf16[512,512]{1,0:T(8,128)(2,1)} %get-tuple-element.170), channel_id=1, source_target_pairs={{1,0},{2,1},{3,2},{5,4},{6,5},{7,6},{9,8},{10,9},{11,10},{13,12},{... | collective-permute-start | bytes 1572872 | tf_op jit(solution)/shard_map/ppermute | solution.py:1125
  345.3 32.5 %collective-permute-start.37 = (bf16[2,4,560,128]{3,2,1,0:T(8,128)(2,1)}, bf16[2,4,560,128]{3,2,1,0:T(8,128)(2,1)}, u32[]{:S(2)}, u32[]{:S(2)}) collective-permute-start(bf16[2,4,560,128]{3,2,1,0:T(8,128)(2,1)} %get-tuple-element.175), channel_id=1, source_target_pairs={{0,1},{1,0},{2,3},{3,2},{4,5},{5,4},{6,7},{7,6},{8,9},{9,8},{10,11... | collective-permute-start | bytes 3440648 | tf_op jit(solution)/shard_map/ppermute | solution.py:1115
  347.9 29.8 %collective-permute-start.38 = (bf16[2,4,560,128]{3,2,1,0:T(8,128)(2,1)}, bf16[2,4,560,128]{3,2,1,0:T(8,128)(2,1)}, u32[]{:S(2)}, u32[]{:S(2)}) collective-permute-start(bf16[2,4,560,128]{3,2,1,0:T(8,128)(2,1)} %get-tuple-element.177), channel_id=1, source_target_pairs={{0,2},{1,3},{2,0},{3,1},{4,6},{5,7},{6,4},{7,5},{8,10},{9,11},{10,... | collective-permute-start | bytes 3440648 | tf_op jit(solution)/shard_map/ppermute | solution.py:1115
  391.2 18.9 %collective-permute-start.56 = (bf16[2,1120,128]{2,1,0:T(8,128)(2,1)S(1)}, bf16[2,1120,128]{2,1,0:T(8,128)(2,1)S(1)}, u32[]{:S(2)}, u32[]{:S(2)}) collective-permute-start(bf16[2,1120,128]{2,1,0:T(8,128)(2,1)S(1)} %copy-done.49), channel_id=1, source_target_pairs={{0,4},{1,5},{2,6},{3,7},{4,0},{5,1},{6,2},{7,3},{8,12},{9,13},{10,... | collective-permute-start | bytes 1720328 | tf_op jit(solution)/shard_map/ppermute | solution.py:1115
  396.5 15.8 %collective-permute-start.40 = (bf16[4,560,128]{2,1,0:T(8,128)(2,1)S(1)}, bf16[4,560,128]{2,1,0:T(8,128)(2,1)S(1)}, u32[]{:S(2)}, u32[]{:S(2)}) collective-permute-start(bf16[4,560,128]{2,1,0:T(8,128)(2,1)S(1)} %copy-done.51), channel_id=1, source_target_pairs={{0,2},{1,3},{2,0},{3,1},{4,6},{5,7},{6,4},{7,5},{8,10},{9,11},{10,... | collective-permute-start | bytes 1720328 | tf_op jit(solution)/shard_map/ppermute | solution.py:1115
  398.2 15.9 %collective-permute-start.41 = (bf16[4,560,128]{2,1,0:T(8,128)(2,1)S(1)}, bf16[4,560,128]{2,1,0:T(8,128)(2,1)S(1)}, u32[]{:S(2)}, u32[]{:S(2)}) collective-permute-start(bf16[4,560,128]{2,1,0:T(8,128)(2,1)S(1)} %copy-done.50), channel_id=1, source_target_pairs={{0,1},{1,0},{2,3},{3,2},{4,5},{5,4},{6,7},{7,6},{8,9},{9,8},{10,11... | collective-permute-start | bytes 1720328 | tf_op jit(solution)/shard_map/ppermute | solution.py:1115
  406.0 18.2 %collective-permute-start.46 = (bf16[2,4,256,128]{3,2,1,0:T(8,128)(2,1)}, bf16[2,4,256,128]{3,2,1,0:T(8,128)(2,1)S(1)}, u32[]{:S(2)}, u32[]{:S(2)}) collective-permute-start(bf16[2,4,256,128]{3,2,1,0:T(8,128)(2,1)} %get-tuple-element.189), channel_id=1, source_target_pairs={{0,1},{1,0},{2,3},{3,2},{4,5},{5,4},{6,7},{7,6},{8,9},{9,8},{10,11... | collective-permute-start | bytes 1572872 | tf_op jit(solution)/shard_map/ppermute | solution.py:1115
  406.5 19.1 %collective-permute-start.47 = (bf16[2,4,256,128]{3,2,1,0:T(8,128)(2,1)}, bf16[2,4,256,128]{3,2,1,0:T(8,128)(2,1)S(1)}, u32[]{:S(2)}, u32[]{:S(2)}) collective-permute-start(bf16[2,4,256,128]{3,2,1,0:T(8,128)(2,1)} %get-tuple-element.191), channel_id=1, source_target_pairs={{0,2},{1,3},{2,0},{3,1},{4,6},{5,7},{6,4},{7,5},{8,10},{9,11},{10,... | collective-permute-start | bytes 1572872 | tf_op jit(solution)/shard_map/ppermute | solution.py:1115
  410.2 29.1 %collective-permute-start.57 = (bf16[1120,128]{1,0:T(8,128)(2,1)S(1)}, bf16[1120,128]{1,0:T(8,128)(2,1)S(1)}, u32[]{:S(2)}, u32[]{:S(2)}) collective-permute-start(bf16[1120,128]{1,0:T(8,128)(2,1)S(1)} %fusion.1), channel_id=1, source_target_pairs={{0,8},{1,9},{2,10},{3,11},{4,12},{5,13},{6,14},{7,15},{8,0},{9,1},... | collective-permute-start | bytes 860168 | tf_op jit(solution)/shard_map/ppermute | solution.py:1115
  418.9 31.6 %collective-permute-start.42 = (bf16[1120,128]{1,0:T(8,128)(2,1)}, bf16[1120,128]{1,0:T(8,128)(2,1)S(1)}, u32[]{:S(2)}, u32[]{:S(2)}) collective-permute-start(bf16[1120,128]{1,0:T(8,128)(2,1)} %get-tuple-element.183), channel_id=1, source_target_pairs={{0,4},{1,5},{2,6},{3,7},{4,0},{5,1},{6,2},{7,3},{8,12},{9,13},{10,... | collective-permute-start | bytes 860168 | tf_op jit(solution)/shard_map/ppermute | solution.py:1115
  419.0 31.6 %collective-permute-start.43 = (bf16[1120,128]{1,0:T(8,128)(2,1)}, bf16[1120,128]{1,0:T(8,128)(2,1)S(1)}, u32[]{:S(2)}, u32[]{:S(2)}) collective-permute-start(bf16[1120,128]{1,0:T(8,128)(2,1)} %get-tuple-element.184), channel_id=1, source_target_pairs={{0,8},{1,9},{2,10},{3,11},{4,12},{5,13},{6,14},{7,15},{8,0},{9,1},... | collective-permute-start | bytes 860168 | tf_op jit(solution)/shard_map/ppermute | solution.py:1115
  424.2 28.3 %collective-permute-start.44 = (bf16[1120,128]{1,0:T(8,128)(2,1)}, bf16[1120,128]{1,0:T(8,128)(2,1)S(1)}, u32[]{:S(2)}, u32[]{:S(2)}) collective-permute-start(bf16[1120,128]{1,0:T(8,128)(2,1)} %get-tuple-element.185), channel_id=1, source_target_pairs={{0,12},{1,13},{2,14},{3,15},{4,8},{5,9},{6,10},{7,11},{8,4},{9,5},... | collective-permute-start | bytes 860168 | tf_op jit(solution)/shard_map/ppermute | solution.py:1115
  428.5 15.0 %collective-permute-start.48 = (bf16[4,256,128]{2,1,0:T(8,128)(2,1)}, bf16[4,256,128]{2,1,0:T(8,128)(2,1)S(1)}, u32[]{:S(2)}, u32[]{:S(2)}) collective-permute-start(bf16[4,256,128]{2,1,0:T(8,128)(2,1)} %get-tuple-element.192), channel_id=1, source_target_pairs={{0,2},{1,3},{2,0},{3,1},{4,6},{5,7},{6,4},{7,5},{8,10},{9,11},{10,... | collective-permute-start | bytes 786440 | tf_op jit(solution)/shard_map/ppermute | solution.py:1115
  443.5 20.4 %collective-permute-start.58 = (bf16[1120,128]{1,0:T(8,128)(2,1)S(1)}, bf16[1120,128]{1,0:T(8,128)(2,1)S(1)}, u32[]{:S(2)}, u32[]{:S(2)}) collective-permute-start(bf16[1120,128]{1,0:T(8,128)(2,1)S(1)} %fusion.refs_4_), channel_id=1, source_target_pairs={{0,1},{1,0},{2,3},{3,2},{4,5},{5,4},{6,7},{7,6},{8,9},{9,8},{10,11... | collective-permute-start | bytes 860168 | tf_op jit(solution)/shard_map/ppermute | solution.py:1115
  446.5 18.0 %collective-permute-start.59 = (bf16[1120,128]{1,0:T(8,128)(2,1)S(1)}, bf16[1120,128]{1,0:T(8,128)(2,1)S(1)}, u32[]{:S(2)}, u32[]{:S(2)}) collective-permute-start(bf16[1120,128]{1,0:T(8,128)(2,1)S(1)} %fusion.refs_4_), channel_id=1, source_target_pairs={{0,2},{1,3},{2,0},{3,1},{4,6},{5,7},{6,4},{7,5},{8,10},{9,11},{10,... | collective-permute-start | bytes 860168 | tf_op jit(solution)/shard_map/ppermute | solution.py:1115
  456.8 34.3 %collective-permute-start.39 = (bf16[2,512,640]{2,1,0:T(8,128)(2,1)}, bf16[2,512,640]{2,1,0:T(8,128)(2,1)}, u32[]{:S(2)}, u32[]{:S(2)}) collective-permute-start(bf16[2,512,640]{2,1,0:T(8,128)(2,1)} %get-tuple-element.274), channel_id=1, source_target_pairs={{0,16},{16,0},{1,17},{17,1},{2,18},{18,2},{3,19},{19,3},{4,20},{20... | collective-permute-start | bytes 3932168 | tf_op jit(solution)/shard_map/ppermute | solution.py:1119
  460.9 24.3 %collective-permute-start.53 = (bf16[1632,128]{1,0:T(8,128)(2,1)S(1)}, bf16[1632,128]{1,0:T(8,128)(2,1)S(1)}, u32[]{:S(2)}, u32[]{:S(2)}) collective-permute-start(bf16[1632,128]{1,0:T(8,128)(2,1)S(1)} %pad_maximum_fusion.2.refs_0_), channel_id=1, source_target_pairs={{0,1},{1,0},{2,3},{3,2},{4,5},{5,4},{6,7},{7,6},{8,9},{9,8},{10,11... | collective-permute-start | bytes 1253384 | tf_op jit(solution)/shard_map/ppermute | solution.py:1115
  462.7 23.4 %collective-permute-start.54 = (bf16[1632,128]{1,0:T(8,128)(2,1)S(1)}, bf16[1632,128]{1,0:T(8,128)(2,1)S(1)}, u32[]{:S(2)}, u32[]{:S(2)}) collective-permute-start(bf16[1632,128]{1,0:T(8,128)(2,1)S(1)} %pad_maximum_fusion.2.refs_0_), channel_id=1, source_target_pairs={{0,2},{1,3},{2,0},{3,1},{4,6},{5,7},{6,4},{7,5},{8,10},{9,11},{10,... | collective-permute-start | bytes 1253384 | tf_op jit(solution)/shard_map/ppermute | solution.py:1115
  463.9 22.2 %collective-permute-start.55 = (bf16[1632,128]{1,0:T(8,128)(2,1)S(1)}, bf16[1632,128]{1,0:T(8,128)(2,1)S(1)}, u32[]{:S(2)}, u32[]{:S(2)}) collective-permute-start(bf16[1632,128]{1,0:T(8,128)(2,1)S(1)} %pad_maximum_fusion.2.refs_0_), channel_id=1, source_target_pairs={{0,3},{1,2},{2,1},{3,0},{4,7},{5,6},{6,5},{7,4},{8,11},{9,10},{10,... | collective-permute-start | bytes 1253384 | tf_op jit(solution)/shard_map/ppermute | solution.py:1115
  464.5 20.7 %collective-permute-start.60 = (bf16[1120,128]{1,0:T(8,128)(2,1)S(1)}, bf16[1120,128]{1,0:T(8,128)(2,1)S(1)}, u32[]{:S(2)}, u32[]{:S(2)}) collective-permute-start(bf16[1120,128]{1,0:T(8,128)(2,1)S(1)} %fusion.refs_4_), channel_id=1, source_target_pairs={{0,3},{1,2},{2,1},{3,0},{4,7},{5,6},{6,5},{7,4},{8,11},{9,10},{10,... | collective-permute-start | bytes 860168 | tf_op jit(solution)/shard_map/ppermute | solution.py:1115
  (68 other events, 661.3 us)
